TPU v7x, 32 devices: a whole 2x2x4 slice. The times are simulated.
32 devices in a mesh: row: 4 (over y, x), col: 8 (over z, core).
Axes of the slice: x: 2, y: 2, z: 4, core: 2. Of those that a mesh axis runs over, the one named last changes fastest.
Arguments:
- b_gate_up: bfloat16 [512, 28672], P('col', 'row'), may hold values from -6 to 6
- b_down: bfloat16 [256, 28672], P('col', 'row'), may hold values from -6 to 6
- a_gate_up: bfloat16 [512, 28672], P(None, 'row'), may hold values from -6 to 6
- a_down: bfloat16 [256, 28672], P(None, 'row'), may hold values from -6 to 6
- transform: bfloat16 [28672, 28672], P('row', 'col'), may hold values from -0.03125 to 0.03125
- check_tokens: bfloat16 [8192, 256], P('col'), may hold values from -6 to 6
Outputs:
- merged_gate_up: bfloat16 [512, 28672], P(None, 'row')
- merged_down: bfloat16 [256, 28672], P(None, 'row')
- check: bfloat16 [8192, 256], P('col', 'row')
All inputs are finite; a program needn't handle non-finite values.
Results may differ from a plain program's by a relative error of at most 0.0081.
Values may be sent and summed in bfloat16 or wider, within the bound.
No kernel may reach another device: no remote copies, remote signals or barrier semaphores. Data moves between devices by JAX's collectives and lax.ppermute only.
A program may use at most 192 MiB of HBM per device.

v0:
```python
import jax
import jax.numpy as jnp
from jax import lax
from jax.sharding import PartitionSpec as P

FF = 28672
R = 256


def broadcast(array, axis, root):
    mine = lax.axis_index(axis) == root
    return lax.psum(jnp.where(mine, array, jnp.zeros_like(array)), axis)


def on_device(b_gate_up, b_down, a_gate_up, a_down, transform, check_tokens):
    col_count = lax.axis_size("col")
    row_count = lax.axis_size("row")
    gate_rows = b_gate_up.shape[0]
    down_rows = b_down.shape[0]
    stacked = jnp.concatenate([b_gate_up, b_down], axis=0)
    partial_sum = jnp.dot(
        lax.all_gather(stacked, "col", axis=0, tiled=True),
        transform,
        preferred_element_type=jnp.float32,
    )
    share = lax.psum_scatter(partial_sum, "row", scatter_dimension=0, tiled=True)
    projected = lax.all_gather(share.astype(jnp.bfloat16), "row", axis=0, tiled=True)
    ratio = col_count // row_count
    first_root = ratio * lax.axis_index("row")
    panels = []
    for member in range(ratio):
        panels.append(broadcast(projected, "col", first_root + member))
    panel = jnp.concatenate(panels, axis=1)
    blocks = panel.reshape(col_count, gate_rows + down_rows, panel.shape[1])
    proj_gate_up = blocks[:, :gate_rows].reshape(col_count * gate_rows, panel.shape[1])
    proj_down = blocks[:, gate_rows:].reshape(col_count * down_rows, panel.shape[1])
    merged_gate_up = (
        0.5 * (a_gate_up.astype(jnp.float32) + proj_gate_up.astype(jnp.float32))
    ).astype(jnp.bfloat16)
    merged_down = (0.5 * (a_down.astype(jnp.float32) + proj_down.astype(jnp.float32))).astype(
        jnp.bfloat16
    )
    features = check_tokens.shape[1]
    gate = jnp.dot(
        check_tokens, merged_gate_up[:features], preferred_element_type=jnp.float32
    ) * R ** (-0.5)
    up_value = jnp.dot(
        check_tokens, merged_gate_up[features:], preferred_element_type=jnp.float32
    ) * R ** (-0.5)
    hidden = (jax.nn.silu(gate) * up_value).astype(jnp.bfloat16)
    partial_check = lax.dot_general(
        hidden, merged_down, (((1,), (1,)), ((), ())), preferred_element_type=jnp.float32
    )
    summed = lax.psum_scatter(partial_check, "row", scatter_dimension=1, tiled=True)
    check = (summed * FF ** (-0.5)).astype(jnp.bfloat16)
    return (merged_gate_up, merged_down, check)


def solution(mesh):
    return jax.shard_map(
        on_device,
        mesh=mesh,
        in_specs=(
            P("col", "row"),
            P("col", "row"),
            P(None, "row"),
            P(None, "row"),
            P("row", "col"),
            P("col", None),
        ),
        out_specs=(P(None, "row"), P(None, "row"), P("col", "row")),
        check_vma=False,
    )
```

profile of v0, /device:TPU:0, one launch (start us, length us, event | category | flops | bytes accessed | tf_op | source)
XLA Modules:
  0.0 666.4 jit_solution(5365542267650799235)
XLA Ops:
  7.2 0.0 copy-start
  7.2 0.0 all-gather.3.cloned.1.call-start
  7.2 2.5 pad_maximum_fusion.1
  9.8 0.0 all-gather.3.cloned.1.call-update
  9.8 0.0 reduce-scatter.3.cloned.1.call-start
  9.8 106.9 %all-gather.3.cloned.1.call-done = bf16[768,7168]{1,0:T(8,128)(2,1)} async-done(((bf16[96,7168]{1,0:T(8,128)(2,1)}), bf16[768,7168]{1,0:T(8,128)(2,1)}) %all-gather.3.cloned.1.call-update) | async-done | bytes 11010064 | tf_op jit(solution)/shard_map/all_gather | solution.py:22
  116.7 48.3 %fusion.18 = f32[768,3584]{1,0:T(8,128)} fusion(bf16[768,7168]{1,0:T(8,128)(2,1)} %all-gather.3.cloned.1.call-done, bf16[7168,3584]{1,0:T(8,128)(2,1)} %param.10), kind=kOutput, calls=%fused_computation.25 | convolution fusion | flops 39460012032 | bytes 73400320 | tf_op jit(solution)/shard_map/dot_general | solution.py:21
  165.0 0.0 reduce-scatter.3.cloned.1.call-update
  165.0 0.0 all-gather.5.cloned.1.call-start
  165.1 106.3 %reduce-scatter.3.cloned.1.call-done = f32[192,3584]{1,0:T(8,128)} async-done(((f32[768,3584]{1,0:T(8,128)}), f32[192,3584]{1,0:T(8,128)}) %reduce-scatter.3.cloned.1.call-update) | async-done | bytes 2752528 | tf_op jit(solution)/shard_map/reduce_scatter | solution.py:26
  271.4 3.0 convert_element_type.34
  274.4 0.0 all-gather.5.cloned.1.call-update
  274.4 0.0 all-reduce.3.cloned.1.call-start
  274.4 63.7 %all-gather.5.cloned.1.call-done = bf16[768,3584]{1,0:T(8,128)(2,1)} async-done(((bf16[192,3584]{1,0:T(8,128)(2,1)}), bf16[768,3584]{1,0:T(8,128)(2,1)}) %all-gather.5.cloned.1.call-update) | async-done | bytes 5505040 | tf_op jit(solution)/shard_map/all_gather | solution.py:27
  338.1 7.5 %broadcast_select_fusion.1 = (bf16[768,3584]{1,0:T(8,128)(2,1)}, bf16[768,3584]{1,0:T(8,128)(2,1)}) fusion(bf16[768,3584]{1,0:T(8,128)(2,1)} %all-gather.5.cloned.1.call-done, pred[]{:T(512)S(6)} %eq.6, pred[]{:T(512)S(6)} %eq.7), kind=kLoop, calls=%fused_computation.17 | loop fusion | flops 5505024 | bytes 16515074 | tf_op jit(solution)/shard_map/jit(_where)/select_n | solution.py:12
  345.6 0.0 all-reduce.3.cloned.1.call-update
  345.7 0.2 reduce-scatter.5.cloned.1.call-start
  345.9 225.3 %all-reduce.3.cloned.1.call-done = (bf16[768,3584]{1,0:T(8,128)(2,1)}, bf16[768,3584]{1,0:T(8,128)(2,1)}) async-done(((bf16[768,3584]{1,0:T(8,128)(2,1)}, bf16[768,3584]{1,0:T(8,128)(2,1)}), (bf16[768,3584]{1,0:T(8,128)(2,1)}, bf16[768,3584]{1,0:T(8,128)(2,1)})) %all-reduce.3.cloned.1.call-update) | async-done | bytes 11010064 | tf_op jit(solution)/shard_map/psum | solution.py:12
  571.2 5.7 pad_maximum_fusion
  576.9 2.2 slice.17
  579.1 3.4 slice.16
  582.5 10.7 %fusion.5 = bf16[512,7168]{1,0:T(8,128)(2,1)} fusion(bf16[512,7168]{1,0:T(8,128)(2,1)} %param.8, bf16[8,64,7168]{2,1,0:T(8,128)(2,1)} %slice.16), kind=kLoop, calls=%fused_computation.9 | loop fusion | flops 18350080 | bytes 22020096 | tf_op jit(solution)/shard_map/convert_element_type | solution.py:39
  593.2 0.0 copy-start.1
  593.2 6.4 fusion.11
  599.6 0.0 copy-done
  599.6 0.0 copy-done.1
  599.6 11.7 %fusion.14 = f32[7168,1024]{1,0:T(8,128)} fusion(bf16[1024,256]{1,0:T(8,128)(2,1)S(1)} %copy-done, bf16[512,7168]{1,0:T(8,128)(2,1)S(1)} %copy-done.1), kind=kOutput, calls=%fused_computation.19 | convolution fusion | flops 3758096384 | bytes 33554432 | tf_op jit(solution)/shard_map/dot_general | solution.py:44
  611.3 19.0 %fusion.6 = f32[1024,256]{0,1:T(8,128)} fusion(bf16[256,7168]{1,0:T(8,128)(2,1)} %fusion.11, f32[7168,1024]{1,0:T(8,128)} %fusion.14, bf16[1024,256]{1,0:T(8,128)(2,1)S(1)} %copy-done, bf16[512,7168]{1,0:T(8,128)(2,1)} %fusion.5), kind=kOutput, calls=%fused_computation.10 | convolution fusion | flops 7574913024 | bytes 38273024 | tf_op jit(solution)/shard_map/dot_general | solution.py:51
  630.2 0.0 reduce-scatter.5.cloned.1.call-update
  630.3 28.0 %reduce-scatter.5.cloned.1.call-done = f32[1024,64]{0,1:T(8,128)} async-done(((f32[1024,256]{0,1:T(8,128)}), f32[1024,64]{0,1:T(8,128)}) %reduce-scatter.5.cloned.1.call-update) | async-done | bytes 262160 | tf_op jit(solution)/shard_map/reduce_scatter | solution.py:54
  658.3 1.6 multiply_convert_fusion
Async XLA Ops:
  7.2 592.4 %copy-start = (bf16[1024,256]{1,0:T(8,128)(2,1)S(1)}, bf16[1024,256]{1,0:T(8,128)(2,1)}, u32[]{:S(2)}) copy-start(bf16[1024,256]{1,0:T(8,128)(2,1)} %param.11) | copy-start | bytes 1572868
  7.2 109.5 %all-gather.3.cloned.1.call-start = ((), (), s32[]{:S(2)}) async-start(), calls=%async_computation.2 | async-start | bytes 12386304 | tf_op jit(solution)/shard_map/all_gather | solution.py:22
  9.8 261.6 %reduce-scatter.3.cloned.1.call-start = ((), (), s32[]{:S(2)}) async-start(), calls=%async_computation.3 | async-start | bytes 13762560 | tf_op jit(solution)/shard_map/reduce_scatter | solution.py:26
  165.0 173.1 %all-gather.5.cloned.1.call-start = ((), (), s32[]{:S(2)}) async-start(), calls=%async_computation.4 | async-start | bytes 6881280 | tf_op jit(solution)/shard_map/all_gather | solution.py:27
  274.4 296.8 %all-reduce.3.cloned.1.call-start = ((), (), s32[]{:S(2)}) async-start(), calls=%async_computation.6 | async-start | bytes 22020096 | tf_op jit(solution)/shard_map/psum | solution.py:12
  345.7 312.6 %reduce-scatter.5.cloned.1.call-start = ((), (), s32[]{:S(2)}) async-start(), calls=%async_computation.5 | async-start | bytes 1310720 | tf_op jit(solution)/shard_map/reduce_scatter | solution.py:54
  593.2 6.4 copy-start.1
Sparse Core Ops, SparseCore 0:
  10.2 106.4 all-gather.2
  165.2 106.1 reduce-scatter.2
  274.5 63.5 all-gather.4
  345.8 225.3 all-reduce.2
  630.4 27.8 reduce-scatter.4
where the time goes:
time: 667 us; the launch traced here: 666 us
  waiting for transfers between devices  530 us (79%)
  matrix products  79 us (12%)
  other arithmetic  37.5 us (6%)
  between operations  13.8 us (2%)
    psum x1, waiting for transfers between devices, broadcast(): return lax.psum(jnp.where(mine, array, jnp.zeros_like(array)), axis)  225 us
    all_gather x1, waiting for transfers between devices, on_device(): lax.all_gather(stacked, 'col', axis=0, tiled=True)  107 us
    reduce_scatter x1, waiting for transfers between devices, on_device(): lax.psum_scatter(partial_sum, 'row', scatter_dimension=0, tiled=True)  106 us
    all_gather x1, waiting for transfers between devices, on_device(): lax.all_gather(share.astype(jnp.bfloat16), 'row', axis=0, tiled=True)  63.7 us
    dot_general x1, matrix products, on_device(): jnp.dot(lax.all_gather(stacked, 'col', axis=0, tiled=True), transform, pr...  48.3 us
    reduce_scatter x1, waiting for transfers between devices, on_device(): lax.psum_scatter(partial_check, 'row', scatter_dimension=1, tiled=True)  28 us
    dot_general x1, matrix products, on_device(): lax.dot_general(hidden, merged_down, (((1,), (1,)), ((), ())), preferred_...  19 us
  transfers between devices with their start and end apart: 5, of which 5 were waited for; matrix products, arithmetic and copies ran while one was open for 0% of the time, Pallas kernels for 0%

commit v1 on v0

v1 whole, which is shorter than its diff:
```python
import functools

import jax
import jax.numpy as jnp
from jax import lax
from jax.experimental import pallas as pl
from jax.experimental.pallas import tpu as pltpu
from jax.sharding import PartitionSpec as P

BF16 = jnp.bfloat16
F32 = jnp.float32
VMEM_BYTES = 48 * 2**20


def ring_order(n):
    return [0, *range(1, n, 2), *reversed(range(2, n, 2))]


def look_up(table, index):
    return sum(jnp.where(index == i, v, 0) for i, v in enumerate(table))


def pick(arrays, index):
    out = arrays[0]
    for i in range(1, len(arrays)):
        out = jnp.where(index == i, arrays[i], out)
    return out


def block_of(width):
    return max(b for b in range(128, 513, 128) if width % b == 0)


def project_kernel(scalars, mine, theirs, panel, out, rows):
    count = mine.shape[0]

    @pl.when(pl.program_id(0) == 0)
    def _():
        rows[:count] = mine[...]
        rows[count:] = theirs[...]

    core = scalars[0]
    product = jnp.dot(rows[...], panel[...], preferred_element_type=F32).astype(BF16)
    out[core] = product[:count]
    out[1 - core] = product[count:]


def project(scalars, mine, theirs, panel):
    count, depth = mine.shape
    width = panel.shape[1]
    block = block_of(width)
    once = pl.Buffered(1)
    return pl.pallas_call(
        project_kernel,
        grid_spec=pltpu.PrefetchScalarGridSpec(
            num_scalar_prefetch=1,
            grid=(width // block,),
            in_specs=[
                pl.BlockSpec((count, depth), lambda i, s: (0, 0), pipeline_mode=once),
                pl.BlockSpec((count, depth), lambda i, s: (0, 0), pipeline_mode=once),
                pl.BlockSpec((depth, block), lambda i, s: (0, i)),
            ],
            out_specs=pl.BlockSpec((2, count, block), lambda i, s: (0, 0, i)),
            scratch_shapes=[pltpu.VMEM((2 * count, depth), BF16)],
        ),
        out_shape=jax.ShapeDtypeStruct((2, count, width), BF16),
        compiler_params=pltpu.CompilerParams(vmem_limit_bytes=VMEM_BYTES),
        name="project",
    )(scalars, mine, theirs, panel).reshape(2 * count, width)


def forward_kernel(steps, groups, scalars, tokens, *refs):
    own, far = refs[:groups], refs[groups : 2 * groups]
    a_gu, a_dn, gu_out, dn_out, check_out, proj, total = refs[2 * groups :]
    step = pl.program_id(0)
    features = tokens.shape[1]
    scale = features ** (-0.5)
    gu_rows = a_gu.shape[0] // (2 * groups)

    def gather(pieces):
        for t in range(groups):
            place = scalars[1 + t]
            proj[2 * place] = pieces[t][: proj.shape[1]]
            proj[2 * place + 1] = pieces[t][proj.shape[1] :]

    @pl.when(step < steps)
    def _():
        gather(own)

    @pl.when(step >= steps)
    def _():
        gather(far)

    proj_gu = proj[:, :gu_rows].reshape(a_gu.shape).astype(F32)
    proj_dn = proj[:, gu_rows:].reshape(a_dn.shape).astype(F32)
    merged_gu = (0.5 * (a_gu[...].astype(F32) + proj_gu)).astype(BF16)
    merged_dn = (0.5 * (a_dn[...].astype(F32) + proj_dn)).astype(BF16)
    gu_out[...] = merged_gu
    dn_out[...] = merged_dn
    gate = jnp.dot(tokens[...], merged_gu[:features], preferred_element_type=F32) * (0.5 * scale)
    up = jnp.dot(tokens[...], merged_gu[features:], preferred_element_type=F32) * scale
    hidden = (gate * (1.0 + jnp.tanh(gate)) * up).astype(BF16)
    part = lax.dot_general(hidden, merged_dn, (((1,), (1,)), ((), ())), preferred_element_type=F32)

    @pl.when(step == 0)
    def _():
        total[...] = part

    @pl.when(step > 0)
    def _():
        total[...] += part

    @pl.when(step == 2 * steps - 1)
    def _():
        width = features // groups
        fold = max(1, 128 // width)
        rows = total.shape[0] // fold
        for j in range(groups):
            packed = [total[f * rows : (f + 1) * rows, j * width : (j + 1) * width] for f in range(fold)]
            check_out[j] = jnp.concatenate(packed, axis=1).astype(BF16)


def forward(scalars, tokens, own, far, a_gu, a_dn):
    groups = len(own)
    piece_rows, width = own[0].shape
    block = block_of(width)
    steps = width // block
    count, features = tokens.shape
    fold = max(1, 128 // (features // groups))
    check_shape = (groups, count // fold, fold * features // groups)

    def own_place(i, s):
        return (0, jnp.minimum(i, steps - 1))

    def far_place(i, s):
        return (0, jnp.maximum(i - steps, 0))

    def place(i, s):
        half = jnp.where(i < steps, s[0], 1 - s[0])
        return (0, half * steps + lax.rem(i, steps))

    gu_spec = pl.BlockSpec((a_gu.shape[0], block), place)
    dn_spec = pl.BlockSpec((a_dn.shape[0], block), place)
    return pl.pallas_call(
        functools.partial(forward_kernel, steps, groups),
        grid_spec=pltpu.PrefetchScalarGridSpec(
            num_scalar_prefetch=1,
            grid=(2 * steps,),
            in_specs=[pl.BlockSpec(tokens.shape, lambda i, s: (0, 0))]
            + [pl.BlockSpec((piece_rows, block), own_place)] * groups
            + [pl.BlockSpec((piece_rows, block), far_place)] * groups
            + [gu_spec, dn_spec],
            out_specs=[gu_spec, dn_spec, pl.BlockSpec(check_shape, lambda i, s: (0, 0, 0))],
            scratch_shapes=[
                pltpu.VMEM((2 * groups, piece_rows // 2, block), BF16),
                pltpu.VMEM((count, features), F32),
            ],
        ),
        out_shape=[
            jax.ShapeDtypeStruct(a_gu.shape, BF16),
            jax.ShapeDtypeStruct(a_dn.shape, BF16),
            jax.ShapeDtypeStruct(check_shape, BF16),
        ],
        compiler_params=pltpu.CompilerParams(vmem_limit_bytes=VMEM_BYTES),
        name="forward",
    )(scalars, tokens, *own, *far, a_gu, a_dn)


def on_device(b_gate_up, b_down, a_gate_up, a_down, transform, check_tokens):
    n = lax.axis_size("row")
    assert lax.axis_size("col") == 2 * n
    q = lax.axis_index("row")
    col = lax.axis_index("col")
    z, core = col // 2, col % 2
    order = ring_order(n)
    place = [order.index(i) for i in range(n)]
    after = {order[i]: order[(i + 1) % n] for i in range(n)}
    ring = [(2 * i + k, 2 * after[i] + k) for i in range(n) for k in range(2)]
    twin = [(i, i ^ 1) for i in range(2 * n)]
    began = [look_up(order, (look_up(place, q) - t) % n) for t in range(n)]
    scalars = jnp.stack([core, *began]).astype(jnp.int32)

    def peers(d):
        return [(i, i ^ d) for i in range(n)]

    width = transform.shape[1]
    rows = jnp.concatenate([b_gate_up, b_down], axis=0)
    part_rows = 2 * rows.shape[0] // n

    def stages(t, rows):
        with jax.named_scope(f"rows_ring_{t}"):
            following = [lax.ppermute(rows, "col", ring)] if t < n - 1 else []
        with jax.named_scope(f"rows_twin_{t}"):
            other = lax.ppermute(rows, "col", twin)
        *_, partial = yield [*following, project(scalars, rows, other, transform)]

        parts = partial.reshape(n, part_rows, width)
        sums = [lax.dynamic_index_in_dim(parts, q, keepdims=False)]
        for d in range(1, n):
            with jax.named_scope(f"reduce_{t}_{d}"):
                part = lax.dynamic_index_in_dim(parts, q ^ d, keepdims=False)
                sums.append(lax.ppermute(part, "row", peers(d)))
        sums = yield sums
        held = [sum(v.astype(F32) for v in sums).astype(BF16)]

        for hop in range(n - 1):
            with jax.named_scope(f"shares_ring_{t}_{hop}"):
                held.append(lax.ppermute(held[-1], "col", ring))
            held = yield held

        def for_row(r):
            return pick(held, (look_up(place, z) - look_up(place, r)) % n)

        got = [for_row(q)]
        for d in range(1, n):
            with jax.named_scope(f"deliver_{t}_{d}"):
                got.append(lax.ppermute(for_row(q ^ d), "row", peers(d)))
        got = yield got

        mine = jnp.concatenate([pick(got, q ^ j) for j in range(n)], axis=0)
        with jax.named_scope(f"deliver_twin_{t}"):
            theirs = lax.ppermute(mine, "col", twin)
        yield [mine, theirs]

    own = [None] * n
    far = [None] * n
    running = {}
    ready = {}
    step = 0
    while step < n or running:
        handed = {t: running[t].send(ready[t]) for t in running}
        if step < n:
            running[step] = stages(step, rows)
            handed[step] = next(running[step])
        flat = lax.optimization_barrier([v for vs in handed.values() for v in vs])
        ready = {}
        for t, vs in handed.items():
            ready[t], flat = flat[: len(vs)], flat[len(vs) :]
        rows = ready[step][0] if step < n else None
        step += 1
        for t in [t for t in ready if step - t == n + 3]:
            own[t], far[t] = ready.pop(t)
            del running[t]

    merged_gate_up, merged_down, parts = forward(scalars, check_tokens, own, far, a_gate_up, a_down)
    total = lax.dynamic_index_in_dim(parts, q, keepdims=False).astype(F32)
    for d in range(1, n):
        with jax.named_scope(f"check_reduce_{d}"):
            sent = lax.dynamic_index_in_dim(parts, q ^ d, keepdims=False)
            total = total + lax.ppermute(sent, "row", peers(d)).astype(F32)
    hidden_units = n * transform.shape[0]
    check = (total * hidden_units ** (-0.5)).astype(BF16)
    count, features = check_tokens.shape
    share = features // n
    check = check.reshape(check.shape[0], -1, share).swapaxes(0, 1).reshape(count, share)
    return merged_gate_up, merged_down, check


def solution(mesh):
    return jax.shard_map(
        on_device,
        mesh=mesh,
        in_specs=(
            P("col", "row"),
            P("col", "row"),
            P(None, "row"),
            P(None, "row"),
            P("row", "col"),
            P("col", None),
        ),
        out_specs=(P(None, "row"), P(None, "row"), P("col", "row")),
        check_vma=False,
    )
```

time: 667 us -> 295 us (0.44)
  waiting for transfers between devices: 530 us -> 123 us
  Pallas kernels: 0 us -> 105 us
  matrix products: 79 us -> 0 us
  starting transfers between devices: 0.39 us -> 51 us
  other arithmetic: 37.5 us -> 3.76 us
  between operations: 13.8 us -> 1.03 us
    psum x1 -> x0, waiting for transfers between devices: 225 us -> none  [broadcast(): return lax.psum(jnp.where(mine, array, jnp.zeros_like(array)), axis)]
    all_gather x2 -> x0, waiting for transfers between devices: 171 us -> none  [the longest x1 107 us: on_device(): lax.all_gather(stacked, 'col', axis=0, tiled=True)]
    reduce_scatter x2 -> x0, waiting for transfers between devices: 134 us -> none  [the longest x1 106 us: on_device(): lax.psum_scatter(partial_sum, 'row', scatter_dimension=0, tiled=True)]
    ppermute x0 -> x50, waiting for transfers between devices: none -> 123 us  [the longest x12 64.7 us: stages(): held.append(lax.ppermute(held[-1], 'col', ring))]
    pallas_call x0 -> x5, Pallas kernels: none -> 105 us  [the longest x4 80.5 us: project(): pl.pallas_call(project_kernel, grid_spec=pltpu.PrefetchScalarGridSpec(num...]
    dot_general x3 -> x0, matrix products: 79 us -> none  [the longest x1 48.3 us: on_device(): jnp.dot(lax.all_gather(stacked, 'col', axis=0, tiled=True), transform, pr...]
    ppermute x0 -> x50, starting transfers between devices: none -> 51 us  [the longest x12 15.1 us: stages(): sums.append(lax.ppermute(part, 'row', peers(d)))]
    convert_element_type x4 -> x5, other arithmetic: 21.7 us -> 2.08 us  [the longest x4 2 us: stages(): held = [sum((v.astype(F32) for v in sums)).astype(BF16)]]
  transfers between devices with their start and end apart: 5 -> 50, of which waited for: 5 -> 26; matrix products, arithmetic and copies ran while one was open for 0% -> 1% of each run, Pallas kernels for 0% -> 27%
where the time goes in v1:
time: 295 us; the launch traced here: 294 us
  waiting for transfers between devices  123 us (42%)
  Pallas kernels  105 us (36%)
  starting transfers between devices  51 us (17%)
  local copies, waits for them, and re-layouts  9.81 us (3%)
  other arithmetic  3.76 us (1%)
    pallas_call x4, Pallas kernels, project(): pl.pallas_call(project_kernel, grid_spec=pltpu.PrefetchScalarGridSpec(num...  80.5 us
    ppermute x12, waiting for transfers between devices, stages(): held.append(lax.ppermute(held[-1], 'col', ring))  64.7 us
    ppermute x12, waiting for transfers between devices, stages(): got.append(lax.ppermute(for_row(q ^ d), 'row', peers(d)))  30.1 us
    pallas_call x1, Pallas kernels, forward(): pl.pallas_call(functools.partial(forward_kernel, steps, groups), grid_spe...  24.7 us
    ppermute x3, waiting for transfers between devices, stages(): following = [lax.ppermute(rows, 'col', ring)] if t < n - 1 else []  18 us
    ppermute x12, starting transfers between devices, stages(): sums.append(lax.ppermute(part, 'row', peers(d)))  15.1 us
    ppermute x12, starting transfers between devices, stages(): got.append(lax.ppermute(for_row(q ^ d), 'row', peers(d)))  13.8 us
    ppermute x12, starting transfers between devices, stages(): held.append(lax.ppermute(held[-1], 'col', ring))  13.3 us
  transfers between devices with their start and end apart: 50, of which 26 were waited for; matrix products, arithmetic and copies ran while one was open for 1% of the time, Pallas kernels for 27%

profile of v1, /device:TPU:0, one launch (start us, length us, event | category | flops | bytes accessed | tf_op | source)
XLA Modules:
  0.0 293.9 jit_solution(16663000204530262126)
XLA Ops:
  0.6 1.3 constant_dynamic-update-slice_fusion.1
  2.5 2.6 collective-permute-start
  5.3 1.1 copy-done
  6.3 1.3 copy-done.1
  7.7 19.9 %project.4 = bf16[2,96,3584]{2,1,0:T(8,128)(2,1)S(1)} custom-call(s32[5]{0:T(128)S(1)} %stack.23.scalars, bf16[96,7168]{1,0:T(8,128)(2,1)S(1)} %constant_dynamic-update-slice_fusion.mine, bf16[96,7168]{1,0:T(8,128)(2,1)S(1)} %copy-done.1, bf16[7168,3584]{1,0:T(8,128)(2,1)} %panel.7), custom_call_target="tpu_custom_call" | custom-call | tf_op jit(solution)/shard_map/project/pallas_call | solution.py:53
  27.6 9.4 %collective-permute-done.mine = bf16[96,7168]{1,0:T(8,128)(2,1)} collective-permute-done((bf16[96,7168]{1,0:T(8,128)(2,1)S(1)}, bf16[96,7168]{1,0:T(8,128)(2,1)}, u32[]{:S(2)}, u32[]{:S(2)}) %collective-permute-start) | collective-permute-done | bytes 1376288 | tf_op jit(solution)/shard_map/rows_ring_0/ppermute | solution.py:192
  37.9 2.5 collective-permute-start.4
  41.4 20.7 %project.5 = bf16[2,96,3584]{2,1,0:T(8,128)(2,1)S(1)} custom-call(s32[5]{0:T(128)S(1)} %stack.23.scalars, bf16[96,7168]{1,0:T(8,128)(2,1)} %collective-permute-done.mine, bf16[96,7168]{1,0:T(8,128)(2,1)} %collective-permute-done.6.theirs, bf16[7168,3584]{1,0:T(8,128)(2,1)} %panel.7), custom_call_target="tpu_custom_call" | custom-call | tf_op jit(solution)/shard_map/project/pallas_call | solution.py:53
  62.2 8.5 %collective-permute-done.5.mine = bf16[96,7168]{1,0:T(8,128)(2,1)S(1)} collective-permute-done((bf16[96,7168]{1,0:T(8,128)(2,1)}, bf16[96,7168]{1,0:T(8,128)(2,1)S(1)}, u32[]{:S(2)}, u32[]{:S(2)}) %collective-permute-start.5) | collective-permute-done | bytes 1376288 | tf_op jit(solution)/shard_map/rows_ring_1/ppermute | solution.py:192
  71.9 3.3 %collective-permute-start.7 = (bf16[48,3584]{1,0:T(8,128)(2,1)S(1)}, bf16[48,3584]{1,0:T(8,128)(2,1)S(1)}, u32[]{:S(2)}, u32[]{:S(2)}) collective-permute-start(bf16[48,3584]{1,0:T(8,128)(2,1)S(1)} %add_convert_fusion.3), channel_id=1, source_target_pairs={{0,2},{1,3},{2,6},{3,7},{4,0},{5,1},{6,4},{7,5},{8,10},{9,11},{10,... | collective-permute-start | bytes 1032200 | tf_op jit(solution)/shard_map/shares_ring_0_0/ppermute | solution.py:208
  75.3 2.5 collective-permute-start.10
  78.9 19.9 %project.6 = bf16[2,96,3584]{2,1,0:T(8,128)(2,1)S(1)} custom-call(s32[5]{0:T(128)S(1)} %stack.23.scalars, bf16[96,7168]{1,0:T(8,128)(2,1)S(1)} %collective-permute-done.5.mine, bf16[96,7168]{1,0:T(8,128)(2,1)S(1)} %collective-permute-done.12.theirs, bf16[7168,3584]{1,0:T(8,128)(2,1)} %panel.7), custom_call_target="tpu_custom_call" | custom-call | tf_op jit(solution)/shard_map/project/pallas_call | solution.py:53
  98.8 12.8 %collective-permute-done.7 = bf16[48,3584]{1,0:T(8,128)(2,1)S(1)} collective-permute-done((bf16[48,3584]{1,0:T(8,128)(2,1)S(1)}, bf16[48,3584]{1,0:T(8,128)(2,1)S(1)}, u32[]{:S(2)}, u32[]{:S(2)}) %collective-permute-start.7) | collective-permute-done | bytes 344096 | tf_op jit(solution)/shard_map/shares_ring_0_0/ppermute | solution.py:208
  112.8 3.4 %collective-permute-start.13 = (bf16[48,3584]{1,0:T(8,128)(2,1)S(1)}, bf16[48,3584]{1,0:T(8,128)(2,1)S(1)}, u32[]{:S(2)}, u32[]{:S(2)}) collective-permute-start(bf16[48,3584]{1,0:T(8,128)(2,1)S(1)} %collective-permute-done.7), channel_id=1, source_target_pairs={{0,2},{1,3},{2,6},{3,7},{4,0},{5,1},{6,4},{7,5},{8,10},{9,11},{10,... | collective-permute-start | bytes 1032200 | tf_op jit(solution)/shard_map/shares_ring_0_1/ppermute | solution.py:208
  116.3 2.5 collective-permute-start.17
  119.8 19.9 %project.7 = bf16[2,96,3584]{2,1,0:T(8,128)(2,1)S(1)} custom-call(s32[5]{0:T(128)S(1)} %stack.23.scalars, bf16[96,7168]{1,0:T(8,128)(2,1)S(1)} %collective-permute-done.11.mine, bf16[96,7168]{1,0:T(8,128)(2,1)S(1)} %collective-permute-done.18.theirs, bf16[7168,3584]{1,0:T(8,128)(2,1)} %panel.7), custom_call_target="tpu_custom_call" | custom-call | tf_op jit(solution)/shard_map/project/pallas_call | solution.py:53
  142.7 2.5 collective-permute-start.24
  145.6 6.4 %collective-permute-done.21 = bf16[48,3584]{1,0:T(8,128)(2,1)S(1)} collective-permute-done((bf16[48,3584]{1,0:T(8,128)(2,1)S(1)}, bf16[48,3584]{1,0:T(8,128)(2,1)S(1)}, u32[]{:S(2)}, u32[]{:S(2)}) %collective-permute-start.21) | collective-permute-done | bytes 344096 | tf_op jit(solution)/shard_map/shares_ring_2_0/ppermute | solution.py:208
  152.0 1.5 collective-permute-start.22
  153.4 5.9 %collective-permute-done.19 = bf16[48,3584]{1,0:T(8,128)(2,1)S(1)} collective-permute-done((bf16[48,3584]{1,0:T(8,128)(2,1)S(1)}, bf16[48,3584]{1,0:T(8,128)(2,1)S(1)}, u32[]{:S(2)}, u32[]{:S(2)}) %collective-permute-start.19) | collective-permute-done | bytes 344096 | tf_op jit(solution)/shard_map/shares_ring_0_2/ppermute | solution.py:208
  159.3 5.4 %collective-permute-done.20 = bf16[48,3584]{1,0:T(8,128)(2,1)S(1)} collective-permute-done((bf16[48,3584]{1,0:T(8,128)(2,1)S(1)}, bf16[48,3584]{1,0:T(8,128)(2,1)S(1)}, u32[]{:S(2)}, u32[]{:S(2)}) %collective-permute-start.20) | collective-permute-done | bytes 344096 | tf_op jit(solution)/shard_map/shares_ring_1_1/ppermute | solution.py:208
  164.8 1.5 add_convert_fusion
  166.6 2.5 collective-permute-start.27
  170.1 1.4 collective-permute-start.28
  171.6 6.7 %collective-permute-done.30 = bf16[48,3584]{1,0:T(8,128)(2,1)S(1)} collective-permute-done((bf16[48,3584]{1,0:T(8,128)(2,1)S(1)}, bf16[48,3584]{1,0:T(8,128)(2,1)S(1)}, u32[]{:S(2)}, u32[]{:S(2)}) %collective-permute-start.30) | collective-permute-done | bytes 344096 | tf_op jit(solution)/shard_map/shares_ring_3_0/ppermute | solution.py:208
  178.6 4.5 %collective-permute-done.26 = bf16[48,3584]{1,0:T(8,128)(2,1)S(1)} collective-permute-done((bf16[48,3584]{1,0:T(8,128)(2,1)S(1)}, bf16[48,3584]{1,0:T(8,128)(2,1)S(1)}, u32[]{:S(2)}, u32[]{:S(2)}) %collective-permute-start.26) | collective-permute-done | bytes 344096 | tf_op jit(solution)/shard_map/deliver_0_2/ppermute | solution.py:217
  183.1 2.5 collective-permute-done.28
  185.6 4.5 %collective-permute-done.29 = bf16[48,3584]{1,0:T(8,128)(2,1)S(1)} collective-permute-done((bf16[48,3584]{1,0:T(8,128)(2,1)S(1)}, bf16[48,3584]{1,0:T(8,128)(2,1)S(1)}, u32[]{:S(2)}, u32[]{:S(2)}) %collective-permute-start.29) | collective-permute-done | bytes 344096 | tf_op jit(solution)/shard_map/shares_ring_2_1/ppermute | solution.py:208
  190.6 2.3 collective-permute-start.36
  194.6 7.7 %collective-permute-done.35 = bf16[48,3584]{1,0:T(8,128)(2,1)S(1)} collective-permute-done((bf16[48,3584]{1,0:T(8,128)(2,1)S(1)}, bf16[48,3584]{1,0:T(8,128)(2,1)S(1)}, u32[]{:S(2)}, u32[]{:S(2)}) %collective-permute-start.35) | collective-permute-done | bytes 344096 | tf_op jit(solution)/shard_map/shares_ring_2_2/ppermute | solution.py:208
  202.3 1.5 collective-permute-start.32
  203.8 5.4 %collective-permute-done.36 = bf16[48,3584]{1,0:T(8,128)(2,1)S(1)} collective-permute-done((bf16[48,3584]{1,0:T(8,128)(2,1)S(1)}, bf16[48,3584]{1,0:T(8,128)(2,1)S(1)}, u32[]{:S(2)}, u32[]{:S(2)}) %collective-permute-start.36) | collective-permute-done | bytes 344096 | tf_op jit(solution)/shard_map/shares_ring_3_1/ppermute | solution.py:208
  209.2 1.7 collective-permute-done.33
  213.2 2.5 collective-permute-start.40
  216.7 7.4 %collective-permute-done.41 = bf16[48,3584]{1,0:T(8,128)(2,1)S(1)} collective-permute-done((bf16[48,3584]{1,0:T(8,128)(2,1)S(1)}, bf16[48,3584]{1,0:T(8,128)(2,1)S(1)}, u32[]{:S(2)}, u32[]{:S(2)}) %collective-permute-start.41) | collective-permute-done | bytes 344096 | tf_op jit(solution)/shard_map/shares_ring_3_2/ppermute | solution.py:208
  225.1 6.6 %collective-permute-done.39 = bf16[48,3584]{1,0:T(8,128)(2,1)S(1)} collective-permute-done((bf16[48,3584]{1,0:T(8,128)(2,1)S(1)}, bf16[48,3584]{1,0:T(8,128)(2,1)S(1)}, u32[]{:S(2)}, u32[]{:S(2)}) %collective-permute-start.39) | collective-permute-done | bytes 344096 | tf_op jit(solution)/shard_map/deliver_2_2/ppermute | solution.py:217
  233.2 1.7 collective-permute-start.45
  235.0 1.3 collective-permute-start.44
  236.8 8.3 %collective-permute-done.45 = bf16[48,3584]{1,0:T(8,128)(2,1)S(1)} collective-permute-done((bf16[48,3584]{1,0:T(8,128)(2,1)S(1)}, bf16[48,3584]{1,0:T(8,128)(2,1)S(1)}, u32[]{:S(2)}, u32[]{:S(2)}) %collective-permute-start.45) | collective-permute-done | bytes 344096 | tf_op jit(solution)/shard_map/deliver_3_3/ppermute | solution.py:217
  245.1 6.9 %collective-permute-done.44 = bf16[48,3584]{1,0:T(8,128)(2,1)S(1)} collective-permute-done((bf16[48,3584]{1,0:T(8,128)(2,1)S(1)}, bf16[48,3584]{1,0:T(8,128)(2,1)S(1)}, u32[]{:S(2)}, u32[]{:S(2)}) %collective-permute-start.44) | collective-permute-done | bytes 344096 | tf_op jit(solution)/shard_map/deliver_3_2/ppermute | solution.py:217
  253.4 3.1 %collective-permute-done.46.refs_7_ = bf16[192,3584]{1,0:T(8,128)(2,1)S(1)} collective-permute-done((bf16[192,3584]{1,0:T(8,128)(2,1)S(1)}, bf16[192,3584]{1,0:T(8,128)(2,1)S(1)}, u32[]{:S(2)}, u32[]{:S(2)}) %collective-permute-start.46) | collective-permute-done | bytes 1376288 | tf_op jit(solution)/shard_map/deliver_twin_3/ppermute | solution.py:222
  256.5 1.1 copy-done.7
  257.6 24.7 %forward.1 = (bf16[512,7168]{1,0:T(8,128)(2,1)}, bf16[256,7168]{1,0:T(8,128)(2,1)}, bf16[4,512,128]{2,1,0:T(8,128)(2,1)S(1)}) custom-call(s32[5]{0:T(128)S(1)} %stack.23.scalars, bf16[1024,256]{1,0:T(8,128)(2,1)S(1)} %copy-done.2, bf16[192,3584]{1,0:T(8,128)(2,1)S(1)} %pad_maximum_fusion.refs_0_, bf16[192,3584]{1,0:T(8,128)(2,1)S(1)} %pad_maximum_fusion.1.refs_1_, ...), custom_call_target="tpu_custom_call" | custom-call | tf_op jit(solution)/shard_map/forward/pallas_call | solution.py:144
  282.3 1.6 collective-permute-start.47
  283.8 1.4 collective-permute-start.49
  285.8 2.9 collective-permute-done.47
  288.7 3.0 %collective-permute-done.49 = bf16[512,128]{1,0:T(8,128)(2,1)S(1)} collective-permute-done((bf16[512,128]{1,0:T(8,128)(2,1)S(1)}, bf16[512,128]{1,0:T(8,128)(2,1)S(1)}, u32[]{:S(2)}, u32[]{:S(2)}) %collective-permute-start.49) | collective-permute-done | bytes 131104 | tf_op jit(solution)/shard_map/check_reduce_3/ppermute | solution.py:250
  291.7 1.4 collective-permute-done.48
  (110 shorter events, 23.3 us)
Async XLA Ops:
  2.5 34.5 %collective-permute-start = (bf16[96,7168]{1,0:T(8,128)(2,1)S(1)}, bf16[96,7168]{1,0:T(8,128)(2,1)}, u32[]{:S(2)}, u32[]{:S(2)}) collective-permute-start(bf16[96,7168]{1,0:T(8,128)(2,1)S(1)} %constant_dynamic-update-slice_fusion.mine), channel_id=1, source_target_pairs={{0,2},{1,3},{2,6},{3,7},{4,0},{5,1},{6,4},{7,5},{8,10},{9,11},{10,... | collective-permute-start | bytes 4128776 | tf_op jit(solution)/shard_map/rows_ring_0/ppermute | solution.py:192
  37.0 4.4 %collective-permute-start.6 = (bf16[96,7168]{1,0:T(8,128)(2,1)}, bf16[96,7168]{1,0:T(8,128)(2,1)}, u32[]{:S(2)}, u32[]{:S(2)}) collective-permute-start(bf16[96,7168]{1,0:T(8,128)(2,1)} %collective-permute-done.mine), channel_id=1, source_target_pairs={{0,1},{1,0},{2,3},{3,2},{4,5},{5,4},{6,7},{7,6},{8,9},{9,8},{10,11... | collective-permute-start | bytes 4128776 | tf_op jit(solution)/shard_map/rows_twin_1/ppermute | solution.py:194
  37.0 33.7 %collective-permute-start.5 = (bf16[96,7168]{1,0:T(8,128)(2,1)}, bf16[96,7168]{1,0:T(8,128)(2,1)S(1)}, u32[]{:S(2)}, u32[]{:S(2)}) collective-permute-start(bf16[96,7168]{1,0:T(8,128)(2,1)} %collective-permute-done.mine), channel_id=1, source_target_pairs={{0,2},{1,3},{2,6},{3,7},{4,0},{5,1},{6,4},{7,5},{8,10},{9,11},{10,... | collective-permute-start | bytes 4128776 | tf_op jit(solution)/shard_map/rows_ring_1/ppermute | solution.py:192
  37.9 24.3 %collective-permute-start.4 = (bf16[48,3584]{1,0:T(8,128)(2,1)S(1)}, bf16[48,3584]{1,0:T(8,128)(2,1)S(1)}, u32[]{:S(2)}, u32[]{:S(2)}) collective-permute-start(bf16[48,3584]{1,0:T(8,128)(2,1)S(1)} %get-tuple-element.219), channel_id=1, source_target_pairs={{0,24},{8,16},{16,8},{24,0},{1,25},{9,17},{17,9},{25,1},{2,26},{10... | collective-permute-start | bytes 1032200 | tf_op jit(solution)/shard_map/reduce_0_3/ppermute | solution.py:202
  40.4 21.8 %collective-permute-start.3 = (bf16[48,3584]{1,0:T(8,128)(2,1)S(1)}, bf16[48,3584]{1,0:T(8,128)(2,1)S(1)}, u32[]{:S(2)}, u32[]{:S(2)}) collective-permute-start(bf16[48,3584]{1,0:T(8,128)(2,1)S(1)} %get-tuple-element.220), channel_id=1, source_target_pairs={{0,16},{8,24},{16,0},{24,8},{1,17},{9,25},{17,1},{25,9},{2,18},{10... | collective-permute-start | bytes 1032200 | tf_op jit(solution)/shard_map/reduce_0_2/ppermute | solution.py:202
  40.9 21.3 %collective-permute-start.2 = (bf16[48,3584]{1,0:T(8,128)(2,1)S(1)}, bf16[48,3584]{1,0:T(8,128)(2,1)S(1)}, u32[]{:S(2)}, u32[]{:S(2)}) collective-permute-start(bf16[48,3584]{1,0:T(8,128)(2,1)S(1)} %get-tuple-element.221), channel_id=1, source_target_pairs={{0,8},{8,0},{16,24},{24,16},{1,9},{9,1},{17,25},{25,17},{2,10},{10... | collective-permute-start | bytes 1032200 | tf_op jit(solution)/shard_map/reduce_0_1/ppermute | solution.py:202
  70.8 7.6 %collective-permute-start.12 = (bf16[96,7168]{1,0:T(8,128)(2,1)S(1)}, bf16[96,7168]{1,0:T(8,128)(2,1)S(1)}, u32[]{:S(2)}, u32[]{:S(2)}) collective-permute-start(bf16[96,7168]{1,0:T(8,128)(2,1)S(1)} %collective-permute-done.5.mine), channel_id=1, source_target_pairs={{0,1},{1,0},{2,3},{3,2},{4,5},{5,4},{6,7},{7,6},{8,9},{9,8},{10,11... | collective-permute-start | bytes 4128776 | tf_op jit(solution)/shard_map/rows_twin_2/ppermute | solution.py:194
  70.8 40.9 %collective-permute-start.11 = (bf16[96,7168]{1,0:T(8,128)(2,1)S(1)}, bf16[96,7168]{1,0:T(8,128)(2,1)S(1)}, u32[]{:S(2)}, u32[]{:S(2)}) collective-permute-start(bf16[96,7168]{1,0:T(8,128)(2,1)S(1)} %collective-permute-done.5.mine), channel_id=1, source_target_pairs={{0,2},{1,3},{2,6},{3,7},{4,0},{5,1},{6,4},{7,5},{8,10},{9,11},{10,... | collective-permute-start | bytes 4128776 | tf_op jit(solution)/shard_map/rows_ring_2/ppermute | solution.py:192
  71.9 39.7 %collective-permute-start.7 = (bf16[48,3584]{1,0:T(8,128)(2,1)S(1)}, bf16[48,3584]{1,0:T(8,128)(2,1)S(1)}, u32[]{:S(2)}, u32[]{:S(2)}) collective-permute-start(bf16[48,3584]{1,0:T(8,128)(2,1)S(1)} %add_convert_fusion.3), channel_id=1, source_target_pairs={{0,2},{1,3},{2,6},{3,7},{4,0},{5,1},{6,4},{7,5},{8,10},{9,11},{10,... | collective-permute-start | bytes 1032200 | tf_op jit(solution)/shard_map/shares_ring_0_0/ppermute | solution.py:208
  75.3 36.3 %collective-permute-start.10 = (bf16[48,3584]{1,0:T(8,128)(2,1)S(1)}, bf16[48,3584]{1,0:T(8,128)(2,1)S(1)}, u32[]{:S(2)}, u32[]{:S(2)}) collective-permute-start(bf16[48,3584]{1,0:T(8,128)(2,1)S(1)} %get-tuple-element.215), channel_id=1, source_target_pairs={{0,24},{8,16},{16,8},{24,0},{1,25},{9,17},{17,9},{25,1},{2,26},{10... | collective-permute-start | bytes 1032200 | tf_op jit(solution)/shard_map/reduce_1_3/ppermute | solution.py:202
  77.8 33.8 %collective-permute-start.9 = (bf16[48,3584]{1,0:T(8,128)(2,1)S(1)}, bf16[48,3584]{1,0:T(8,128)(2,1)S(1)}, u32[]{:S(2)}, u32[]{:S(2)}) collective-permute-start(bf16[48,3584]{1,0:T(8,128)(2,1)S(1)} %get-tuple-element.216), channel_id=1, source_target_pairs={{0,16},{8,24},{16,0},{24,8},{1,17},{9,25},{17,1},{25,9},{2,18},{10... | collective-permute-start | bytes 1032200 | tf_op jit(solution)/shard_map/reduce_1_2/ppermute | solution.py:202
  78.3 33.3 %collective-permute-start.8 = (bf16[48,3584]{1,0:T(8,128)(2,1)S(1)}, bf16[48,3584]{1,0:T(8,128)(2,1)S(1)}, u32[]{:S(2)}, u32[]{:S(2)}) collective-permute-start(bf16[48,3584]{1,0:T(8,128)(2,1)S(1)} %get-tuple-element.217), channel_id=1, source_target_pairs={{0,8},{8,0},{16,24},{24,16},{1,9},{9,1},{17,25},{25,17},{2,10},{10... | collective-permute-start | bytes 1032200 | tf_op jit(solution)/shard_map/reduce_1_1/ppermute | solution.py:202
  111.6 7.6 %collective-permute-start.18 = (bf16[96,7168]{1,0:T(8,128)(2,1)S(1)}, bf16[96,7168]{1,0:T(8,128)(2,1)S(1)}, u32[]{:S(2)}, u32[]{:S(2)}) collective-permute-start(bf16[96,7168]{1,0:T(8,128)(2,1)S(1)} %collective-permute-done.11.mine), channel_id=1, source_target_pairs={{0,1},{1,0},{2,3},{3,2},{4,5},{5,4},{6,7},{7,6},{8,9},{9,8},{10,11... | collective-permute-start | bytes 4128776 | tf_op jit(solution)/shard_map/rows_twin_3/ppermute | solution.py:194
  111.9 27.9 %collective-permute-start.14 = (bf16[48,3584]{1,0:T(8,128)(2,1)S(1)}, bf16[48,3584]{1,0:T(8,128)(2,1)S(1)}, u32[]{:S(2)}, u32[]{:S(2)}) collective-permute-start(bf16[48,3584]{1,0:T(8,128)(2,1)S(1)} %add_convert_fusion.2), channel_id=1, source_target_pairs={{0,2},{1,3},{2,6},{3,7},{4,0},{5,1},{6,4},{7,5},{8,10},{9,11},{10,... | collective-permute-start | bytes 1032200 | tf_op jit(solution)/shard_map/shares_ring_1_0/ppermute | solution.py:208
  112.8 27.0 %collective-permute-start.13 = (bf16[48,3584]{1,0:T(8,128)(2,1)S(1)}, bf16[48,3584]{1,0:T(8,128)(2,1)S(1)}, u32[]{:S(2)}, u32[]{:S(2)}) collective-permute-start(bf16[48,3584]{1,0:T(8,128)(2,1)S(1)} %collective-permute-done.7), channel_id=1, source_target_pairs={{0,2},{1,3},{2,6},{3,7},{4,0},{5,1},{6,4},{7,5},{8,10},{9,11},{10,... | collective-permute-start | bytes 1032200 | tf_op jit(solution)/shard_map/shares_ring_0_1/ppermute | solution.py:208
  116.3 23.5 %collective-permute-start.17 = (bf16[48,3584]{1,0:T(8,128)(2,1)S(1)}, bf16[48,3584]{1,0:T(8,128)(2,1)S(1)}, u32[]{:S(2)}, u32[]{:S(2)}) collective-permute-start(bf16[48,3584]{1,0:T(8,128)(2,1)S(1)} %get-tuple-element.211), channel_id=1, source_target_pairs={{0,24},{8,16},{16,8},{24,0},{1,25},{9,17},{17,9},{25,1},{2,26},{10... | collective-permute-start | bytes 1032200 | tf_op jit(solution)/shard_map/reduce_2_3/ppermute | solution.py:202
  118.8 21.0 %collective-permute-start.16 = (bf16[48,3584]{1,0:T(8,128)(2,1)S(1)}, bf16[48,3584]{1,0:T(8,128)(2,1)S(1)}, u32[]{:S(2)}, u32[]{:S(2)}) collective-permute-start(bf16[48,3584]{1,0:T(8,128)(2,1)S(1)} %get-tuple-element.212), channel_id=1, source_target_pairs={{0,16},{8,24},{16,0},{24,8},{1,17},{9,25},{17,1},{25,9},{2,18},{10... | collective-permute-start | bytes 1032200 | tf_op jit(solution)/shard_map/reduce_2_2/ppermute | solution.py:202
  119.3 20.5 %collective-permute-start.15 = (bf16[48,3584]{1,0:T(8,128)(2,1)S(1)}, bf16[48,3584]{1,0:T(8,128)(2,1)S(1)}, u32[]{:S(2)}, u32[]{:S(2)}) collective-permute-start(bf16[48,3584]{1,0:T(8,128)(2,1)S(1)} %get-tuple-element.213), channel_id=1, source_target_pairs={{0,8},{8,0},{16,24},{24,16},{1,9},{9,1},{17,25},{25,17},{2,10},{10... | collective-permute-start | bytes 1032200 | tf_op jit(solution)/shard_map/reduce_2_1/ppermute | solution.py:202
  140.0 12.0 %collective-permute-start.21 = (bf16[48,3584]{1,0:T(8,128)(2,1)S(1)}, bf16[48,3584]{1,0:T(8,128)(2,1)S(1)}, u32[]{:S(2)}, u32[]{:S(2)}) collective-permute-start(bf16[48,3584]{1,0:T(8,128)(2,1)S(1)} %add_convert_fusion.1), channel_id=1, source_target_pairs={{0,2},{1,3},{2,6},{3,7},{4,0},{5,1},{6,4},{7,5},{8,10},{9,11},{10,... | collective-permute-start | bytes 1032200 | tf_op jit(solution)/shard_map/shares_ring_2_0/ppermute | solution.py:208
  140.1 19.2 %collective-permute-start.19 = (bf16[48,3584]{1,0:T(8,128)(2,1)S(1)}, bf16[48,3584]{1,0:T(8,128)(2,1)S(1)}, u32[]{:S(2)}, u32[]{:S(2)}) collective-permute-start(bf16[48,3584]{1,0:T(8,128)(2,1)S(1)} %collective-permute-done.13), channel_id=1, source_target_pairs={{0,2},{1,3},{2,6},{3,7},{4,0},{5,1},{6,4},{7,5},{8,10},{9,11},{10,... | collective-permute-start | bytes 1032200 | tf_op jit(solution)/shard_map/shares_ring_0_2/ppermute | solution.py:208
  140.8 24.0 %collective-permute-start.20 = (bf16[48,3584]{1,0:T(8,128)(2,1)S(1)}, bf16[48,3584]{1,0:T(8,128)(2,1)S(1)}, u32[]{:S(2)}, u32[]{:S(2)}) collective-permute-start(bf16[48,3584]{1,0:T(8,128)(2,1)S(1)} %collective-permute-done.14), channel_id=1, source_target_pairs={{0,2},{1,3},{2,6},{3,7},{4,0},{5,1},{6,4},{7,5},{8,10},{9,11},{10,... | collective-permute-start | bytes 1032200 | tf_op jit(solution)/shard_map/shares_ring_1_1/ppermute | solution.py:208
  142.7 22.1 %collective-permute-start.24 = (bf16[48,3584]{1,0:T(8,128)(2,1)}, bf16[48,3584]{1,0:T(8,128)(2,1)}, u32[]{:S(2)}, u32[]{:S(2)}) collective-permute-start(bf16[48,3584]{1,0:T(8,128)(2,1)} %get-tuple-element.207), channel_id=1, source_target_pairs={{0,24},{8,16},{16,8},{24,0},{1,25},{9,17},{17,9},{25,1},{2,26},{10... | collective-permute-start | bytes 1032200 | tf_op jit(solution)/shard_map/reduce_3_3/ppermute | solution.py:202
  145.1 19.7 %collective-permute-start.23 = (bf16[48,3584]{1,0:T(8,128)(2,1)}, bf16[48,3584]{1,0:T(8,128)(2,1)}, u32[]{:S(2)}, u32[]{:S(2)}) collective-permute-start(bf16[48,3584]{1,0:T(8,128)(2,1)} %get-tuple-element.208), channel_id=1, source_target_pairs={{0,16},{8,24},{16,0},{24,8},{1,17},{9,25},{17,1},{25,9},{2,18},{10... | collective-permute-start | bytes 1032200 | tf_op jit(solution)/shard_map/reduce_3_2/ppermute | solution.py:202
  152.0 12.8 %collective-permute-start.22 = (bf16[48,3584]{1,0:T(8,128)(2,1)}, bf16[48,3584]{1,0:T(8,128)(2,1)}, u32[]{:S(2)}, u32[]{:S(2)}) collective-permute-start(bf16[48,3584]{1,0:T(8,128)(2,1)} %get-tuple-element.209), channel_id=1, source_target_pairs={{0,8},{8,0},{16,24},{24,16},{1,9},{9,1},{17,25},{25,17},{2,10},{10... | collective-permute-start | bytes 1032200 | tf_op jit(solution)/shard_map/reduce_3_1/ppermute | solution.py:202
  166.3 11.9 %collective-permute-start.30 = (bf16[48,3584]{1,0:T(8,128)(2,1)S(1)}, bf16[48,3584]{1,0:T(8,128)(2,1)S(1)}, u32[]{:S(2)}, u32[]{:S(2)}) collective-permute-start(bf16[48,3584]{1,0:T(8,128)(2,1)S(1)} %add_convert_fusion), channel_id=1, source_target_pairs={{0,2},{1,3},{2,6},{3,7},{4,0},{5,1},{6,4},{7,5},{8,10},{9,11},{10,... | collective-permute-start | bytes 1032200 | tf_op jit(solution)/shard_map/shares_ring_3_0/ppermute | solution.py:208
  166.6 12.0 %collective-permute-start.27 = (bf16[48,3584]{1,0:T(8,128)(2,1)S(1)}, bf16[48,3584]{1,0:T(8,128)(2,1)S(1)}, u32[]{:S(2)}, u32[]{:S(2)}) collective-permute-start(bf16[48,3584]{1,0:T(8,128)(2,1)S(1)} %get-tuple-element.203), channel_id=1, source_target_pairs={{0,24},{8,16},{16,8},{24,0},{1,25},{9,17},{17,9},{25,1},{2,26},{10... | collective-permute-start | bytes 1032200 | tf_op jit(solution)/shard_map/deliver_0_3/ppermute | solution.py:217
  169.1 14.0 %collective-permute-start.26 = (bf16[48,3584]{1,0:T(8,128)(2,1)S(1)}, bf16[48,3584]{1,0:T(8,128)(2,1)S(1)}, u32[]{:S(2)}, u32[]{:S(2)}) collective-permute-start(bf16[48,3584]{1,0:T(8,128)(2,1)S(1)} %get-tuple-element.204), channel_id=1, source_target_pairs={{0,16},{8,24},{16,0},{24,8},{1,17},{9,25},{17,1},{25,9},{2,18},{10... | collective-permute-start | bytes 1032200 | tf_op jit(solution)/shard_map/deliver_0_2/ppermute | solution.py:217
  169.6 13.6 %collective-permute-start.25 = (bf16[48,3584]{1,0:T(8,128)(2,1)S(1)}, bf16[48,3584]{1,0:T(8,128)(2,1)S(1)}, u32[]{:S(2)}, u32[]{:S(2)}) collective-permute-start(bf16[48,3584]{1,0:T(8,128)(2,1)S(1)} %get-tuple-element.205), channel_id=1, source_target_pairs={{0,8},{8,0},{16,24},{24,16},{1,9},{9,1},{17,25},{25,17},{2,10},{10... | collective-permute-start | bytes 1032200 | tf_op jit(solution)/shard_map/deliver_0_1/ppermute | solution.py:217
  170.1 15.5 %collective-permute-start.28 = (bf16[48,3584]{1,0:T(8,128)(2,1)S(1)}, bf16[48,3584]{1,0:T(8,128)(2,1)S(1)}, u32[]{:S(2)}, u32[]{:S(2)}) collective-permute-start(bf16[48,3584]{1,0:T(8,128)(2,1)S(1)} %collective-permute-done.20), channel_id=1, source_target_pairs={{0,2},{1,3},{2,6},{3,7},{4,0},{5,1},{6,4},{7,5},{8,10},{9,11},{10,... | collective-permute-start | bytes 1032200 | tf_op jit(solution)/shard_map/shares_ring_1_2/ppermute | solution.py:208
  178.2 11.9 %collective-permute-start.29 = (bf16[48,3584]{1,0:T(8,128)(2,1)S(1)}, bf16[48,3584]{1,0:T(8,128)(2,1)S(1)}, u32[]{:S(2)}, u32[]{:S(2)}) collective-permute-start(bf16[48,3584]{1,0:T(8,128)(2,1)S(1)} %collective-permute-done.21), channel_id=1, source_target_pairs={{0,2},{1,3},{2,6},{3,7},{4,0},{5,1},{6,4},{7,5},{8,10},{9,11},{10,... | collective-permute-start | bytes 1032200 | tf_op jit(solution)/shard_map/shares_ring_2_1/ppermute | solution.py:208
  190.4 21.1 %collective-permute-start.31 = (bf16[192,3584]{1,0:T(8,128)(2,1)S(1)}, bf16[192,3584]{1,0:T(8,128)(2,1)S(1)}, u32[]{:S(2)}, u32[]{:S(2)}) collective-permute-start(bf16[192,3584]{1,0:T(8,128)(2,1)S(1)} %pad_maximum_fusion.refs_0_), channel_id=1, source_target_pairs={{0,1},{1,0},{2,3},{3,2},{4,5},{5,4},{6,7},{7,6},{8,9},{9,8},{10,11... | collective-permute-start | bytes 4128776 | tf_op jit(solution)/shard_map/deliver_twin_0/ppermute | solution.py:222
  190.5 11.8 %collective-permute-start.35 = (bf16[48,3584]{1,0:T(8,128)(2,1)S(1)}, bf16[48,3584]{1,0:T(8,128)(2,1)S(1)}, u32[]{:S(2)}, u32[]{:S(2)}) collective-permute-start(bf16[48,3584]{1,0:T(8,128)(2,1)S(1)} %collective-permute-done.29), channel_id=1, source_target_pairs={{0,2},{1,3},{2,6},{3,7},{4,0},{5,1},{6,4},{7,5},{8,10},{9,11},{10,... | collective-permute-start | bytes 1032200 | tf_op jit(solution)/shard_map/shares_ring_2_2/ppermute | solution.py:208
  190.6 18.7 %collective-permute-start.36 = (bf16[48,3584]{1,0:T(8,128)(2,1)S(1)}, bf16[48,3584]{1,0:T(8,128)(2,1)S(1)}, u32[]{:S(2)}, u32[]{:S(2)}) collective-permute-start(bf16[48,3584]{1,0:T(8,128)(2,1)S(1)} %collective-permute-done.30), channel_id=1, source_target_pairs={{0,2},{1,3},{2,6},{3,7},{4,0},{5,1},{6,4},{7,5},{8,10},{9,11},{10,... | collective-permute-start | bytes 1032200 | tf_op jit(solution)/shard_map/shares_ring_3_1/ppermute | solution.py:208
  193.0 16.2 %collective-permute-start.34 = (bf16[48,3584]{1,0:T(8,128)(2,1)S(1)}, bf16[48,3584]{1,0:T(8,128)(2,1)S(1)}, u32[]{:S(2)}, u32[]{:S(2)}) collective-permute-start(bf16[48,3584]{1,0:T(8,128)(2,1)S(1)} %get-tuple-element.195), channel_id=1, source_target_pairs={{0,24},{8,16},{16,8},{24,0},{1,25},{9,17},{17,9},{25,1},{2,26},{10... | collective-permute-start | bytes 1032200 | tf_op jit(solution)/shard_map/deliver_1_3/ppermute | solution.py:217
  194.0 16.9 %collective-permute-start.33 = (bf16[48,3584]{1,0:T(8,128)(2,1)S(1)}, bf16[48,3584]{1,0:T(8,128)(2,1)S(1)}, u32[]{:S(2)}, u32[]{:S(2)}) collective-permute-start(bf16[48,3584]{1,0:T(8,128)(2,1)S(1)} %get-tuple-element.196), channel_id=1, source_target_pairs={{0,16},{8,24},{16,0},{24,8},{1,17},{9,25},{17,1},{25,9},{2,18},{10... | collective-permute-start | bytes 1032200 | tf_op jit(solution)/shard_map/deliver_1_2/ppermute | solution.py:217
  202.3 9.2 %collective-permute-start.32 = (bf16[48,3584]{1,0:T(8,128)(2,1)S(1)}, bf16[48,3584]{1,0:T(8,128)(2,1)S(1)}, u32[]{:S(2)}, u32[]{:S(2)}) collective-permute-start(bf16[48,3584]{1,0:T(8,128)(2,1)S(1)} %get-tuple-element.197), channel_id=1, source_target_pairs={{0,8},{8,0},{16,24},{24,16},{1,9},{9,1},{17,25},{25,17},{2,10},{10... | collective-permute-start | bytes 1032200 | tf_op jit(solution)/shard_map/deliver_1_1/ppermute | solution.py:217
  212.7 19.2 %collective-permute-start.37 = (bf16[192,3584]{1,0:T(8,128)(2,1)S(1)}, bf16[192,3584]{1,0:T(8,128)(2,1)S(1)}, u32[]{:S(2)}, u32[]{:S(2)}) collective-permute-start(bf16[192,3584]{1,0:T(8,128)(2,1)S(1)} %pad_maximum_fusion.1.refs_1_), channel_id=1, source_target_pairs={{0,1},{1,0},{2,3},{3,2},{4,5},{5,4},{6,7},{7,6},{8,9},{9,8},{10,11... | collective-permute-start | bytes 4128776 | tf_op jit(solution)/shard_map/deliver_twin_1/ppermute | solution.py:222
  212.7 11.4 %collective-permute-start.41 = (bf16[48,3584]{1,0:T(8,128)(2,1)S(1)}, bf16[48,3584]{1,0:T(8,128)(2,1)S(1)}, u32[]{:S(2)}, u32[]{:S(2)}) collective-permute-start(bf16[48,3584]{1,0:T(8,128)(2,1)S(1)} %collective-permute-done.36), channel_id=1, source_target_pairs={{0,2},{1,3},{2,6},{3,7},{4,0},{5,1},{6,4},{7,5},{8,10},{9,11},{10,... | collective-permute-start | bytes 1032200 | tf_op jit(solution)/shard_map/shares_ring_3_2/ppermute | solution.py:208
  213.2 11.9 %collective-permute-start.40 = (bf16[48,3584]{1,0:T(8,128)(2,1)S(1)}, bf16[48,3584]{1,0:T(8,128)(2,1)S(1)}, u32[]{:S(2)}, u32[]{:S(2)}) collective-permute-start(bf16[48,3584]{1,0:T(8,128)(2,1)S(1)} %get-tuple-element.187), channel_id=1, source_target_pairs={{0,24},{8,16},{16,8},{24,0},{1,25},{9,17},{17,9},{25,1},{2,26},{10... | collective-permute-start | bytes 1032200 | tf_op jit(solution)/shard_map/deliver_2_3/ppermute | solution.py:217
  215.7 16.0 %collective-permute-start.39 = (bf16[48,3584]{1,0:T(8,128)(2,1)S(1)}, bf16[48,3584]{1,0:T(8,128)(2,1)S(1)}, u32[]{:S(2)}, u32[]{:S(2)}) collective-permute-start(bf16[48,3584]{1,0:T(8,128)(2,1)S(1)} %get-tuple-element.188), channel_id=1, source_target_pairs={{0,16},{8,24},{16,0},{24,8},{1,17},{9,25},{17,1},{25,9},{2,18},{10... | collective-permute-start | bytes 1032200 | tf_op jit(solution)/shard_map/deliver_2_2/ppermute | solution.py:217
  216.2 15.6 %collective-permute-start.38 = (bf16[48,3584]{1,0:T(8,128)(2,1)S(1)}, bf16[48,3584]{1,0:T(8,128)(2,1)S(1)}, u32[]{:S(2)}, u32[]{:S(2)}) collective-permute-start(bf16[48,3584]{1,0:T(8,128)(2,1)S(1)} %get-tuple-element.189), channel_id=1, source_target_pairs={{0,8},{8,0},{16,24},{24,16},{1,9},{9,1},{17,25},{25,17},{2,10},{10... | collective-permute-start | bytes 1032200 | tf_op jit(solution)/shard_map/deliver_2_1/ppermute | solution.py:217
  233.0 19.1 %collective-permute-start.42 = (bf16[192,3584]{1,0:T(8,128)(2,1)S(1)}, bf16[192,3584]{1,0:T(8,128)(2,1)S(1)}, u32[]{:S(2)}, u32[]{:S(2)}) collective-permute-start(bf16[192,3584]{1,0:T(8,128)(2,1)S(1)} %pad_maximum_fusion.2.refs_2_), channel_id=1, source_target_pairs={{0,1},{1,0},{2,3},{3,2},{4,5},{5,4},{6,7},{7,6},{8,9},{9,8},{10,11... | collective-permute-start | bytes 4128776 | tf_op jit(solution)/shard_map/deliver_twin_2/ppermute | solution.py:222
  233.2 11.9 %collective-permute-start.45 = (bf16[48,3584]{1,0:T(8,128)(2,1)S(1)}, bf16[48,3584]{1,0:T(8,128)(2,1)S(1)}, u32[]{:S(2)}, u32[]{:S(2)}) collective-permute-start(bf16[48,3584]{1,0:T(8,128)(2,1)S(1)} %get-tuple-element.179), channel_id=1, source_target_pairs={{0,24},{8,16},{16,8},{24,0},{1,25},{9,17},{17,9},{25,1},{2,26},{10... | collective-permute-start | bytes 1032200 | tf_op jit(solution)/shard_map/deliver_3_3/ppermute | solution.py:217
  235.0 17.1 %collective-permute-start.44 = (bf16[48,3584]{1,0:T(8,128)(2,1)S(1)}, bf16[48,3584]{1,0:T(8,128)(2,1)S(1)}, u32[]{:S(2)}, u32[]{:S(2)}) collective-permute-start(bf16[48,3584]{1,0:T(8,128)(2,1)S(1)} %get-tuple-element.180), channel_id=1, source_target_pairs={{0,16},{8,24},{16,0},{24,8},{1,17},{9,25},{17,1},{25,9},{2,18},{10... | collective-permute-start | bytes 1032200 | tf_op jit(solution)/shard_map/deliver_3_2/ppermute | solution.py:217
  236.3 15.8 %collective-permute-start.43 = (bf16[48,3584]{1,0:T(8,128)(2,1)S(1)}, bf16[48,3584]{1,0:T(8,128)(2,1)S(1)}, u32[]{:S(2)}, u32[]{:S(2)}) collective-permute-start(bf16[48,3584]{1,0:T(8,128)(2,1)S(1)} %get-tuple-element.181), channel_id=1, source_target_pairs={{0,8},{8,0},{16,24},{24,16},{1,9},{9,1},{17,25},{25,17},{2,10},{10... | collective-permute-start | bytes 1032200 | tf_op jit(solution)/shard_map/deliver_3_1/ppermute | solution.py:217
  282.3 6.4 %collective-permute-start.47 = (bf16[512,128]{1,0:T(8,128)(2,1)S(1)}, bf16[512,128]{1,0:T(8,128)(2,1)S(1)}, u32[]{:S(2)}, u32[]{:S(2)}) collective-permute-start(bf16[512,128]{1,0:T(8,128)(2,1)S(1)} %get-tuple-element.223), channel_id=1, source_target_pairs={{0,8},{8,0},{16,24},{24,16},{1,9},{9,1},{17,25},{25,17},{2,10},{10... | collective-permute-start | bytes 393224 | tf_op jit(solution)/shard_map/check_reduce_1/ppermute | solution.py:250
  283.8 7.8 %collective-permute-start.49 = (bf16[512,128]{1,0:T(8,128)(2,1)S(1)}, bf16[512,128]{1,0:T(8,128)(2,1)S(1)}, u32[]{:S(2)}, u32[]{:S(2)}) collective-permute-start(bf16[512,128]{1,0:T(8,128)(2,1)S(1)} %get-tuple-element.224), channel_id=1, source_target_pairs={{0,24},{8,16},{16,8},{24,0},{1,25},{9,17},{17,9},{25,1},{2,26},{10... | collective-permute-start | bytes 393224 | tf_op jit(solution)/shard_map/check_reduce_3/ppermute | solution.py:250
  285.2 7.8 %collective-permute-start.48 = (bf16[512,128]{1,0:T(8,128)(2,1)S(1)}, bf16[512,128]{1,0:T(8,128)(2,1)S(1)}, u32[]{:S(2)}, u32[]{:S(2)}) collective-permute-start(bf16[512,128]{1,0:T(8,128)(2,1)S(1)} %get-tuple-element.225), channel_id=1, source_target_pairs={{0,16},{8,24},{16,0},{24,8},{1,17},{9,25},{17,1},{25,9},{2,18},{10... | collective-permute-start | bytes 393224 | tf_op jit(solution)/shard_map/check_reduce_2/ppermute | solution.py:250
  (15 other events, 37.0 us)

commit v2 on v1

v2 whole, which is shorter than its diff:
```python
import functools

import jax
import jax.numpy as jnp
from jax import lax
from jax.experimental import pallas as pl
from jax.experimental.pallas import tpu as pltpu
from jax.sharding import PartitionSpec as P

BF16 = jnp.bfloat16
F32 = jnp.float32
VMEM_BYTES = 48 * 2**20


def ring_order(n):
    return [0, *range(1, n, 2), *reversed(range(2, n, 2))]


def look_up(table, index):
    return sum(jnp.where(index == i, v, 0) for i, v in enumerate(table))


def pick(arrays, index):
    out = arrays[0]
    for i in range(1, len(arrays)):
        out = jnp.where(index == i, arrays[i], out)
    return out


def block_of(width, limit):
    return max(b for b in range(128, limit + 1, 128) if width % b == 0)


def project_kernel(scalars, mine, theirs, panel, out, rows):
    count = mine.shape[0]

    @pl.when(pl.program_id(0) == 0)
    def _():
        rows[:count] = mine[...]
        rows[count:] = theirs[...]

    core = scalars[0]
    product = jnp.dot(rows[...], panel[...], preferred_element_type=F32).astype(BF16)
    out[core] = product[:count]
    out[1 - core] = product[count:]


def project(scalars, mine, theirs, panel):
    count, depth = mine.shape
    width = panel.shape[1]
    block = block_of(width, 512)
    once = pl.Buffered(1)
    return pl.pallas_call(
        project_kernel,
        grid_spec=pltpu.PrefetchScalarGridSpec(
            num_scalar_prefetch=1,
            grid=(width // block,),
            in_specs=[
                pl.BlockSpec((count, depth), lambda i, s: (0, 0), pipeline_mode=once),
                pl.BlockSpec((count, depth), lambda i, s: (0, 0), pipeline_mode=once),
                pl.BlockSpec((depth, block), lambda i, s: (0, i)),
            ],
            out_specs=pl.BlockSpec((2, count, block), lambda i, s: (0, 0, i)),
            scratch_shapes=[pltpu.VMEM((2 * count, depth), BF16)],
        ),
        out_shape=jax.ShapeDtypeStruct((2, count, width), BF16),
        compiler_params=pltpu.CompilerParams(vmem_limit_bytes=VMEM_BYTES),
        name="project",
    )(scalars, mine, theirs, panel).reshape(2 * count, width)


def merge(a, projected):
    return (0.5 * (a.astype(F32) + projected.astype(F32))).astype(BF16)


def merge_kernel(steps, scalars, own, far, a_gu, a_dn, *refs):
    gu_out, dn_out = refs[-2:]
    shard = own.shape[0] // 2
    gu_rows, dn_rows = a_gu.shape[0] // 2, a_dn.shape[0] // 2

    def fill(piece):
        for k in range(2):
            gu, dn = pl.ds(k * gu_rows, gu_rows), pl.ds(k * dn_rows, dn_rows)
            gu_out[gu] = merge(a_gu[gu], piece[pl.ds(k * shard, gu_rows)])
            dn_out[dn] = merge(a_dn[dn], piece[pl.ds(k * shard + gu_rows, dn_rows)])

    @pl.when(pl.program_id(0) < steps)
    def _():
        fill(own)

    @pl.when(pl.program_id(0) >= steps)
    def _():
        fill(far)


def column_specs(width, block, t, groups, piece, a_gu, a_dn):
    steps = width // block
    piece_rows = (a_gu.shape[0] + a_dn.shape[0]) // groups

    def column(i, s):
        return jnp.where(i < steps, s[0], 1 - s[0]) * steps + lax.rem(i, steps)

    own = pl.BlockSpec((piece_rows, block), lambda i, s: (piece, jnp.minimum(i, steps - 1)))
    far = pl.BlockSpec((piece_rows, block), lambda i, s: (piece, jnp.maximum(i - steps, 0)))
    group = [pl.BlockSpec((a.shape[0] // groups, block), lambda i, s: (s[1 + t], column(i, s))) for a in (a_gu, a_dn)]
    slab = [pl.BlockSpec((a.shape[0], block), lambda i, s: (0, column(i, s))) for a in (a_gu, a_dn)]
    return steps, [own, far], group, slab


def merge_group(scalars, t, groups, piece, own, far, a_gu, a_dn, sofar):
    width = own.shape[1]
    block = block_of(width, 2048)
    steps, pieces, group, _ = column_specs(width, block, t, groups, piece, a_gu, a_dn)
    anywhere = [pl.BlockSpec(memory_space=pl.ANY)] * len(sofar)
    return pl.pallas_call(
        functools.partial(merge_kernel, steps),
        grid_spec=pltpu.PrefetchScalarGridSpec(
            num_scalar_prefetch=1, grid=(2 * steps,), in_specs=pieces + group + anywhere, out_specs=group
        ),
        out_shape=[jax.ShapeDtypeStruct(a.shape, BF16) for a in (a_gu, a_dn)],
        input_output_aliases={5 + i: i for i in range(len(sofar))},
        compiler_params=pltpu.CompilerParams(vmem_limit_bytes=VMEM_BYTES),
        name="merge",
    )(scalars, own, far, a_gu, a_dn, *sofar)


def forward_kernel(steps, groups, t, scalars, tokens, own, far, a_gu, a_dn, gu, dn, gu_out, dn_out, check_out, gu_all, dn_all, total):
    step = pl.program_id(0)
    features = tokens.shape[1]
    scale = features ** (-0.5)
    merge_kernel(steps, scalars, own, far, a_gu, a_dn, gu_out, dn_out)
    for whole, before, part in ((gu_all, gu, gu_out), (dn_all, dn, dn_out)):
        whole[...] = before[...]
        rows = part.shape[0]
        whole[pl.ds(pl.multiple_of(scalars[1 + t] * rows, rows), rows)] = part[...]
    block = gu.shape[1]
    chunk = block_of(block, 256)
    part = 0.0
    for start in range(0, block, chunk):
        columns = slice(start, start + chunk)
        gate = jnp.dot(tokens[...], gu_all[:features, columns], preferred_element_type=F32) * (0.5 * scale)
        up = jnp.dot(tokens[...], gu_all[features:, columns], preferred_element_type=F32) * scale
        hidden = (gate * (1.0 + jnp.tanh(gate)) * up).astype(BF16)
        part += lax.dot_general(hidden, dn_all[:, columns], (((1,), (1,)), ((), ())), preferred_element_type=F32)

    @pl.when(step == 0)
    def _():
        total[...] = part

    @pl.when(step > 0)
    def _():
        total[...] += part

    @pl.when(step == 2 * steps - 1)
    def _():
        width = features // groups
        fold = max(1, 128 // width)
        rows = total.shape[0] // fold
        for j in range(groups):
            packed = [total[f * rows : (f + 1) * rows, j * width : (j + 1) * width] for f in range(fold)]
            check_out[j] = jnp.concatenate(packed, axis=1).astype(BF16)


def forward(scalars, tokens, t, groups, own, far, a_gu, a_dn, sofar):
    width = own.shape[1]
    block = block_of(width, 2048)
    count, features = tokens.shape
    fold = max(1, 128 // (features // groups))
    check_shape = (groups, count // fold, fold * features // groups)
    steps, pieces, group, slab = column_specs(width, block, t, groups, 0, a_gu, a_dn)
    return pl.pallas_call(
        functools.partial(forward_kernel, steps, groups, t),
        grid_spec=pltpu.PrefetchScalarGridSpec(
            num_scalar_prefetch=1,
            grid=(2 * steps,),
            in_specs=[pl.BlockSpec(tokens.shape, lambda i, s: (0, 0))] + pieces + group + slab,
            out_specs=group + [pl.BlockSpec(check_shape, lambda i, s: (0, 0, 0))],
            scratch_shapes=[
                pltpu.VMEM((a_gu.shape[0], block), BF16),
                pltpu.VMEM((a_dn.shape[0], block), BF16),
                pltpu.VMEM((count, features), F32),
            ],
        ),
        out_shape=[
            jax.ShapeDtypeStruct(a_gu.shape, BF16),
            jax.ShapeDtypeStruct(a_dn.shape, BF16),
            jax.ShapeDtypeStruct(check_shape, BF16),
        ],
        input_output_aliases={6: 0, 7: 1},
        compiler_params=pltpu.CompilerParams(vmem_limit_bytes=VMEM_BYTES),
        name="forward",
    )(scalars, tokens, own, far, a_gu, a_dn, *sofar)


def on_device(b_gate_up, b_down, a_gate_up, a_down, transform, check_tokens):
    n = lax.axis_size("row")
    assert lax.axis_size("col") == 2 * n
    q = lax.axis_index("row")
    col = lax.axis_index("col")
    z, core = col // 2, col % 2
    order = ring_order(n)
    place = [order.index(i) for i in range(n)]
    after = {order[i]: order[(i + 1) % n] for i in range(n)}
    ring = [(2 * i + k, 2 * after[i] + k) for i in range(n) for k in range(2)]
    back = [(j, i) for i, j in ring]
    twin = [(i, i ^ 1) for i in range(2 * n)]
    began = [look_up(order, (look_up(place, q) - t) % n) for t in range(n)]
    scalars = jnp.stack([core, *began]).astype(jnp.int32)

    def peers(d):
        return [(i, i ^ d) for i in range(n)]

    width = transform.shape[1]
    rows = jnp.concatenate([b_gate_up, b_down], axis=0)
    part_rows = 2 * rows.shape[0] // n

    def cat(arrays):
        return arrays[0] if len(arrays) == 1 else jnp.concatenate(arrays, axis=0)

    def along_ring(perm, name, held, step):
        if not step:
            return None
        with jax.named_scope(name):
            return lax.ppermute(cat([held[t][i] for t, i, _ in step]), "col", perm)

    def split(arrived, held, step):
        for i, (t, _, to) in enumerate(step):
            held[t][to] = arrived[i * part_rows : (i + 1) * part_rows]

    def for_row(held, r):
        return pick([held[i] for i in range(n)], (look_up(place, r) - look_up(place, z)) % n)

    half = n // 2
    partial, sums, held, got = {}, {}, {}, {}
    sofar = []
    for step in range(n + half + 3):
        out = {}
        if step < n:
            if step < n - 1:
                with jax.named_scope(f"rows_ring_{step}"):
                    out["rows"] = lax.ppermute(rows, "col", ring)
            with jax.named_scope(f"rows_twin_{step}"):
                other = lax.ppermute(rows, "col", twin)
            out["partial"] = project(scalars, rows, other, transform)
        if 0 <= step - 1 < n:
            parts = partial[step - 1].reshape(n, part_rows, width)
            out["sums"] = [lax.dynamic_index_in_dim(parts, q, keepdims=False)]
            for d in range(1, n):
                with jax.named_scope(f"reduce_{step - 1}_{d}"):
                    part = lax.dynamic_index_in_dim(parts, q ^ d, keepdims=False)
                    out["sums"].append(lax.ppermute(part, "row", peers(d)))
        if 0 <= step - 2 < n:
            held[step - 2] = {0: sum(v.astype(F32) for v in sums[step - 2]).astype(BF16)}
        onward, backward = [], []
        for t in range(n):
            hop = step - 2 - t
            if 0 <= hop < half:
                onward.append((t, hop, hop + 1))
                if hop:
                    backward.append((t, (1 - hop) % n, n - hop))
        out["onward"] = along_ring(back, f"shares_onward_{step}", held, onward)
        out["backward"] = along_ring(ring, f"shares_backward_{step}", held, backward)
        deliver = [t for t in range(n) if step == max(t + 2 + half, n + 1)]
        if deliver:
            out["got"] = [cat([for_row(held[t], q) for t in deliver])]
            for d in range(1, n):
                with jax.named_scope(f"deliver_{step}_{d}"):
                    out["got"].append(lax.ppermute(cat([for_row(held[t], q ^ d) for t in deliver]), "row", peers(d)))
        if got:
            arrived = got.pop(step - 1)
            count = arrived[0].shape[0] // part_rows
            pieces = []
            for i in range(count):
                own = [v[i * part_rows : (i + 1) * part_rows] for v in arrived]
                pieces += [pick(own, q ^ j) for j in range(n)]
            own = cat(pieces)
            with jax.named_scope(f"deliver_twin_{step}"):
                far = lax.ppermute(own, "col", twin)
            for i, t in enumerate(delivered):
                if t < n - 1:
                    sofar = merge_group(scalars, t, n, i, own, far, a_gate_up, a_down, sofar)
        out["sofar"] = sofar

        leaves, tree = jax.tree.flatten(out)
        out = jax.tree.unflatten(tree, lax.optimization_barrier(leaves))
        rows = out.get("rows")
        if "partial" in out:
            partial[step] = out["partial"]
        if "sums" in out:
            sums[step - 1] = out["sums"]
        split(out["onward"], held, onward)
        split(out["backward"], held, backward)
        if "got" in out:
            got[step] = out["got"]
            delivered = deliver
        sofar = out["sofar"]

    merged_gate_up, merged_down, parts = forward(
        scalars, check_tokens, n - 1, n, own, far, a_gate_up, a_down, sofar
    )
    total = lax.dynamic_index_in_dim(parts, q, keepdims=False).astype(F32)
    for d in range(1, n):
        with jax.named_scope(f"check_reduce_{d}"):
            sent = lax.dynamic_index_in_dim(parts, q ^ d, keepdims=False)
            total = total + lax.ppermute(sent, "row", peers(d)).astype(F32)
    hidden_units = n * transform.shape[0]
    check = (total * hidden_units ** (-0.5)).astype(BF16)
    count, features = check_tokens.shape
    share = features // n
    check = check.reshape(check.shape[0], -1, share).swapaxes(0, 1).reshape(count, share)
    return merged_gate_up, merged_down, check


def solution(mesh):
    return jax.shard_map(
        on_device,
        mesh=mesh,
        in_specs=(
            P("col", "row"),
            P("col", "row"),
            P(None, "row"),
            P(None, "row"),
            P("row", "col"),
            P("col", None),
        ),
        out_specs=(P(None, "row"), P(None, "row"), P("col", "row")),
        check_vma=False,
    )
```

time: 295 us -> 275 us (0.932)
  waiting for transfers between devices: 123 us -> 82.8 us
  Pallas kernels: 105 us -> 115 us
  starting transfers between devices: 51 us -> 59.5 us
  other arithmetic: 3.76 us -> 8.83 us
    ppermute x47 -> x40, waiting for transfers between devices: 116 us -> 76.7 us  [the longest x9 31 us: along_ring(): return lax.ppermute(cat([held[t][i] for t, i, _ in step]), 'col', perm)]
    pallas_call x1 -> x4, Pallas kernels: 24.7 us -> 34.1 us  [the longest x1 18.9 us: forward(): pl.pallas_call(functools.partial(forward_kernel, steps, groups, t), grid_...]
    ppermute x47 -> x40, starting transfers between devices: 47.4 us -> 55.9 us  [the longest x9 25.9 us: along_ring(): return lax.ppermute(cat([held[t][i] for t, i, _ in step]), 'col', perm)]
    unnamed x27 -> x15, local copies, waits for them, and re-layouts: 7.59 us -> 3.73 us
  transfers between devices with their start and end apart: 50 -> 43, of which waited for: 26 -> 17; matrix products, arithmetic and copies ran while one was open for 1% -> 3% of each run, Pallas kernels for 27% -> 35%
where the time goes in v2:
time: 275 us; the launch traced here: 274 us
  Pallas kernels  115 us (42%)
  waiting for transfers between devices  82.8 us (30%)
  starting transfers between devices  59.5 us (22%)
  other arithmetic  8.83 us (3%)
  local copies, waits for them, and re-layouts  7.03 us (3%)
    pallas_call x4, Pallas kernels, project(): pl.pallas_call(project_kernel, grid_spec=pltpu.PrefetchScalarGridSpec(num...  80.6 us
    ppermute x9, waiting for transfers between devices, along_ring(): return lax.ppermute(cat([held[t][i] for t, i, _ in step]), 'col', perm)  31 us
    ppermute x9, starting transfers between devices, along_ring(): return lax.ppermute(cat([held[t][i] for t, i, _ in step]), 'col', perm)  25.9 us
    ppermute x9, waiting for transfers between devices, on_device(): lax.ppermute(cat([for_row(held[t], q ^ d) for t in deliver]), 'row', peer...  24.6 us
    pallas_call x1, Pallas kernels, forward(): pl.pallas_call(functools.partial(forward_kernel, steps, groups, t), grid_...  18.9 us
    ppermute x3, waiting for transfers between devices, on_device(): out['rows'] = lax.ppermute(rows, 'col', ring)  18 us
    pallas_call x3, Pallas kernels, merge_group(): pl.pallas_call(functools.partial(merge_kernel, steps), grid_spec=pltpu.Pr...  15.2 us
    ppermute x12, starting transfers between devices, on_device(): out['sums'].append(lax.ppermute(part, 'row', peers(d)))  14.1 us
  transfers between devices with their start and end apart: 43, of which 17 were waited for; matrix products, arithmetic and copies ran while one was open for 3% of the time, Pallas kernels for 35%

profile of v2, /device:TPU:0, one launch (start us, length us, event | category | flops | bytes accessed | tf_op | source)
XLA Modules:
  0.0 273.8 jit_solution(9068474191634391754)
XLA Ops:
  0.6 1.3 constant_dynamic-update-slice_fusion.1
  2.5 2.6 collective-permute-start.1
  6.3 1.3 copy-done.1
  7.7 19.9 %project.4 = bf16[2,96,3584]{2,1,0:T(8,128)(2,1)S(1)} custom-call(s32[5]{0:T(128)S(1)} %stack.23.scalars, bf16[96,7168]{1,0:T(8,128)(2,1)S(1)} %constant_dynamic-update-slice_fusion.mine, bf16[96,7168]{1,0:T(8,128)(2,1)S(1)} %copy-done.1, bf16[7168,3584]{1,0:T(8,128)(2,1)} %panel.7), custom_call_target="tpu_custom_call" | custom-call | tf_op jit(solution)/shard_map/project/pallas_call | solution.py:53
  27.6 9.4 %collective-permute-done.1.mine = bf16[96,7168]{1,0:T(8,128)(2,1)} collective-permute-done((bf16[96,7168]{1,0:T(8,128)(2,1)S(1)}, bf16[96,7168]{1,0:T(8,128)(2,1)}, u32[]{:S(2)}, u32[]{:S(2)}) %collective-permute-start.1) | collective-permute-done | bytes 1376288 | tf_op jit(solution)/shard_map/rows_ring_0/ppermute | solution.py:241
  37.9 1.6 collective-permute-start.4
  39.4 1.5 collective-permute-start.5
  41.4 20.7 %project.5 = bf16[2,96,3584]{2,1,0:T(8,128)(2,1)S(1)} custom-call(s32[5]{0:T(128)S(1)} %stack.23.scalars, bf16[96,7168]{1,0:T(8,128)(2,1)} %collective-permute-done.1.mine, bf16[96,7168]{1,0:T(8,128)(2,1)} %collective-permute-done.2.theirs, bf16[7168,3584]{1,0:T(8,128)(2,1)} %panel.7), custom_call_target="tpu_custom_call" | custom-call | tf_op jit(solution)/shard_map/project/pallas_call | solution.py:53
  62.2 8.5 %collective-permute-done.3.mine = bf16[96,7168]{1,0:T(8,128)(2,1)S(1)} collective-permute-done((bf16[96,7168]{1,0:T(8,128)(2,1)}, bf16[96,7168]{1,0:T(8,128)(2,1)S(1)}, u32[]{:S(2)}, u32[]{:S(2)}) %collective-permute-start.3) | collective-permute-done | bytes 1376288 | tf_op jit(solution)/shard_map/rows_ring_1/ppermute | solution.py:241
  71.8 1.6 collective-permute-start.10
  73.4 1.5 collective-permute-start.11
  75.5 2.0 collective-permute-start.7
  77.6 19.9 %project.6 = bf16[2,96,3584]{2,1,0:T(8,128)(2,1)S(1)} custom-call(s32[5]{0:T(128)S(1)} %stack.23.scalars, bf16[96,7168]{1,0:T(8,128)(2,1)S(1)} %collective-permute-done.3.mine, bf16[96,7168]{1,0:T(8,128)(2,1)S(1)} %collective-permute-done.8.theirs, bf16[7168,3584]{1,0:T(8,128)(2,1)} %panel.7), custom_call_target="tpu_custom_call" | custom-call | tf_op jit(solution)/shard_map/project/pallas_call | solution.py:53
  97.5 1.4 collective-permute-start.14
  98.9 13.9 %collective-permute-done.7 = bf16[48,3584]{1,0:T(8,128)(2,1)S(1)} collective-permute-done((bf16[48,3584]{1,0:T(8,128)(2,1)S(1)}, bf16[48,3584]{1,0:T(8,128)(2,1)S(1)}, u32[]{:S(2)}, u32[]{:S(2)}) %collective-permute-start.7) | collective-permute-done | bytes 344096 | tf_op jit(solution)/shard_map/shares_onward_2/ppermute | solution.py:224
  115.2 1.5 collective-permute-start.17
  116.7 1.5 collective-permute-start.18
  118.7 19.9 %project.7 = bf16[2,96,3584]{2,1,0:T(8,128)(2,1)S(1)} custom-call(s32[5]{0:T(128)S(1)} %stack.23.scalars, bf16[96,7168]{1,0:T(8,128)(2,1)S(1)} %collective-permute-done.9.mine, bf16[96,7168]{1,0:T(8,128)(2,1)S(1)} %collective-permute-done.16.theirs, bf16[7168,3584]{1,0:T(8,128)(2,1)} %panel.7), custom_call_target="tpu_custom_call" | custom-call | tf_op jit(solution)/shard_map/project/pallas_call | solution.py:53
  138.6 1.9 collective-permute-start.13
  141.6 1.4 add_convert_fusion.1
  143.0 1.5 collective-permute-start.20
  144.6 1.6 collective-permute-start.21
  146.1 1.5 collective-permute-start.22
  148.1 1.2 select_select_fusion.17
  150.1 12.6 %collective-permute-start.25 = (bf16[48,3584]{1,0:T(8,128)(2,1)S(1)}, bf16[48,3584]{1,0:T(8,128)(2,1)S(1)}, u32[]{:S(2)}, u32[]{:S(2)}) collective-permute-start(bf16[48,3584]{1,0:T(8,128)(2,1)S(1)} %add_convert_fusion.1), channel_id=1, source_target_pairs={{0,2},{1,3},{2,6},{3,7},{4,0},{5,1},{6,4},{7,5},{8,10},{9,11},{10,... | collective-permute-start | bytes 1032200 | tf_op jit(solution)/shard_map/shares_backward_5/ppermute | solution.py:224
  162.7 2.6 collective-permute-done.20
  166.7 2.0 collective-permute-start.29
  168.7 2.5 collective-permute-start.28
  174.4 13.0 %collective-permute-done.29 = bf16[96,3584]{1,0:T(8,128)(2,1)S(1)} collective-permute-done((bf16[96,3584]{1,0:T(8,128)(2,1)S(1)}, bf16[96,3584]{1,0:T(8,128)(2,1)S(1)}, u32[]{:S(2)}, u32[]{:S(2)}) %collective-permute-start.29) | collective-permute-done | bytes 688160 | tf_op jit(solution)/shard_map/shares_onward_5/ppermute | solution.py:224
  188.1 11.7 %collective-permute-done.27 = bf16[96,3584]{1,0:T(8,128)(2,1)S(1)} collective-permute-done((bf16[96,3584]{1,0:T(8,128)(2,1)S(1)}, bf16[96,3584]{1,0:T(8,128)(2,1)S(1)}, u32[]{:S(2)}, u32[]{:S(2)}) %collective-permute-start.27) | collective-permute-done | bytes 688160 | tf_op jit(solution)/shard_map/deliver_5_2/ppermute | solution.py:268
  201.4 2.0 collective-permute-start.24
  203.5 1.6 collective-permute-start.30
  205.9 1.2 collective-permute-start.32
  207.1 2.4 collective-permute-start.33
  209.5 5.1 %merge.3 = (bf16[512,7168]{1,0:T(8,128)(2,1)}, bf16[256,7168]{1,0:T(8,128)(2,1)}) custom-call(s32[5]{0:T(128)S(1)} %stack.23.scalars, bf16[384,3584]{1,0:T(8,128)(2,1)S(1)} %select_dynamic-update-slice_fusion.own, bf16[384,3584]{1,0:T(8,128)(2,1)S(1)} %collective-permute-done.34.far, bf16[512,7168]{1,0:T(8,128)(2,1)} %a_gu.7, bf16[256,7168]{1,0:T(8,128)(2,1)} %a_dn.7), custom_call_target="tpu_custom_call" | custom-call | tf_op jit(solution)/shard_map/merge/pallas_call | solution.py:115
  214.6 5.0 %merge.4 = (bf16[512,7168]{1,0:T(8,128)(2,1)}, bf16[256,7168]{1,0:T(8,128)(2,1)}) custom-call(s32[5]{0:T(128)S(1)} %stack.23.scalars, bf16[384,3584]{1,0:T(8,128)(2,1)S(1)} %select_dynamic-update-slice_fusion.own, bf16[384,3584]{1,0:T(8,128)(2,1)S(1)} %collective-permute-done.34.far, ...), custom_call_target="tpu_custom_call", output_to_operand_aliasing={{0}: (5, {}), {1}: (6, {})} | custom-call | tf_op jit(solution)/shard_map/merge/pallas_call | solution.py:115
  219.7 2.5 collective-permute-done.31
  223.2 1.4 collective-permute-start.36
  224.7 1.6 collective-permute-start.37
  226.2 5.0 %merge.5 = (bf16[512,7168]{1,0:T(8,128)(2,1)}, bf16[256,7168]{1,0:T(8,128)(2,1)}) custom-call(s32[5]{0:T(128)S(1)} %stack.23.scalars, bf16[192,3584]{1,0:T(8,128)(2,1)S(1)} %pad_maximum_fusion.own, bf16[192,3584]{1,0:T(8,128)(2,1)S(1)} %collective-permute-done.38.far, bf16[512,7168]{1,0:T(8,128)(2,1)} %a_gu.7, ...), custom_call_target="tpu_custom_call", output_to_operand_aliasing={{0}: (5, {}), {1}: (6, {})} | custom-call | tf_op jit(solution)/shard_map/merge/pallas_call | solution.py:115
  231.3 2.3 collective-permute-done.35
  233.8 7.0 %collective-permute-done.37 = bf16[48,3584]{1,0:T(8,128)(2,1)S(1)} collective-permute-done((bf16[48,3584]{1,0:T(8,128)(2,1)S(1)}, bf16[48,3584]{1,0:T(8,128)(2,1)S(1)}, u32[]{:S(2)}, u32[]{:S(2)}) %collective-permute-start.37) | collective-permute-done | bytes 344096 | tf_op jit(solution)/shard_map/deliver_7_3/ppermute | solution.py:268
  241.1 3.1 %collective-permute-done.39.far = bf16[192,3584]{1,0:T(8,128)(2,1)S(1)} collective-permute-done((bf16[192,3584]{1,0:T(8,128)(2,1)S(1)}, bf16[192,3584]{1,0:T(8,128)(2,1)S(1)}, u32[]{:S(2)}, u32[]{:S(2)}) %collective-permute-start.39) | collective-permute-done | bytes 1376288 | tf_op jit(solution)/shard_map/deliver_twin_8/ppermute | solution.py:278
  244.3 18.9 %forward.1 = (bf16[512,7168]{1,0:T(8,128)(2,1)}, bf16[256,7168]{1,0:T(8,128)(2,1)}, bf16[4,512,128]{2,1,0:T(8,128)(2,1)S(1)}) custom-call(s32[5]{0:T(128)S(1)} %stack.23.scalars, bf16[1024,256]{1,0:T(8,128)(2,1)S(1)} %copy-done.2, bf16[192,3584]{1,0:T(8,128)(2,1)S(1)} %pad_maximum_fusion.1.own, ...), custom_call_target="tpu_custom_call", output_to_operand_aliasing={{0}: (6, {}), {1}: (7, {})} | custom-call | tf_op jit(solution)/shard_map/forward/pallas_call | solution.py:171
  263.2 1.6 collective-permute-start.40
  265.6 1.2 collective-permute-start.42
  266.8 2.4 collective-permute-done.40
  269.2 3.7 %collective-permute-done.41 = bf16[512,128]{1,0:T(8,128)(2,1)S(1)} collective-permute-done((bf16[512,128]{1,0:T(8,128)(2,1)S(1)}, bf16[512,128]{1,0:T(8,128)(2,1)S(1)}, u32[]{:S(2)}, u32[]{:S(2)}) %collective-permute-start.41) | collective-permute-done | bytes 131104 | tf_op jit(solution)/shard_map/check_reduce_2/ppermute | solution.py:305
  (101 shorter events, 21.2 us)
Async XLA Ops:
  0.6 1.3 copy-start.6
  2.0 3.3 %collective-permute-start = (bf16[96,7168]{1,0:T(8,128)(2,1)S(1)}, bf16[96,7168]{1,0:T(8,128)(2,1)S(1)}, u32[]{:S(2)}, u32[]{:S(2)}) collective-permute-start(bf16[96,7168]{1,0:T(8,128)(2,1)S(1)} %constant_dynamic-update-slice_fusion.mine), channel_id=1, source_target_pairs={{0,1},{1,0},{2,3},{3,2},{4,5},{5,4},{6,7},{7,6},{8,9},{9,8},{10,11... | collective-permute-start | bytes 4128776 | tf_op jit(solution)/shard_map/rows_twin_0/ppermute | solution.py:243
  2.5 34.5 %collective-permute-start.1 = (bf16[96,7168]{1,0:T(8,128)(2,1)S(1)}, bf16[96,7168]{1,0:T(8,128)(2,1)}, u32[]{:S(2)}, u32[]{:S(2)}) collective-permute-start(bf16[96,7168]{1,0:T(8,128)(2,1)S(1)} %constant_dynamic-update-slice_fusion.mine), channel_id=1, source_target_pairs={{0,2},{1,3},{2,6},{3,7},{4,0},{5,1},{6,4},{7,5},{8,10},{9,11},{10,... | collective-permute-start | bytes 4128776 | tf_op jit(solution)/shard_map/rows_ring_0/ppermute | solution.py:241
  6.3 1.3 copy-start.1
  37.0 4.4 %collective-permute-start.2 = (bf16[96,7168]{1,0:T(8,128)(2,1)}, bf16[96,7168]{1,0:T(8,128)(2,1)}, u32[]{:S(2)}, u32[]{:S(2)}) collective-permute-start(bf16[96,7168]{1,0:T(8,128)(2,1)} %collective-permute-done.1.mine), channel_id=1, source_target_pairs={{0,1},{1,0},{2,3},{3,2},{4,5},{5,4},{6,7},{7,6},{8,9},{9,8},{10,11... | collective-permute-start | bytes 4128776 | tf_op jit(solution)/shard_map/rows_twin_1/ppermute | solution.py:243
  37.0 33.7 %collective-permute-start.3 = (bf16[96,7168]{1,0:T(8,128)(2,1)}, bf16[96,7168]{1,0:T(8,128)(2,1)S(1)}, u32[]{:S(2)}, u32[]{:S(2)}) collective-permute-start(bf16[96,7168]{1,0:T(8,128)(2,1)} %collective-permute-done.1.mine), channel_id=1, source_target_pairs={{0,2},{1,3},{2,6},{3,7},{4,0},{5,1},{6,4},{7,5},{8,10},{9,11},{10,... | collective-permute-start | bytes 4128776 | tf_op jit(solution)/shard_map/rows_ring_1/ppermute | solution.py:241
  37.9 24.3 %collective-permute-start.4 = (bf16[48,3584]{1,0:T(8,128)(2,1)S(1)}, bf16[48,3584]{1,0:T(8,128)(2,1)S(1)}, u32[]{:S(2)}, u32[]{:S(2)}) collective-permute-start(bf16[48,3584]{1,0:T(8,128)(2,1)S(1)} %get-tuple-element.157), channel_id=1, source_target_pairs={{0,8},{8,0},{16,24},{24,16},{1,9},{9,1},{17,25},{25,17},{2,10},{10... | collective-permute-start | bytes 1032200 | tf_op jit(solution)/shard_map/reduce_0_1/ppermute | solution.py:251
  39.4 22.8 %collective-permute-start.5 = (bf16[48,3584]{1,0:T(8,128)(2,1)S(1)}, bf16[48,3584]{1,0:T(8,128)(2,1)S(1)}, u32[]{:S(2)}, u32[]{:S(2)}) collective-permute-start(bf16[48,3584]{1,0:T(8,128)(2,1)S(1)} %get-tuple-element.156), channel_id=1, source_target_pairs={{0,16},{8,24},{16,0},{24,8},{1,17},{9,25},{17,1},{25,9},{2,18},{10... | collective-permute-start | bytes 1032200 | tf_op jit(solution)/shard_map/reduce_0_2/ppermute | solution.py:251
  41.0 21.3 %collective-permute-start.6 = (bf16[48,3584]{1,0:T(8,128)(2,1)S(1)}, bf16[48,3584]{1,0:T(8,128)(2,1)S(1)}, u32[]{:S(2)}, u32[]{:S(2)}) collective-permute-start(bf16[48,3584]{1,0:T(8,128)(2,1)S(1)} %get-tuple-element.155), channel_id=1, source_target_pairs={{0,24},{8,16},{16,8},{24,0},{1,25},{9,17},{17,9},{25,1},{2,26},{10... | collective-permute-start | bytes 1032200 | tf_op jit(solution)/shard_map/reduce_0_3/ppermute | solution.py:251
  70.8 4.8 %collective-permute-start.8 = (bf16[96,7168]{1,0:T(8,128)(2,1)S(1)}, bf16[96,7168]{1,0:T(8,128)(2,1)S(1)}, u32[]{:S(2)}, u32[]{:S(2)}) collective-permute-start(bf16[96,7168]{1,0:T(8,128)(2,1)S(1)} %collective-permute-done.3.mine), channel_id=1, source_target_pairs={{0,1},{1,0},{2,3},{3,2},{4,5},{5,4},{6,7},{7,6},{8,9},{9,8},{10,11... | collective-permute-start | bytes 4128776 | tf_op jit(solution)/shard_map/rows_twin_2/ppermute | solution.py:243
  70.8 42.0 %collective-permute-start.9 = (bf16[96,7168]{1,0:T(8,128)(2,1)S(1)}, bf16[96,7168]{1,0:T(8,128)(2,1)S(1)}, u32[]{:S(2)}, u32[]{:S(2)}) collective-permute-start(bf16[96,7168]{1,0:T(8,128)(2,1)S(1)} %collective-permute-done.3.mine), channel_id=1, source_target_pairs={{0,2},{1,3},{2,6},{3,7},{4,0},{5,1},{6,4},{7,5},{8,10},{9,11},{10,... | collective-permute-start | bytes 4128776 | tf_op jit(solution)/shard_map/rows_ring_2/ppermute | solution.py:241
  71.8 25.7 %collective-permute-start.10 = (bf16[48,3584]{1,0:T(8,128)(2,1)S(1)}, bf16[48,3584]{1,0:T(8,128)(2,1)S(1)}, u32[]{:S(2)}, u32[]{:S(2)}) collective-permute-start(bf16[48,3584]{1,0:T(8,128)(2,1)S(1)} %get-tuple-element.153), channel_id=1, source_target_pairs={{0,8},{8,0},{16,24},{24,16},{1,9},{9,1},{17,25},{25,17},{2,10},{10... | collective-permute-start | bytes 1032200 | tf_op jit(solution)/shard_map/reduce_1_1/ppermute | solution.py:251
  73.4 25.5 %collective-permute-start.11 = (bf16[48,3584]{1,0:T(8,128)(2,1)S(1)}, bf16[48,3584]{1,0:T(8,128)(2,1)S(1)}, u32[]{:S(2)}, u32[]{:S(2)}) collective-permute-start(bf16[48,3584]{1,0:T(8,128)(2,1)S(1)} %get-tuple-element.152), channel_id=1, source_target_pairs={{0,16},{8,24},{16,0},{24,8},{1,17},{9,25},{17,1},{25,9},{2,18},{10... | collective-permute-start | bytes 1032200 | tf_op jit(solution)/shard_map/reduce_1_2/ppermute | solution.py:251
  74.9 24.0 %collective-permute-start.12 = (bf16[48,3584]{1,0:T(8,128)(2,1)S(1)}, bf16[48,3584]{1,0:T(8,128)(2,1)S(1)}, u32[]{:S(2)}, u32[]{:S(2)}) collective-permute-start(bf16[48,3584]{1,0:T(8,128)(2,1)S(1)} %get-tuple-element.151), channel_id=1, source_target_pairs={{0,24},{8,16},{16,8},{24,0},{1,25},{9,17},{17,9},{25,1},{2,26},{10... | collective-permute-start | bytes 1032200 | tf_op jit(solution)/shard_map/reduce_1_3/ppermute | solution.py:251
  75.5 37.2 %collective-permute-start.7 = (bf16[48,3584]{1,0:T(8,128)(2,1)S(1)}, bf16[48,3584]{1,0:T(8,128)(2,1)S(1)}, u32[]{:S(2)}, u32[]{:S(2)}) collective-permute-start(bf16[48,3584]{1,0:T(8,128)(2,1)S(1)} %add_convert_fusion.3), channel_id=1, source_target_pairs={{2,0},{3,1},{6,2},{7,3},{0,4},{1,5},{4,6},{5,7},{10,8},{11,9},{14,... | collective-permute-start | bytes 1032200 | tf_op jit(solution)/shard_map/shares_onward_2/ppermute | solution.py:224
  97.5 41.1 %collective-permute-start.14 = (bf16[48,3584]{1,0:T(8,128)(2,1)S(1)}, bf16[48,3584]{1,0:T(8,128)(2,1)}, u32[]{:S(2)}, u32[]{:S(2)}) collective-permute-start(bf16[48,3584]{1,0:T(8,128)(2,1)S(1)} %add_convert_fusion.3), channel_id=1, source_target_pairs={{0,2},{1,3},{2,6},{3,7},{4,0},{5,1},{6,4},{7,5},{8,10},{9,11},{10,... | collective-permute-start | bytes 1032200 | tf_op jit(solution)/shard_map/shares_backward_3/ppermute | solution.py:224
  112.8 5.4 %collective-permute-start.16 = (bf16[96,7168]{1,0:T(8,128)(2,1)S(1)}, bf16[96,7168]{1,0:T(8,128)(2,1)S(1)}, u32[]{:S(2)}, u32[]{:S(2)}) collective-permute-start(bf16[96,7168]{1,0:T(8,128)(2,1)S(1)} %collective-permute-done.9.mine), channel_id=1, source_target_pairs={{0,1},{1,0},{2,3},{3,2},{4,5},{5,4},{6,7},{7,6},{8,9},{9,8},{10,11... | collective-permute-start | bytes 4128776 | tf_op jit(solution)/shard_map/rows_twin_3/ppermute | solution.py:243
  113.9 26.7 %collective-permute-start.15 = (bf16[96,3584]{1,0:T(8,128)(2,1)}, bf16[96,3584]{1,0:T(8,128)(2,1)}, u32[]{:S(2)}, u32[]{:S(2)}) collective-permute-start(bf16[96,3584]{1,0:T(8,128)(2,1)} %pad_maximum_fusion.2), channel_id=1, source_target_pairs={{2,0},{3,1},{6,2},{7,3},{0,4},{1,5},{4,6},{5,7},{10,8},{11,9},{14,... | collective-permute-start | bytes 2064392 | tf_op jit(solution)/shard_map/shares_onward_3/ppermute | solution.py:224
  115.2 25.3 %collective-permute-start.17 = (bf16[48,3584]{1,0:T(8,128)(2,1)}, bf16[48,3584]{1,0:T(8,128)(2,1)}, u32[]{:S(2)}, u32[]{:S(2)}) collective-permute-start(bf16[48,3584]{1,0:T(8,128)(2,1)} %get-tuple-element.149), channel_id=1, source_target_pairs={{0,8},{8,0},{16,24},{24,16},{1,9},{9,1},{17,25},{25,17},{2,10},{10... | collective-permute-start | bytes 1032200 | tf_op jit(solution)/shard_map/reduce_2_1/ppermute | solution.py:251
  116.7 23.9 %collective-permute-start.18 = (bf16[48,3584]{1,0:T(8,128)(2,1)}, bf16[48,3584]{1,0:T(8,128)(2,1)}, u32[]{:S(2)}, u32[]{:S(2)}) collective-permute-start(bf16[48,3584]{1,0:T(8,128)(2,1)} %get-tuple-element.148), channel_id=1, source_target_pairs={{0,16},{8,24},{16,0},{24,8},{1,17},{9,25},{17,1},{25,9},{2,18},{10... | collective-permute-start | bytes 1032200 | tf_op jit(solution)/shard_map/reduce_2_2/ppermute | solution.py:251
  118.2 22.3 %collective-permute-start.19 = (bf16[48,3584]{1,0:T(8,128)(2,1)}, bf16[48,3584]{1,0:T(8,128)(2,1)}, u32[]{:S(2)}, u32[]{:S(2)}) collective-permute-start(bf16[48,3584]{1,0:T(8,128)(2,1)} %get-tuple-element.147), channel_id=1, source_target_pairs={{0,24},{8,16},{16,8},{24,0},{1,25},{9,17},{17,9},{25,1},{2,26},{10... | collective-permute-start | bytes 1032200 | tf_op jit(solution)/shard_map/reduce_2_3/ppermute | solution.py:251
  118.7 22.9 %copy-start.5 = (bf16[48,3584]{1,0:T(8,128)(2,1)S(1)}, bf16[48,3584]{1,0:T(8,128)(2,1)}, u32[]{:S(2)}) copy-start(bf16[48,3584]{1,0:T(8,128)(2,1)} %get-tuple-element.78) | copy-start | bytes 1032196
  138.6 11.5 %collective-permute-start.13 = (bf16[48,3584]{1,0:T(8,128)(2,1)S(1)}, bf16[48,3584]{1,0:T(8,128)(2,1)S(1)}, u32[]{:S(2)}, u32[]{:S(2)}) collective-permute-start(bf16[48,3584]{1,0:T(8,128)(2,1)S(1)} %add_convert_fusion.2), channel_id=1, source_target_pairs={{0,2},{1,3},{2,6},{3,7},{4,0},{5,1},{6,4},{7,5},{8,10},{9,11},{10,... | collective-permute-start | bytes 1032200 | tf_op jit(solution)/shard_map/shares_backward_4/ppermute | solution.py:224
  143.0 22.3 %collective-permute-start.20 = (bf16[96,3584]{1,0:T(8,128)(2,1)S(1)}, bf16[96,3584]{1,0:T(8,128)(2,1)S(1)}, u32[]{:S(2)}, u32[]{:S(2)}) collective-permute-start(bf16[96,3584]{1,0:T(8,128)(2,1)S(1)} %pad_maximum_fusion.3), channel_id=1, source_target_pairs={{2,0},{3,1},{6,2},{7,3},{0,4},{1,5},{4,6},{5,7},{10,8},{11,9},{14,... | collective-permute-start | bytes 2064392 | tf_op jit(solution)/shard_map/shares_onward_4/ppermute | solution.py:224
  144.5 3.7 %copy-start.4 = (bf16[48,3584]{1,0:T(8,128)(2,1)S(1)}, bf16[48,3584]{1,0:T(8,128)(2,1)}, u32[]{:S(2)}) copy-start(bf16[48,3584]{1,0:T(8,128)(2,1)} %copy-done.3) | copy-start | bytes 1032196
  144.6 18.1 %collective-permute-start.21 = (bf16[48,3584]{1,0:T(8,128)(2,1)S(1)}, bf16[48,3584]{1,0:T(8,128)(2,1)S(1)}, u32[]{:S(2)}, u32[]{:S(2)}) collective-permute-start(bf16[48,3584]{1,0:T(8,128)(2,1)S(1)} %get-tuple-element.145), channel_id=1, source_target_pairs={{0,8},{8,0},{16,24},{24,16},{1,9},{9,1},{17,25},{25,17},{2,10},{10... | collective-permute-start | bytes 1032200 | tf_op jit(solution)/shard_map/reduce_3_1/ppermute | solution.py:251
  146.1 16.5 %collective-permute-start.22 = (bf16[48,3584]{1,0:T(8,128)(2,1)S(1)}, bf16[48,3584]{1,0:T(8,128)(2,1)S(1)}, u32[]{:S(2)}, u32[]{:S(2)}) collective-permute-start(bf16[48,3584]{1,0:T(8,128)(2,1)S(1)} %get-tuple-element.144), channel_id=1, source_target_pairs={{0,16},{8,24},{16,0},{24,8},{1,17},{9,25},{17,1},{25,9},{2,18},{10... | collective-permute-start | bytes 1032200 | tf_op jit(solution)/shard_map/reduce_3_2/ppermute | solution.py:251
  147.7 15.0 %collective-permute-start.23 = (bf16[48,3584]{1,0:T(8,128)(2,1)S(1)}, bf16[48,3584]{1,0:T(8,128)(2,1)S(1)}, u32[]{:S(2)}, u32[]{:S(2)}) collective-permute-start(bf16[48,3584]{1,0:T(8,128)(2,1)S(1)} %get-tuple-element.143), channel_id=1, source_target_pairs={{0,24},{8,16},{16,8},{24,0},{1,25},{9,17},{17,9},{25,1},{2,26},{10... | collective-permute-start | bytes 1032200 | tf_op jit(solution)/shard_map/reduce_3_3/ppermute | solution.py:251
  150.1 24.3 %collective-permute-start.25 = (bf16[48,3584]{1,0:T(8,128)(2,1)S(1)}, bf16[48,3584]{1,0:T(8,128)(2,1)S(1)}, u32[]{:S(2)}, u32[]{:S(2)}) collective-permute-start(bf16[48,3584]{1,0:T(8,128)(2,1)S(1)} %add_convert_fusion.1), channel_id=1, source_target_pairs={{0,2},{1,3},{2,6},{3,7},{4,0},{5,1},{6,4},{7,5},{8,10},{9,11},{10,... | collective-permute-start | bytes 1032200 | tf_op jit(solution)/shard_map/shares_backward_5/ppermute | solution.py:224
  166.7 20.7 %collective-permute-start.29 = (bf16[96,3584]{1,0:T(8,128)(2,1)S(1)}, bf16[96,3584]{1,0:T(8,128)(2,1)S(1)}, u32[]{:S(2)}, u32[]{:S(2)}) collective-permute-start(bf16[96,3584]{1,0:T(8,128)(2,1)S(1)} %pad_maximum_fusion.8), channel_id=1, source_target_pairs={{2,0},{3,1},{6,2},{7,3},{0,4},{1,5},{4,6},{5,7},{10,8},{11,9},{14,... | collective-permute-start | bytes 2064392 | tf_op jit(solution)/shard_map/shares_onward_5/ppermute | solution.py:224
  168.7 19.4 %collective-permute-start.28 = (bf16[96,3584]{1,0:T(8,128)(2,1)S(1)}, bf16[96,3584]{1,0:T(8,128)(2,1)S(1)}, u32[]{:S(2)}, u32[]{:S(2)}) collective-permute-start(bf16[96,3584]{1,0:T(8,128)(2,1)S(1)} %pad_maximum_fusion.7), channel_id=1, source_target_pairs={{0,24},{8,16},{16,8},{24,0},{1,25},{9,17},{17,9},{25,1},{2,26},{10... | collective-permute-start | bytes 2064392 | tf_op jit(solution)/shard_map/deliver_5_3/ppermute | solution.py:268
  171.3 28.5 %collective-permute-start.27 = (bf16[96,3584]{1,0:T(8,128)(2,1)S(1)}, bf16[96,3584]{1,0:T(8,128)(2,1)S(1)}, u32[]{:S(2)}, u32[]{:S(2)}) collective-permute-start(bf16[96,3584]{1,0:T(8,128)(2,1)S(1)} %pad_maximum_fusion.6), channel_id=1, source_target_pairs={{0,16},{8,24},{16,0},{24,8},{1,17},{9,25},{17,1},{25,9},{2,18},{10... | collective-permute-start | bytes 2064392 | tf_op jit(solution)/shard_map/deliver_5_2/ppermute | solution.py:268
  171.9 28.0 %collective-permute-start.26 = (bf16[96,3584]{1,0:T(8,128)(2,1)S(1)}, bf16[96,3584]{1,0:T(8,128)(2,1)S(1)}, u32[]{:S(2)}, u32[]{:S(2)}) collective-permute-start(bf16[96,3584]{1,0:T(8,128)(2,1)S(1)} %pad_maximum_fusion.5), channel_id=1, source_target_pairs={{0,8},{8,0},{16,24},{24,16},{1,9},{9,1},{17,25},{25,17},{2,10},{10... | collective-permute-start | bytes 2064392 | tf_op jit(solution)/shard_map/deliver_5_1/ppermute | solution.py:268
  201.3 5.7 %collective-permute-start.34 = (bf16[384,3584]{1,0:T(8,128)(2,1)S(1)}, bf16[384,3584]{1,0:T(8,128)(2,1)S(1)}, u32[]{:S(2)}, u32[]{:S(2)}) collective-permute-start(bf16[384,3584]{1,0:T(8,128)(2,1)S(1)} %select_dynamic-update-slice_fusion.own), channel_id=1, source_target_pairs={{0,1},{1,0},{2,3},{3,2},{4,5},{5,4},{6,7},{7,6},{8,9},{9,8},{10,11... | collective-permute-start | bytes 8257544 | tf_op jit(solution)/shard_map/deliver_twin_6/ppermute | solution.py:278
  201.4 18.2 %collective-permute-start.24 = (bf16[48,3584]{1,0:T(8,128)(2,1)S(1)}, bf16[48,3584]{1,0:T(8,128)(2,1)S(1)}, u32[]{:S(2)}, u32[]{:S(2)}) collective-permute-start(bf16[48,3584]{1,0:T(8,128)(2,1)S(1)} %add_convert_fusion), channel_id=1, source_target_pairs={{0,2},{1,3},{2,6},{3,7},{4,0},{5,1},{6,4},{7,5},{8,10},{9,11},{10,... | collective-permute-start | bytes 1032200 | tf_op jit(solution)/shard_map/shares_backward_6/ppermute | solution.py:224
  203.5 16.1 %collective-permute-start.30 = (bf16[48,3584]{1,0:T(8,128)(2,1)S(1)}, bf16[48,3584]{1,0:T(8,128)(2,1)S(1)}, u32[]{:S(2)}, u32[]{:S(2)}) collective-permute-start(bf16[48,3584]{1,0:T(8,128)(2,1)S(1)} %get-tuple-element.123), channel_id=1, source_target_pairs={{0,8},{8,0},{16,24},{24,16},{1,9},{9,1},{17,25},{25,17},{2,10},{10... | collective-permute-start | bytes 1032200 | tf_op jit(solution)/shard_map/deliver_6_1/ppermute | solution.py:268
  205.1 17.0 %collective-permute-start.31 = (bf16[48,3584]{1,0:T(8,128)(2,1)S(1)}, bf16[48,3584]{1,0:T(8,128)(2,1)S(1)}, u32[]{:S(2)}, u32[]{:S(2)}) collective-permute-start(bf16[48,3584]{1,0:T(8,128)(2,1)S(1)} %get-tuple-element.122), channel_id=1, source_target_pairs={{0,16},{8,24},{16,0},{24,8},{1,17},{9,25},{17,1},{25,9},{2,18},{10... | collective-permute-start | bytes 1032200 | tf_op jit(solution)/shard_map/deliver_6_2/ppermute | solution.py:268
  205.9 16.2 %collective-permute-start.32 = (bf16[48,3584]{1,0:T(8,128)(2,1)S(1)}, bf16[48,3584]{1,0:T(8,128)(2,1)S(1)}, u32[]{:S(2)}, u32[]{:S(2)}) collective-permute-start(bf16[48,3584]{1,0:T(8,128)(2,1)S(1)} %get-tuple-element.121), channel_id=1, source_target_pairs={{0,24},{8,16},{16,8},{24,0},{1,25},{9,17},{17,9},{25,1},{2,26},{10... | collective-permute-start | bytes 1032200 | tf_op jit(solution)/shard_map/deliver_6_3/ppermute | solution.py:268
  207.1 15.1 %collective-permute-start.33 = (bf16[48,3584]{1,0:T(8,128)(2,1)S(1)}, bf16[48,3584]{1,0:T(8,128)(2,1)S(1)}, u32[]{:S(2)}, u32[]{:S(2)}) collective-permute-start(bf16[48,3584]{1,0:T(8,128)(2,1)S(1)} %get-tuple-element.159), channel_id=1, source_target_pairs={{2,0},{3,1},{6,2},{7,3},{0,4},{1,5},{4,6},{5,7},{10,8},{11,9},{14,... | collective-permute-start | bytes 1032200 | tf_op jit(solution)/shard_map/shares_onward_6/ppermute | solution.py:224
  222.4 3.8 %collective-permute-start.38 = (bf16[192,3584]{1,0:T(8,128)(2,1)S(1)}, bf16[192,3584]{1,0:T(8,128)(2,1)S(1)}, u32[]{:S(2)}, u32[]{:S(2)}) collective-permute-start(bf16[192,3584]{1,0:T(8,128)(2,1)S(1)} %pad_maximum_fusion.own), channel_id=1, source_target_pairs={{0,1},{1,0},{2,3},{3,2},{4,5},{5,4},{6,7},{7,6},{8,9},{9,8},{10,11... | collective-permute-start | bytes 4128776 | tf_op jit(solution)/shard_map/deliver_twin_7/ppermute | solution.py:278
  222.7 10.9 %collective-permute-start.35 = (bf16[48,3584]{1,0:T(8,128)(2,1)S(1)}, bf16[48,3584]{1,0:T(8,128)(2,1)S(1)}, u32[]{:S(2)}, u32[]{:S(2)}) collective-permute-start(bf16[48,3584]{1,0:T(8,128)(2,1)S(1)} %get-tuple-element.129), channel_id=1, source_target_pairs={{0,8},{8,0},{16,24},{24,16},{1,9},{9,1},{17,25},{25,17},{2,10},{10... | collective-permute-start | bytes 1032200 | tf_op jit(solution)/shard_map/deliver_7_1/ppermute | solution.py:268
  223.2 10.6 %collective-permute-start.36 = (bf16[48,3584]{1,0:T(8,128)(2,1)S(1)}, bf16[48,3584]{1,0:T(8,128)(2,1)S(1)}, u32[]{:S(2)}, u32[]{:S(2)}) collective-permute-start(bf16[48,3584]{1,0:T(8,128)(2,1)S(1)} %get-tuple-element.128), channel_id=1, source_target_pairs={{0,16},{8,24},{16,0},{24,8},{1,17},{9,25},{17,1},{25,9},{2,18},{10... | collective-permute-start | bytes 1032200 | tf_op jit(solution)/shard_map/deliver_7_2/ppermute | solution.py:268
  224.7 16.1 %collective-permute-start.37 = (bf16[48,3584]{1,0:T(8,128)(2,1)S(1)}, bf16[48,3584]{1,0:T(8,128)(2,1)S(1)}, u32[]{:S(2)}, u32[]{:S(2)}) collective-permute-start(bf16[48,3584]{1,0:T(8,128)(2,1)S(1)} %get-tuple-element.127), channel_id=1, source_target_pairs={{0,24},{8,16},{16,8},{24,0},{1,25},{9,17},{17,9},{25,1},{2,26},{10... | collective-permute-start | bytes 1032200 | tf_op jit(solution)/shard_map/deliver_7_3/ppermute | solution.py:268
  241.0 3.3 %copy-start.2 = (bf16[1024,256]{1,0:T(8,128)(2,1)S(1)}, bf16[1024,256]{1,0:T(8,128)(2,1)}, u32[]{:S(2)}) copy-start(bf16[1024,256]{1,0:T(8,128)(2,1)} %tokens.1) | copy-start | bytes 1572868
  241.1 3.2 %collective-permute-start.39 = (bf16[192,3584]{1,0:T(8,128)(2,1)S(1)}, bf16[192,3584]{1,0:T(8,128)(2,1)S(1)}, u32[]{:S(2)}, u32[]{:S(2)}) collective-permute-start(bf16[192,3584]{1,0:T(8,128)(2,1)S(1)} %pad_maximum_fusion.1.own), channel_id=1, source_target_pairs={{0,1},{1,0},{2,3},{3,2},{4,5},{5,4},{6,7},{7,6},{8,9},{9,8},{10,11... | collective-permute-start | bytes 4128776 | tf_op jit(solution)/shard_map/deliver_twin_8/ppermute | solution.py:278
  263.2 5.9 %collective-permute-start.40 = (bf16[512,128]{1,0:T(8,128)(2,1)S(1)}, bf16[512,128]{1,0:T(8,128)(2,1)S(1)}, u32[]{:S(2)}, u32[]{:S(2)}) collective-permute-start(bf16[512,128]{1,0:T(8,128)(2,1)S(1)} %get-tuple-element.161), channel_id=1, source_target_pairs={{0,8},{8,0},{16,24},{24,16},{1,9},{9,1},{17,25},{25,17},{2,10},{10... | collective-permute-start | bytes 393224 | tf_op jit(solution)/shard_map/check_reduce_1/ppermute | solution.py:305
  264.8 8.1 %collective-permute-start.41 = (bf16[512,128]{1,0:T(8,128)(2,1)S(1)}, bf16[512,128]{1,0:T(8,128)(2,1)S(1)}, u32[]{:S(2)}, u32[]{:S(2)}) collective-permute-start(bf16[512,128]{1,0:T(8,128)(2,1)S(1)} %get-tuple-element.163), channel_id=1, source_target_pairs={{0,16},{8,24},{16,0},{24,8},{1,17},{9,25},{17,1},{25,9},{2,18},{10... | collective-permute-start | bytes 393224 | tf_op jit(solution)/shard_map/check_reduce_2/ppermute | solution.py:305
  265.6 7.3 %collective-permute-start.42 = (bf16[512,128]{1,0:T(8,128)(2,1)S(1)}, bf16[512,128]{1,0:T(8,128)(2,1)S(1)}, u32[]{:S(2)}, u32[]{:S(2)}) collective-permute-start(bf16[512,128]{1,0:T(8,128)(2,1)S(1)} %get-tuple-element.162), channel_id=1, source_target_pairs={{0,24},{8,16},{16,8},{24,0},{1,25},{9,17},{17,9},{25,1},{2,26},{10... | collective-permute-start | bytes 393224 | tf_op jit(solution)/shard_map/check_reduce_3/ppermute | solution.py:305
  (2 other events, 2.2 us)

commit v3 on v2

--- a/solution.py
+++ b/solution.py
@@ -124,32 +124,79 @@
     )(scalars, own, far, a_gu, a_dn, *sofar)
 
 
-def forward_kernel(steps, groups, t, scalars, tokens, own, far, a_gu, a_dn, gu, dn, gu_out, dn_out, check_out, gu_all, dn_all, total):
+def ready_kernel(scalars, tokens, rows, out):
+    out[...] = jnp.dot(tokens[...], rows[...], preferred_element_type=F32).astype(BF16)
+
+
+def gate_is_ready(scalars, t, groups):
+    return scalars[1 + t] >= groups // 2
+
+
+def ready_half(scalars, tokens, t, groups, gu):
+    count, features = tokens.shape
+    block = block_of(gu.shape[1], 2048)
+    return pl.pallas_call(
+        ready_kernel,
+        grid_spec=pltpu.PrefetchScalarGridSpec(
+            num_scalar_prefetch=1,
+            grid=(gu.shape[1] // block,),
+            in_specs=[
+                pl.BlockSpec(tokens.shape, lambda i, s: (0, 0)),
+                pl.BlockSpec((features, block), lambda i, s: (jnp.where(gate_is_ready(s, t, groups), 0, 1), i)),
+            ],
+            out_specs=pl.BlockSpec((count, block), lambda i, s: (0, i)),
+        ),
+        out_shape=jax.ShapeDtypeStruct((count, gu.shape[1]), BF16),
+        compiler_params=pltpu.CompilerParams(vmem_limit_bytes=VMEM_BYTES),
+        name="ready",
+    )(scalars, tokens, gu)
+
+
+def forward_kernel(steps, groups, t, scalars, tokens, own, far, a_gu, a_dn, ready, gu, dn, gu_out, dn_out, check_out, total, hidden):
     step = pl.program_id(0)
     features = tokens.shape[1]
     scale = features ** (-0.5)
     merge_kernel(steps, scalars, own, far, a_gu, a_dn, gu_out, dn_out)
-    for whole, before, part in ((gu_all, gu, gu_out), (dn_all, dn, dn_out)):
-        whole[...] = before[...]
-        rows = part.shape[0]
-        whole[pl.ds(pl.multiple_of(scalars[1 + t] * rows, rows), rows)] = part[...]
+    place = scalars[1 + t]
+    gate_ready = gate_is_ready(scalars, t, groups)
     block = gu.shape[1]
     chunk = block_of(block, 256)
-    part = 0.0
-    for start in range(0, block, chunk):
-        columns = slice(start, start + chunk)
-        gate = jnp.dot(tokens[...], gu_all[:features, columns], preferred_element_type=F32) * (0.5 * scale)
-        up = jnp.dot(tokens[...], gu_all[features:, columns], preferred_element_type=F32) * scale
-        hidden = (gate * (1.0 + jnp.tanh(gate)) * up).astype(BF16)
-        part += lax.dot_general(hidden, dn_all[:, columns], (((1,), (1,)), ((), ())), preferred_element_type=F32)
+
+    def with_last(others, part, place, columns):
+        rows = part.shape[0]
+        pieces = [others[i * rows : (i + 1) * rows, columns] for i in range(others.shape[0] // rows)]
+        return jnp.concatenate([jnp.where(place == i, part[:, columns], v) for i, v in enumerate(pieces)], axis=0)
+
+    def run(gate_ready):
+        part = 0.0
+        for start in range(0, block, chunk):
+            columns = slice(start, start + chunk)
+            rows = with_last(gu, gu_out, place - groups // 2 if gate_ready else place, columns)
+            found = jnp.dot(tokens[...], rows, preferred_element_type=F32)
+            known = ready[:, columns].astype(F32)
+            gate, up = (known, found) if gate_ready else (found, known)
+            gate = gate * (0.5 * scale)
+            value = (gate * (1.0 + jnp.tanh(gate)) * (up * scale)).astype(BF16)
+            part += lax.dot_general(
+                value, with_last(dn, dn_out, place, columns), (((1,), (1,)), ((), ())), preferred_element_type=F32
+            )
+        hidden[...] = part
+
+    @pl.when(gate_ready)
+    def _():
+        run(True)
+
+    @pl.when(jnp.logical_not(gate_ready))
+    def _():
+        run(False)
 
     @pl.when(step == 0)
     def _():
-        total[...] = part
+        total[...] = hidden[...]
 
     @pl.when(step > 0)
     def _():
-        total[...] += part
+        total[...] += hidden[...]
 
     @pl.when(step == 2 * steps - 1)
     def _():
@@ -161,35 +208,39 @@
             check_out[j] = jnp.concatenate(packed, axis=1).astype(BF16)
 
 
-def forward(scalars, tokens, t, groups, own, far, a_gu, a_dn, sofar):
+def forward(scalars, tokens, t, groups, own, far, a_gu, a_dn, ready, sofar):
     width = own.shape[1]
     block = block_of(width, 2048)
     count, features = tokens.shape
     fold = max(1, 128 // (features // groups))
     check_shape = (groups, count // fold, fold * features // groups)
     steps, pieces, group, slab = column_specs(width, block, t, groups, 0, a_gu, a_dn)
+
+    def column(i, s):
+        return jnp.where(i < steps, s[0], 1 - s[0]) * steps + lax.rem(i, steps)
+
+    half = pl.BlockSpec(
+        (features, block), lambda i, s: (jnp.where(gate_is_ready(s, t, groups), 1, 0), column(i, s))
+    )
+    known = pl.BlockSpec((count, block), lambda i, s: (0, column(i, s)))
     return pl.pallas_call(
         functools.partial(forward_kernel, steps, groups, t),
         grid_spec=pltpu.PrefetchScalarGridSpec(
             num_scalar_prefetch=1,
             grid=(2 * steps,),
-            in_specs=[pl.BlockSpec(tokens.shape, lambda i, s: (0, 0))] + pieces + group + slab,
+            in_specs=[pl.BlockSpec(tokens.shape, lambda i, s: (0, 0))] + pieces + group + [known, half, slab[1]],
             out_specs=group + [pl.BlockSpec(check_shape, lambda i, s: (0, 0, 0))],
-            scratch_shapes=[
-                pltpu.VMEM((a_gu.shape[0], block), BF16),
-                pltpu.VMEM((a_dn.shape[0], block), BF16),
-                pltpu.VMEM((count, features), F32),
-            ],
+            scratch_shapes=[pltpu.VMEM((count, features), F32), pltpu.VMEM((count, features), F32)],
         ),
         out_shape=[
             jax.ShapeDtypeStruct(a_gu.shape, BF16),
             jax.ShapeDtypeStruct(a_dn.shape, BF16),
             jax.ShapeDtypeStruct(check_shape, BF16),
         ],
-        input_output_aliases={6: 0, 7: 1},
+        input_output_aliases={7: 0, 8: 1},
         compiler_params=pltpu.CompilerParams(vmem_limit_bytes=VMEM_BYTES),
         name="forward",
-    )(scalars, tokens, own, far, a_gu, a_dn, *sofar)
+    )(scalars, tokens, own, far, a_gu, a_dn, ready, *sofar)
 
 
 def on_device(b_gate_up, b_down, a_gate_up, a_down, transform, check_tokens):
@@ -232,7 +283,7 @@
 
     half = n // 2
     partial, sums, held, got = {}, {}, {}, {}
-    sofar = []
+    sofar, ready = [], None
     for step in range(n + half + 3):
         out = {}
         if step < n:
@@ -256,7 +307,10 @@
             hop = step - 2 - t
             if 0 <= hop < half:
                 onward.append((t, hop, hop + 1))
-                if hop:
+                if t == n - 1:
+                    if hop + 1 < half:
+                        backward.append((t, -hop % n, n - hop - 1))
+                elif hop:
                     backward.append((t, (1 - hop) % n, n - hop))
         out["onward"] = along_ring(back, f"shares_onward_{step}", held, onward)
         out["backward"] = along_ring(ring, f"shares_backward_{step}", held, backward)
@@ -279,7 +333,10 @@
             for i, t in enumerate(delivered):
                 if t < n - 1:
                     sofar = merge_group(scalars, t, n, i, own, far, a_gate_up, a_down, sofar)
+            if n - 1 not in delivered:
+                ready = ready_half(scalars, check_tokens, n - 1, n, sofar[0]) if n - 2 in delivered else None
         out["sofar"] = sofar
+        out["ready"] = ready
 
         leaves, tree = jax.tree.flatten(out)
         out = jax.tree.unflatten(tree, lax.optimization_barrier(leaves))
@@ -293,10 +350,10 @@
         if "got" in out:
             got[step] = out["got"]
             delivered = deliver
-        sofar = out["sofar"]
+        sofar, ready = out["sofar"], out["ready"]
 
     merged_gate_up, merged_down, parts = forward(
-        scalars, check_tokens, n - 1, n, own, far, a_gate_up, a_down, sofar
+        scalars, check_tokens, n - 1, n, own, far, a_gate_up, a_down, ready, sofar
     )
     total = lax.dynamic_index_in_dim(parts, q, keepdims=False).astype(F32)
     for d in range(1, n):

time: 275 us -> 273 us (level)
  starting transfers between devices: 59.5 us -> 44.4 us
  waiting for transfers between devices: 82.8 us -> 89.2 us
  Pallas kernels: 115 us -> 121 us
    ppermute x9 -> x8, starting transfers between devices: 25.9 us -> 10.7 us  [along_ring(): return lax.ppermute(cat([held[t][i] for t, i, _ in step]), 'col', perm)]
    pallas_call x0 -> x1, Pallas kernels: none -> 9.61 us  [ready_half(): pl.pallas_call(ready_kernel, grid_spec=pltpu.PrefetchScalarGridSpec(num_s...]
    ppermute x9, waiting for transfers between devices: 24.6 us -> 30.3 us  [on_device(): lax.ppermute(cat([for_row(held[t], q ^ d) for t in deliver]), 'row', peer...]
    pallas_call x1, Pallas kernels: 18.9 us -> 16 us  [forward(): pl.pallas_call(functools.partial(forward_kernel, steps, groups, t), grid_...]
    ppermute x9 -> x8, waiting for transfers between devices: 31 us -> 29.9 us  [along_ring(): return lax.ppermute(cat([held[t][i] for t, i, _ in step]), 'col', perm)]
  transfers between devices with their start and end apart: 43 -> 42, of which waited for: 17 -> 15; matrix products, arithmetic and copies ran while one was open for 3% -> 3% of each run, Pallas kernels for 35% -> 39%
where the time goes in v3:
time: 273 us; the launch traced here: 272 us
  Pallas kernels  121 us (44%)
  waiting for transfers between devices  89.2 us (33%)
  starting transfers between devices  44.4 us (16%)
  other arithmetic  8.92 us (3%)
  local copies, waits for them, and re-layouts  7.02 us (3%)
    pallas_call x4, Pallas kernels, project(): pl.pallas_call(project_kernel, grid_spec=pltpu.PrefetchScalarGridSpec(num...  80.6 us
    ppermute x9, waiting for transfers between devices, on_device(): lax.ppermute(cat([for_row(held[t], q ^ d) for t in deliver]), 'row', peer...  30.3 us
    ppermute x8, waiting for transfers between devices, along_ring(): return lax.ppermute(cat([held[t][i] for t, i, _ in step]), 'col', perm)  29.9 us
    ppermute x3, waiting for transfers between devices, on_device(): out['rows'] = lax.ppermute(rows, 'col', ring)  18 us
    pallas_call x1, Pallas kernels, forward(): pl.pallas_call(functools.partial(forward_kernel, steps, groups, t), grid_...  16 us
    pallas_call x3, Pallas kernels, merge_group(): pl.pallas_call(functools.partial(merge_kernel, steps), grid_spec=pltpu.Pr...  15.2 us
    ppermute x12, starting transfers between devices, on_device(): out['sums'].append(lax.ppermute(part, 'row', peers(d)))  14.2 us
    ppermute x9, starting transfers between devices, on_device(): lax.ppermute(cat([for_row(held[t], q ^ d) for t in deliver]), 'row', peer...  10.9 us
  transfers between devices with their start and end apart: 42, of which 15 were waited for; matrix products, arithmetic and copies ran while one was open for 3% of the time, Pallas kernels for 39%

profile of v3, /device:TPU:0, one launch (start us, length us, event | category | flops | bytes accessed | tf_op | source)
XLA Modules:
  0.0 271.9 jit_solution(374559677565009812)
XLA Ops:
  0.6 1.3 constant_dynamic-update-slice_fusion.1
  2.5 2.6 collective-permute-start.1
  5.3 1.1 copy-done.1
  6.3 1.3 copy-done.2
  7.7 19.9 %project.4 = bf16[2,96,3584]{2,1,0:T(8,128)(2,1)S(1)} custom-call(s32[5]{0:T(128)S(1)} %stack.23.scalars, bf16[96,7168]{1,0:T(8,128)(2,1)S(1)} %constant_dynamic-update-slice_fusion.mine, bf16[96,7168]{1,0:T(8,128)(2,1)S(1)} %copy-done.2, bf16[7168,3584]{1,0:T(8,128)(2,1)} %panel.7), custom_call_target="tpu_custom_call" | custom-call | tf_op jit(solution)/shard_map/project/pallas_call | solution.py:53
  27.6 9.4 %collective-permute-done.1.mine = bf16[96,7168]{1,0:T(8,128)(2,1)} collective-permute-done((bf16[96,7168]{1,0:T(8,128)(2,1)S(1)}, bf16[96,7168]{1,0:T(8,128)(2,1)}, u32[]{:S(2)}, u32[]{:S(2)}) %collective-permute-start.1) | collective-permute-done | bytes 1376288 | tf_op jit(solution)/shard_map/rows_ring_0/ppermute | solution.py:292
  37.9 2.5 collective-permute-start.6
  41.4 20.7 %project.5 = bf16[2,96,3584]{2,1,0:T(8,128)(2,1)S(1)} custom-call(s32[5]{0:T(128)S(1)} %stack.23.scalars, bf16[96,7168]{1,0:T(8,128)(2,1)} %collective-permute-done.1.mine, bf16[96,7168]{1,0:T(8,128)(2,1)} %collective-permute-done.2.theirs, bf16[7168,3584]{1,0:T(8,128)(2,1)} %panel.7), custom_call_target="tpu_custom_call" | custom-call | tf_op jit(solution)/shard_map/project/pallas_call | solution.py:53
  62.2 8.5 %collective-permute-done.3.mine = bf16[96,7168]{1,0:T(8,128)(2,1)S(1)} collective-permute-done((bf16[96,7168]{1,0:T(8,128)(2,1)}, bf16[96,7168]{1,0:T(8,128)(2,1)S(1)}, u32[]{:S(2)}, u32[]{:S(2)}) %collective-permute-start.3) | collective-permute-done | bytes 1376288 | tf_op jit(solution)/shard_map/rows_ring_1/ppermute | solution.py:292
  70.8 0.9 collective-permute-start.10
  71.9 2.0 collective-permute-start.8
  74.0 2.6 collective-permute-start.13
  77.6 19.9 %project.6 = bf16[2,96,3584]{2,1,0:T(8,128)(2,1)S(1)} custom-call(s32[5]{0:T(128)S(1)} %stack.23.scalars, bf16[96,7168]{1,0:T(8,128)(2,1)S(1)} %collective-permute-done.3.mine, bf16[96,7168]{1,0:T(8,128)(2,1)S(1)} %collective-permute-done.9.theirs, bf16[7168,3584]{1,0:T(8,128)(2,1)} %panel.7), custom_call_target="tpu_custom_call" | custom-call | tf_op jit(solution)/shard_map/project/pallas_call | solution.py:53
  97.5 13.3 %collective-permute-done.8 = bf16[48,3584]{1,0:T(8,128)(2,1)S(1)} collective-permute-done((bf16[48,3584]{1,0:T(8,128)(2,1)S(1)}, bf16[48,3584]{1,0:T(8,128)(2,1)S(1)}, u32[]{:S(2)}, u32[]{:S(2)}) %collective-permute-start.8) | collective-permute-done | bytes 344096 | tf_op jit(solution)/shard_map/shares_onward_2/ppermute | solution.py:275
  110.8 1.6 collective-permute-start.7
  113.6 1.3 collective-permute-start.14
  114.9 1.1 dynamic-slice_bitcast_fusion.4
  116.0 2.5 collective-permute-start.18
  119.5 19.9 %project.7 = bf16[2,96,3584]{2,1,0:T(8,128)(2,1)S(1)} custom-call(s32[5]{0:T(128)S(1)} %stack.23.scalars, bf16[96,7168]{1,0:T(8,128)(2,1)S(1)} %collective-permute-done.10.mine, bf16[96,7168]{1,0:T(8,128)(2,1)S(1)} %collective-permute-done.15.theirs, bf16[7168,3584]{1,0:T(8,128)(2,1)} %panel.7), custom_call_target="tpu_custom_call" | custom-call | tf_op jit(solution)/shard_map/project/pallas_call | solution.py:53
  140.2 1.0 slice.48
  141.3 1.4 add_convert_fusion.1
  142.7 2.3 collective-permute-start.20
  145.1 2.6 collective-permute-start.23
  148.6 1.2 select_select_fusion.17
  149.9 14.7 %collective-permute-done.19 = bf16[48,3584]{1,0:T(8,128)(2,1)S(1)} collective-permute-done((bf16[48,3584]{1,0:T(8,128)(2,1)S(1)}, bf16[48,3584]{1,0:T(8,128)(2,1)S(1)}, u32[]{:S(2)}, u32[]{:S(2)}) %collective-permute-start.19) | collective-permute-done | bytes 344096 | tf_op jit(solution)/shard_map/shares_backward_4/ppermute | solution.py:275
  164.6 1.1 select_select_fusion.16
  165.8 1.6 collective-permute-start.25
  167.5 1.6 collective-permute-start.26
  170.6 1.3 collective-permute-start.24
  171.9 1.1 select_select_fusion.22
  173.1 11.1 %collective-permute-done.25 = bf16[96,3584]{1,0:T(8,128)(2,1)S(1)} collective-permute-done((bf16[96,3584]{1,0:T(8,128)(2,1)S(1)}, bf16[96,3584]{1,0:T(8,128)(2,1)S(1)}, u32[]{:S(2)}, u32[]{:S(2)}) %collective-permute-start.25) | collective-permute-done | bytes 688160 | tf_op jit(solution)/shard_map/deliver_5_1/ppermute | solution.py:322
  184.2 14.9 %collective-permute-done.26 = bf16[96,3584]{1,0:T(8,128)(2,1)S(1)} collective-permute-done((bf16[96,3584]{1,0:T(8,128)(2,1)S(1)}, bf16[96,3584]{1,0:T(8,128)(2,1)S(1)}, u32[]{:S(2)}, u32[]{:S(2)}) %collective-permute-start.26) | collective-permute-done | bytes 688160 | tf_op jit(solution)/shard_map/deliver_5_2/ppermute | solution.py:322
  199.1 1.9 collective-permute-done.24
  202.6 2.5 collective-permute-start.31
  207.6 5.0 %merge.3 = (bf16[512,7168]{1,0:T(8,128)(2,1)}, bf16[256,7168]{1,0:T(8,128)(2,1)}) custom-call(s32[5]{0:T(128)S(1)} %stack.23.scalars, bf16[384,3584]{1,0:T(8,128)(2,1)S(1)} %select_dynamic-update-slice_fusion.own, bf16[384,3584]{1,0:T(8,128)(2,1)S(1)} %collective-permute-done.33.far, bf16[512,7168]{1,0:T(8,128)(2,1)} %a_gu.7, bf16[256,7168]{1,0:T(8,128)(2,1)} %a_dn.7), custom_call_target="tpu_custom_call" | custom-call | tf_op jit(solution)/shard_map/merge/pallas_call | solution.py:115
  212.6 5.0 %merge.4 = (bf16[512,7168]{1,0:T(8,128)(2,1)}, bf16[256,7168]{1,0:T(8,128)(2,1)}) custom-call(s32[5]{0:T(128)S(1)} %stack.23.scalars, bf16[384,3584]{1,0:T(8,128)(2,1)S(1)} %select_dynamic-update-slice_fusion.own, bf16[384,3584]{1,0:T(8,128)(2,1)S(1)} %collective-permute-done.33.far, ...), custom_call_target="tpu_custom_call", output_to_operand_aliasing={{0}: (5, {}), {1}: (6, {})} | custom-call | tf_op jit(solution)/shard_map/merge/pallas_call | solution.py:115
  217.7 3.7 %collective-permute-done.30 = bf16[48,3584]{1,0:T(8,128)(2,1)S(1)} collective-permute-done((bf16[48,3584]{1,0:T(8,128)(2,1)S(1)}, bf16[48,3584]{1,0:T(8,128)(2,1)S(1)}, u32[]{:S(2)}, u32[]{:S(2)}) %collective-permute-start.30) | collective-permute-done | bytes 344096 | tf_op jit(solution)/shard_map/deliver_6_2/ppermute | solution.py:322
  222.0 1.7 collective-permute-start.36
  223.7 1.3 collective-permute-start.35
  225.7 5.1 %merge.5 = (bf16[512,7168]{1,0:T(8,128)(2,1)}, bf16[256,7168]{1,0:T(8,128)(2,1)}) custom-call(s32[5]{0:T(128)S(1)} %stack.23.scalars, bf16[192,3584]{1,0:T(8,128)(2,1)S(1)} %pad_maximum_fusion.own, bf16[192,3584]{1,0:T(8,128)(2,1)S(1)} %collective-permute-done.37.far, bf16[512,7168]{1,0:T(8,128)(2,1)} %a_gu.7, ...), custom_call_target="tpu_custom_call", output_to_operand_aliasing={{0}: (5, {}), {1}: (6, {})} | custom-call | tf_op jit(solution)/shard_map/merge/pallas_call | solution.py:115
  230.7 9.6 %ready.1 = bf16[1024,7168]{1,0:T(8,128)(2,1)} custom-call(s32[5]{0:T(128)S(1)} %stack.23.scalars, bf16[1024,256]{1,0:T(8,128)(2,1)S(1)} %copy-done, bf16[512,7168]{1,0:T(8,128)(2,1)} %get-tuple-element.118.rows.gu), custom_call_target="tpu_custom_call" | custom-call | tf_op jit(solution)/shard_map/ready/pallas_call | solution.py:138
  241.2 3.1 %collective-permute-done.38.far = bf16[192,3584]{1,0:T(8,128)(2,1)S(1)} collective-permute-done((bf16[192,3584]{1,0:T(8,128)(2,1)S(1)}, bf16[192,3584]{1,0:T(8,128)(2,1)S(1)}, u32[]{:S(2)}, u32[]{:S(2)}) %collective-permute-start.38) | collective-permute-done | bytes 1376288 | tf_op jit(solution)/shard_map/deliver_twin_8/ppermute | solution.py:332
  244.3 16.0 %forward.1 = (bf16[512,7168]{1,0:T(8,128)(2,1)}, bf16[256,7168]{1,0:T(8,128)(2,1)}, bf16[4,512,128]{2,1,0:T(8,128)(2,1)S(1)}) custom-call(s32[5]{0:T(128)S(1)} %stack.23.scalars, bf16[1024,256]{1,0:T(8,128)(2,1)S(1)} %copy-done, bf16[192,3584]{1,0:T(8,128)(2,1)S(1)} %pad_maximum_fusion.1.own, ...), custom_call_target="tpu_custom_call", output_to_operand_aliasing={{0}: (7, {}), {1}: (8, {})} | custom-call | tf_op jit(solution)/shard_map/forward/pallas_call | solution.py:226
  260.3 1.2 collective-permute-start.39
  261.5 1.8 collective-permute-start.41
  263.9 2.9 %collective-permute-done.39 = bf16[512,128]{1,0:T(8,128)(2,1)S(1)} collective-permute-done((bf16[512,128]{1,0:T(8,128)(2,1)S(1)}, bf16[512,128]{1,0:T(8,128)(2,1)S(1)}, u32[]{:S(2)}, u32[]{:S(2)}) %collective-permute-start.39) | collective-permute-done | bytes 131104 | tf_op jit(solution)/shard_map/check_reduce_1/ppermute | solution.py:362
  266.7 3.0 %collective-permute-done.41 = bf16[512,128]{1,0:T(8,128)(2,1)S(1)} collective-permute-done((bf16[512,128]{1,0:T(8,128)(2,1)S(1)}, bf16[512,128]{1,0:T(8,128)(2,1)S(1)}, u32[]{:S(2)}, u32[]{:S(2)}) %collective-permute-start.41) | collective-permute-done | bytes 131104 | tf_op jit(solution)/shard_map/check_reduce_3/ppermute | solution.py:362
  269.7 1.4 collective-permute-done.40
  (101 shorter events, 17.1 us)
Async XLA Ops:
  0.6 1.3 copy-start.6
  2.0 3.3 %collective-permute-start = (bf16[96,7168]{1,0:T(8,128)(2,1)S(1)}, bf16[96,7168]{1,0:T(8,128)(2,1)S(1)}, u32[]{:S(2)}, u32[]{:S(2)}) collective-permute-start(bf16[96,7168]{1,0:T(8,128)(2,1)S(1)} %constant_dynamic-update-slice_fusion.mine), channel_id=1, source_target_pairs={{0,1},{1,0},{2,3},{3,2},{4,5},{5,4},{6,7},{7,6},{8,9},{9,8},{10,11... | collective-permute-start | bytes 4128776 | tf_op jit(solution)/shard_map/rows_twin_0/ppermute | solution.py:294
  2.5 34.5 %collective-permute-start.1 = (bf16[96,7168]{1,0:T(8,128)(2,1)S(1)}, bf16[96,7168]{1,0:T(8,128)(2,1)}, u32[]{:S(2)}, u32[]{:S(2)}) collective-permute-start(bf16[96,7168]{1,0:T(8,128)(2,1)S(1)} %constant_dynamic-update-slice_fusion.mine), channel_id=1, source_target_pairs={{0,2},{1,3},{2,6},{3,7},{4,0},{5,1},{6,4},{7,5},{8,10},{9,11},{10,... | collective-permute-start | bytes 4128776 | tf_op jit(solution)/shard_map/rows_ring_0/ppermute | solution.py:292
  6.3 1.3 copy-start.2
  37.0 4.4 %collective-permute-start.2 = (bf16[96,7168]{1,0:T(8,128)(2,1)}, bf16[96,7168]{1,0:T(8,128)(2,1)}, u32[]{:S(2)}, u32[]{:S(2)}) collective-permute-start(bf16[96,7168]{1,0:T(8,128)(2,1)} %collective-permute-done.1.mine), channel_id=1, source_target_pairs={{0,1},{1,0},{2,3},{3,2},{4,5},{5,4},{6,7},{7,6},{8,9},{9,8},{10,11... | collective-permute-start | bytes 4128776 | tf_op jit(solution)/shard_map/rows_twin_1/ppermute | solution.py:294
  37.0 33.7 %collective-permute-start.3 = (bf16[96,7168]{1,0:T(8,128)(2,1)}, bf16[96,7168]{1,0:T(8,128)(2,1)S(1)}, u32[]{:S(2)}, u32[]{:S(2)}) collective-permute-start(bf16[96,7168]{1,0:T(8,128)(2,1)} %collective-permute-done.1.mine), channel_id=1, source_target_pairs={{0,2},{1,3},{2,6},{3,7},{4,0},{5,1},{6,4},{7,5},{8,10},{9,11},{10,... | collective-permute-start | bytes 4128776 | tf_op jit(solution)/shard_map/rows_ring_1/ppermute | solution.py:292
  37.9 24.3 %collective-permute-start.6 = (bf16[48,3584]{1,0:T(8,128)(2,1)S(1)}, bf16[48,3584]{1,0:T(8,128)(2,1)S(1)}, u32[]{:S(2)}, u32[]{:S(2)}) collective-permute-start(bf16[48,3584]{1,0:T(8,128)(2,1)S(1)} %get-tuple-element.156), channel_id=1, source_target_pairs={{0,24},{8,16},{16,8},{24,0},{1,25},{9,17},{17,9},{25,1},{2,26},{10... | collective-permute-start | bytes 1032200 | tf_op jit(solution)/shard_map/reduce_0_3/ppermute | solution.py:302
  40.4 21.8 %collective-permute-start.5 = (bf16[48,3584]{1,0:T(8,128)(2,1)S(1)}, bf16[48,3584]{1,0:T(8,128)(2,1)S(1)}, u32[]{:S(2)}, u32[]{:S(2)}) collective-permute-start(bf16[48,3584]{1,0:T(8,128)(2,1)S(1)} %get-tuple-element.157), channel_id=1, source_target_pairs={{0,16},{8,24},{16,0},{24,8},{1,17},{9,25},{17,1},{25,9},{2,18},{10... | collective-permute-start | bytes 1032200 | tf_op jit(solution)/shard_map/reduce_0_2/ppermute | solution.py:302
  40.9 21.3 %collective-permute-start.4 = (bf16[48,3584]{1,0:T(8,128)(2,1)S(1)}, bf16[48,3584]{1,0:T(8,128)(2,1)S(1)}, u32[]{:S(2)}, u32[]{:S(2)}) collective-permute-start(bf16[48,3584]{1,0:T(8,128)(2,1)S(1)} %get-tuple-element.158), channel_id=1, source_target_pairs={{0,8},{8,0},{16,24},{24,16},{1,9},{9,1},{17,25},{25,17},{2,10},{10... | collective-permute-start | bytes 1032200 | tf_op jit(solution)/shard_map/reduce_0_1/ppermute | solution.py:302
  70.8 41.7 %collective-permute-start.10 = (bf16[96,7168]{1,0:T(8,128)(2,1)S(1)}, bf16[96,7168]{1,0:T(8,128)(2,1)S(1)}, u32[]{:S(2)}, u32[]{:S(2)}) collective-permute-start(bf16[96,7168]{1,0:T(8,128)(2,1)S(1)} %collective-permute-done.3.mine), channel_id=1, source_target_pairs={{0,2},{1,3},{2,6},{3,7},{4,0},{5,1},{6,4},{7,5},{8,10},{9,11},{10,... | collective-permute-start | bytes 4128776 | tf_op jit(solution)/shard_map/rows_ring_2/ppermute | solution.py:292
  71.7 5.4 %collective-permute-start.9 = (bf16[96,7168]{1,0:T(8,128)(2,1)S(1)}, bf16[96,7168]{1,0:T(8,128)(2,1)S(1)}, u32[]{:S(2)}, u32[]{:S(2)}) collective-permute-start(bf16[96,7168]{1,0:T(8,128)(2,1)S(1)} %collective-permute-done.3.mine), channel_id=1, source_target_pairs={{0,1},{1,0},{2,3},{3,2},{4,5},{5,4},{6,7},{7,6},{8,9},{9,8},{10,11... | collective-permute-start | bytes 4128776 | tf_op jit(solution)/shard_map/rows_twin_2/ppermute | solution.py:294
  71.9 39.0 %collective-permute-start.8 = (bf16[48,3584]{1,0:T(8,128)(2,1)S(1)}, bf16[48,3584]{1,0:T(8,128)(2,1)S(1)}, u32[]{:S(2)}, u32[]{:S(2)}) collective-permute-start(bf16[48,3584]{1,0:T(8,128)(2,1)S(1)} %add_convert_fusion.3), channel_id=1, source_target_pairs={{2,0},{3,1},{6,2},{7,3},{0,4},{1,5},{4,6},{5,7},{10,8},{11,9},{14,... | collective-permute-start | bytes 1032200 | tf_op jit(solution)/shard_map/shares_onward_2/ppermute | solution.py:275
  74.0 38.4 %collective-permute-start.13 = (bf16[48,3584]{1,0:T(8,128)(2,1)S(1)}, bf16[48,3584]{1,0:T(8,128)(2,1)S(1)}, u32[]{:S(2)}, u32[]{:S(2)}) collective-permute-start(bf16[48,3584]{1,0:T(8,128)(2,1)S(1)} %get-tuple-element.152), channel_id=1, source_target_pairs={{0,24},{8,16},{16,8},{24,0},{1,25},{9,17},{17,9},{25,1},{2,26},{10... | collective-permute-start | bytes 1032200 | tf_op jit(solution)/shard_map/reduce_1_3/ppermute | solution.py:302
  76.6 35.8 %collective-permute-start.12 = (bf16[48,3584]{1,0:T(8,128)(2,1)S(1)}, bf16[48,3584]{1,0:T(8,128)(2,1)S(1)}, u32[]{:S(2)}, u32[]{:S(2)}) collective-permute-start(bf16[48,3584]{1,0:T(8,128)(2,1)S(1)} %get-tuple-element.153), channel_id=1, source_target_pairs={{0,16},{8,24},{16,0},{24,8},{1,17},{9,25},{17,1},{25,9},{2,18},{10... | collective-permute-start | bytes 1032200 | tf_op jit(solution)/shard_map/reduce_1_2/ppermute | solution.py:302
  77.1 35.3 %collective-permute-start.11 = (bf16[48,3584]{1,0:T(8,128)(2,1)S(1)}, bf16[48,3584]{1,0:T(8,128)(2,1)S(1)}, u32[]{:S(2)}, u32[]{:S(2)}) collective-permute-start(bf16[48,3584]{1,0:T(8,128)(2,1)S(1)} %get-tuple-element.154), channel_id=1, source_target_pairs={{0,8},{8,0},{16,24},{24,16},{1,9},{9,1},{17,25},{25,17},{2,10},{10... | collective-permute-start | bytes 1032200 | tf_op jit(solution)/shard_map/reduce_1_1/ppermute | solution.py:302
  110.8 2.8 %copy-start.3 = (bf16[48,3584]{1,0:T(8,128)(2,1)}, bf16[48,3584]{1,0:T(8,128)(2,1)S(1)}, u32[]{:S(2)}) copy-start(bf16[48,3584]{1,0:T(8,128)(2,1)S(1)} %collective-permute-done.8) | copy-start | bytes 1032196
  110.8 28.6 %collective-permute-start.7 = (bf16[48,3584]{1,0:T(8,128)(2,1)S(1)}, bf16[48,3584]{1,0:T(8,128)(2,1)}, u32[]{:S(2)}, u32[]{:S(2)}) collective-permute-start(bf16[48,3584]{1,0:T(8,128)(2,1)S(1)} %add_convert_fusion.3), channel_id=1, source_target_pairs={{0,2},{1,3},{2,6},{3,7},{4,0},{5,1},{6,4},{7,5},{8,10},{9,11},{10,... | collective-permute-start | bytes 1032200 | tf_op jit(solution)/shard_map/shares_backward_3/ppermute | solution.py:275
  112.4 6.6 %collective-permute-start.15 = (bf16[96,7168]{1,0:T(8,128)(2,1)S(1)}, bf16[96,7168]{1,0:T(8,128)(2,1)S(1)}, u32[]{:S(2)}, u32[]{:S(2)}) collective-permute-start(bf16[96,7168]{1,0:T(8,128)(2,1)S(1)} %collective-permute-done.10.mine), channel_id=1, source_target_pairs={{0,1},{1,0},{2,3},{3,2},{4,5},{5,4},{6,7},{7,6},{8,9},{9,8},{10,11... | collective-permute-start | bytes 4128776 | tf_op jit(solution)/shard_map/rows_twin_3/ppermute | solution.py:294
  113.6 26.6 %collective-permute-start.14 = (bf16[96,3584]{1,0:T(8,128)(2,1)}, bf16[96,3584]{1,0:T(8,128)(2,1)}, u32[]{:S(2)}, u32[]{:S(2)}) collective-permute-start(bf16[96,3584]{1,0:T(8,128)(2,1)} %pad_maximum_fusion.4), channel_id=1, source_target_pairs={{2,0},{3,1},{6,2},{7,3},{0,4},{1,5},{4,6},{5,7},{10,8},{11,9},{14,... | collective-permute-start | bytes 2064392 | tf_op jit(solution)/shard_map/shares_onward_3/ppermute | solution.py:275
  116.0 24.2 %collective-permute-start.18 = (bf16[48,3584]{1,0:T(8,128)(2,1)}, bf16[48,3584]{1,0:T(8,128)(2,1)}, u32[]{:S(2)}, u32[]{:S(2)}) collective-permute-start(bf16[48,3584]{1,0:T(8,128)(2,1)} %get-tuple-element.148), channel_id=1, source_target_pairs={{0,24},{8,16},{16,8},{24,0},{1,25},{9,17},{17,9},{25,1},{2,26},{10... | collective-permute-start | bytes 1032200 | tf_op jit(solution)/shard_map/reduce_2_3/ppermute | solution.py:302
  118.5 21.7 %collective-permute-start.17 = (bf16[48,3584]{1,0:T(8,128)(2,1)}, bf16[48,3584]{1,0:T(8,128)(2,1)}, u32[]{:S(2)}, u32[]{:S(2)}) collective-permute-start(bf16[48,3584]{1,0:T(8,128)(2,1)} %get-tuple-element.149), channel_id=1, source_target_pairs={{0,16},{8,24},{16,0},{24,8},{1,17},{9,25},{17,1},{25,9},{2,18},{10... | collective-permute-start | bytes 1032200 | tf_op jit(solution)/shard_map/reduce_2_2/ppermute | solution.py:302
  119.0 21.2 %collective-permute-start.16 = (bf16[48,3584]{1,0:T(8,128)(2,1)}, bf16[48,3584]{1,0:T(8,128)(2,1)}, u32[]{:S(2)}, u32[]{:S(2)}) collective-permute-start(bf16[48,3584]{1,0:T(8,128)(2,1)} %get-tuple-element.150), channel_id=1, source_target_pairs={{0,8},{8,0},{16,24},{24,16},{1,9},{9,1},{17,25},{25,17},{2,10},{10... | collective-permute-start | bytes 1032200 | tf_op jit(solution)/shard_map/reduce_2_1/ppermute | solution.py:302
  119.5 21.7 %copy-start.5 = (bf16[48,3584]{1,0:T(8,128)(2,1)S(1)}, bf16[48,3584]{1,0:T(8,128)(2,1)}, u32[]{:S(2)}) copy-start(bf16[48,3584]{1,0:T(8,128)(2,1)} %get-tuple-element.78) | copy-start | bytes 1032196
  139.5 25.1 %collective-permute-start.19 = (bf16[48,3584]{1,0:T(8,128)(2,1)S(1)}, bf16[48,3584]{1,0:T(8,128)(2,1)S(1)}, u32[]{:S(2)}, u32[]{:S(2)}) collective-permute-start(bf16[48,3584]{1,0:T(8,128)(2,1)S(1)} %add_convert_fusion.2), channel_id=1, source_target_pairs={{0,2},{1,3},{2,6},{3,7},{4,0},{5,1},{6,4},{7,5},{8,10},{9,11},{10,... | collective-permute-start | bytes 1032200 | tf_op jit(solution)/shard_map/shares_backward_4/ppermute | solution.py:275
  142.7 21.9 %collective-permute-start.20 = (bf16[96,3584]{1,0:T(8,128)(2,1)S(1)}, bf16[96,3584]{1,0:T(8,128)(2,1)S(1)}, u32[]{:S(2)}, u32[]{:S(2)}) collective-permute-start(bf16[96,3584]{1,0:T(8,128)(2,1)S(1)} %pad_maximum_fusion.5), channel_id=1, source_target_pairs={{2,0},{3,1},{6,2},{7,3},{0,4},{1,5},{4,6},{5,7},{10,8},{11,9},{14,... | collective-permute-start | bytes 2064392 | tf_op jit(solution)/shard_map/shares_onward_4/ppermute | solution.py:275
  145.0 3.7 %copy-start.4 = (bf16[48,3584]{1,0:T(8,128)(2,1)S(1)}, bf16[48,3584]{1,0:T(8,128)(2,1)}, u32[]{:S(2)}) copy-start(bf16[48,3584]{1,0:T(8,128)(2,1)} %copy-done.3) | copy-start | bytes 1032196
  145.1 19.5 %collective-permute-start.23 = (bf16[48,3584]{1,0:T(8,128)(2,1)S(1)}, bf16[48,3584]{1,0:T(8,128)(2,1)S(1)}, u32[]{:S(2)}, u32[]{:S(2)}) collective-permute-start(bf16[48,3584]{1,0:T(8,128)(2,1)S(1)} %get-tuple-element.144), channel_id=1, source_target_pairs={{0,24},{8,16},{16,8},{24,0},{1,25},{9,17},{17,9},{25,1},{2,26},{10... | collective-permute-start | bytes 1032200 | tf_op jit(solution)/shard_map/reduce_3_3/ppermute | solution.py:302
  147.6 16.9 %collective-permute-start.22 = (bf16[48,3584]{1,0:T(8,128)(2,1)S(1)}, bf16[48,3584]{1,0:T(8,128)(2,1)S(1)}, u32[]{:S(2)}, u32[]{:S(2)}) collective-permute-start(bf16[48,3584]{1,0:T(8,128)(2,1)S(1)} %get-tuple-element.145), channel_id=1, source_target_pairs={{0,16},{8,24},{16,0},{24,8},{1,17},{9,25},{17,1},{25,9},{2,18},{10... | collective-permute-start | bytes 1032200 | tf_op jit(solution)/shard_map/reduce_3_2/ppermute | solution.py:302
  148.1 16.4 %collective-permute-start.21 = (bf16[48,3584]{1,0:T(8,128)(2,1)S(1)}, bf16[48,3584]{1,0:T(8,128)(2,1)S(1)}, u32[]{:S(2)}, u32[]{:S(2)}) collective-permute-start(bf16[48,3584]{1,0:T(8,128)(2,1)S(1)} %get-tuple-element.146), channel_id=1, source_target_pairs={{0,8},{8,0},{16,24},{24,16},{1,9},{9,1},{17,25},{25,17},{2,10},{10... | collective-permute-start | bytes 1032200 | tf_op jit(solution)/shard_map/reduce_3_1/ppermute | solution.py:302
  165.8 18.4 %collective-permute-start.25 = (bf16[96,3584]{1,0:T(8,128)(2,1)S(1)}, bf16[96,3584]{1,0:T(8,128)(2,1)S(1)}, u32[]{:S(2)}, u32[]{:S(2)}) collective-permute-start(bf16[96,3584]{1,0:T(8,128)(2,1)S(1)} %pad_maximum_fusion.7), channel_id=1, source_target_pairs={{0,8},{8,0},{16,24},{24,16},{1,9},{9,1},{17,25},{25,17},{2,10},{10... | collective-permute-start | bytes 2064392 | tf_op jit(solution)/shard_map/deliver_5_1/ppermute | solution.py:322
  167.5 31.6 %collective-permute-start.26 = (bf16[96,3584]{1,0:T(8,128)(2,1)S(1)}, bf16[96,3584]{1,0:T(8,128)(2,1)S(1)}, u32[]{:S(2)}, u32[]{:S(2)}) collective-permute-start(bf16[96,3584]{1,0:T(8,128)(2,1)S(1)} %pad_maximum_fusion.8), channel_id=1, source_target_pairs={{0,16},{8,24},{16,0},{24,8},{1,17},{9,25},{17,1},{25,9},{2,18},{10... | collective-permute-start | bytes 2064392 | tf_op jit(solution)/shard_map/deliver_5_2/ppermute | solution.py:322
  169.1 30.0 %collective-permute-start.27 = (bf16[96,3584]{1,0:T(8,128)(2,1)S(1)}, bf16[96,3584]{1,0:T(8,128)(2,1)S(1)}, u32[]{:S(2)}, u32[]{:S(2)}) collective-permute-start(bf16[96,3584]{1,0:T(8,128)(2,1)S(1)} %pad_maximum_fusion.9), channel_id=1, source_target_pairs={{0,24},{8,16},{16,8},{24,0},{1,25},{9,17},{17,9},{25,1},{2,26},{10... | collective-permute-start | bytes 2064392 | tf_op jit(solution)/shard_map/deliver_5_3/ppermute | solution.py:322
  169.8 29.2 %collective-permute-start.28 = (bf16[96,3584]{1,0:T(8,128)(2,1)S(1)}, bf16[96,3584]{1,0:T(8,128)(2,1)S(1)}, u32[]{:S(2)}, u32[]{:S(2)}) collective-permute-start(bf16[96,3584]{1,0:T(8,128)(2,1)S(1)} %get-tuple-element.166), channel_id=1, source_target_pairs={{2,0},{3,1},{6,2},{7,3},{0,4},{1,5},{4,6},{5,7},{10,8},{11,9},{14,... | collective-permute-start | bytes 2064392 | tf_op jit(solution)/shard_map/shares_onward_5/ppermute | solution.py:275
  170.6 30.4 %collective-permute-start.24 = (bf16[96,3584]{1,0:T(8,128)(2,1)S(1)}, bf16[96,3584]{1,0:T(8,128)(2,1)S(1)}, u32[]{:S(2)}, u32[]{:S(2)}) collective-permute-start(bf16[96,3584]{1,0:T(8,128)(2,1)S(1)} %get-tuple-element.167), channel_id=1, source_target_pairs={{0,2},{1,3},{2,6},{3,7},{4,0},{5,1},{6,4},{7,5},{8,10},{9,11},{10,... | collective-permute-start | bytes 2064392 | tf_op jit(solution)/shard_map/shares_backward_5/ppermute | solution.py:275
  202.4 5.2 %collective-permute-start.33 = (bf16[384,3584]{1,0:T(8,128)(2,1)S(1)}, bf16[384,3584]{1,0:T(8,128)(2,1)S(1)}, u32[]{:S(2)}, u32[]{:S(2)}) collective-permute-start(bf16[384,3584]{1,0:T(8,128)(2,1)S(1)} %select_dynamic-update-slice_fusion.own), channel_id=1, source_target_pairs={{0,1},{1,0},{2,3},{3,2},{4,5},{5,4},{6,7},{7,6},{8,9},{9,8},{10,11... | collective-permute-start | bytes 8257544 | tf_op jit(solution)/shard_map/deliver_twin_6/ppermute | solution.py:332
  202.6 15.1 %collective-permute-start.31 = (bf16[48,3584]{1,0:T(8,128)(2,1)S(1)}, bf16[48,3584]{1,0:T(8,128)(2,1)S(1)}, u32[]{:S(2)}, u32[]{:S(2)}) collective-permute-start(bf16[48,3584]{1,0:T(8,128)(2,1)S(1)} %get-tuple-element.123), channel_id=1, source_target_pairs={{0,24},{8,16},{16,8},{24,0},{1,25},{9,17},{17,9},{25,1},{2,26},{10... | collective-permute-start | bytes 1032200 | tf_op jit(solution)/shard_map/deliver_6_3/ppermute | solution.py:322
  205.2 16.3 %collective-permute-start.30 = (bf16[48,3584]{1,0:T(8,128)(2,1)S(1)}, bf16[48,3584]{1,0:T(8,128)(2,1)S(1)}, u32[]{:S(2)}, u32[]{:S(2)}) collective-permute-start(bf16[48,3584]{1,0:T(8,128)(2,1)S(1)} %get-tuple-element.124), channel_id=1, source_target_pairs={{0,16},{8,24},{16,0},{24,8},{1,17},{9,25},{17,1},{25,9},{2,18},{10... | collective-permute-start | bytes 1032200 | tf_op jit(solution)/shard_map/deliver_6_2/ppermute | solution.py:322
  205.7 15.8 %collective-permute-start.29 = (bf16[48,3584]{1,0:T(8,128)(2,1)S(1)}, bf16[48,3584]{1,0:T(8,128)(2,1)S(1)}, u32[]{:S(2)}, u32[]{:S(2)}) collective-permute-start(bf16[48,3584]{1,0:T(8,128)(2,1)S(1)} %get-tuple-element.125), channel_id=1, source_target_pairs={{0,8},{8,0},{16,24},{24,16},{1,9},{9,1},{17,25},{25,17},{2,10},{10... | collective-permute-start | bytes 1032200 | tf_op jit(solution)/shard_map/deliver_6_1/ppermute | solution.py:322
  206.3 15.2 %collective-permute-start.32 = (bf16[48,3584]{1,0:T(8,128)(2,1)S(1)}, bf16[48,3584]{1,0:T(8,128)(2,1)S(1)}, u32[]{:S(2)}, u32[]{:S(2)}) collective-permute-start(bf16[48,3584]{1,0:T(8,128)(2,1)S(1)} %get-tuple-element.160), channel_id=1, source_target_pairs={{2,0},{3,1},{6,2},{7,3},{0,4},{1,5},{4,6},{5,7},{10,8},{11,9},{14,... | collective-permute-start | bytes 1032200 | tf_op jit(solution)/shard_map/shares_onward_6/ppermute | solution.py:275
  221.8 3.8 %collective-permute-start.37 = (bf16[192,3584]{1,0:T(8,128)(2,1)S(1)}, bf16[192,3584]{1,0:T(8,128)(2,1)S(1)}, u32[]{:S(2)}, u32[]{:S(2)}) collective-permute-start(bf16[192,3584]{1,0:T(8,128)(2,1)S(1)} %pad_maximum_fusion.own), channel_id=1, source_target_pairs={{0,1},{1,0},{2,3},{3,2},{4,5},{5,4},{6,7},{7,6},{8,9},{9,8},{10,11... | collective-permute-start | bytes 4128776 | tf_op jit(solution)/shard_map/deliver_twin_7/ppermute | solution.py:332
  222.0 18.3 %collective-permute-start.36 = (bf16[48,3584]{1,0:T(8,128)(2,1)S(1)}, bf16[48,3584]{1,0:T(8,128)(2,1)S(1)}, u32[]{:S(2)}, u32[]{:S(2)}) collective-permute-start(bf16[48,3584]{1,0:T(8,128)(2,1)S(1)} %get-tuple-element.126), channel_id=1, source_target_pairs={{0,24},{8,16},{16,8},{24,0},{1,25},{9,17},{17,9},{25,1},{2,26},{10... | collective-permute-start | bytes 1032200 | tf_op jit(solution)/shard_map/deliver_7_3/ppermute | solution.py:322
  223.7 17.1 %collective-permute-start.35 = (bf16[48,3584]{1,0:T(8,128)(2,1)S(1)}, bf16[48,3584]{1,0:T(8,128)(2,1)S(1)}, u32[]{:S(2)}, u32[]{:S(2)}) collective-permute-start(bf16[48,3584]{1,0:T(8,128)(2,1)S(1)} %get-tuple-element.127), channel_id=1, source_target_pairs={{0,16},{8,24},{16,0},{24,8},{1,17},{9,25},{17,1},{25,9},{2,18},{10... | collective-permute-start | bytes 1032200 | tf_op jit(solution)/shard_map/deliver_7_2/ppermute | solution.py:322
  225.0 15.8 %collective-permute-start.34 = (bf16[48,3584]{1,0:T(8,128)(2,1)S(1)}, bf16[48,3584]{1,0:T(8,128)(2,1)S(1)}, u32[]{:S(2)}, u32[]{:S(2)}) collective-permute-start(bf16[48,3584]{1,0:T(8,128)(2,1)S(1)} %get-tuple-element.128), channel_id=1, source_target_pairs={{0,8},{8,0},{16,24},{24,16},{1,9},{9,1},{17,25},{25,17},{2,10},{10... | collective-permute-start | bytes 1032200 | tf_op jit(solution)/shard_map/deliver_7_1/ppermute | solution.py:322
  225.6 5.1 %copy-start = (bf16[1024,256]{1,0:T(8,128)(2,1)S(1)}, bf16[1024,256]{1,0:T(8,128)(2,1)}, u32[]{:S(2)}) copy-start(bf16[1024,256]{1,0:T(8,128)(2,1)} %tokens.3) | copy-start | bytes 1572868
  241.1 3.2 %collective-permute-start.38 = (bf16[192,3584]{1,0:T(8,128)(2,1)S(1)}, bf16[192,3584]{1,0:T(8,128)(2,1)S(1)}, u32[]{:S(2)}, u32[]{:S(2)}) collective-permute-start(bf16[192,3584]{1,0:T(8,128)(2,1)S(1)} %pad_maximum_fusion.1.own), channel_id=1, source_target_pairs={{0,1},{1,0},{2,3},{3,2},{4,5},{5,4},{6,7},{7,6},{8,9},{9,8},{10,11... | collective-permute-start | bytes 4128776 | tf_op jit(solution)/shard_map/deliver_twin_8/ppermute | solution.py:332
  260.3 6.4 %collective-permute-start.39 = (bf16[512,128]{1,0:T(8,128)(2,1)S(1)}, bf16[512,128]{1,0:T(8,128)(2,1)S(1)}, u32[]{:S(2)}, u32[]{:S(2)}) collective-permute-start(bf16[512,128]{1,0:T(8,128)(2,1)S(1)} %get-tuple-element.163), channel_id=1, source_target_pairs={{0,8},{8,0},{16,24},{24,16},{1,9},{9,1},{17,25},{25,17},{2,10},{10... | collective-permute-start | bytes 393224 | tf_op jit(solution)/shard_map/check_reduce_1/ppermute | solution.py:362
  261.5 8.2 %collective-permute-start.41 = (bf16[512,128]{1,0:T(8,128)(2,1)S(1)}, bf16[512,128]{1,0:T(8,128)(2,1)S(1)}, u32[]{:S(2)}, u32[]{:S(2)}) collective-permute-start(bf16[512,128]{1,0:T(8,128)(2,1)S(1)} %get-tuple-element.164), channel_id=1, source_target_pairs={{0,24},{8,16},{16,8},{24,0},{1,25},{9,17},{17,9},{25,1},{2,26},{10... | collective-permute-start | bytes 393224 | tf_op jit(solution)/shard_map/check_reduce_3/ppermute | solution.py:362
  263.3 7.8 %collective-permute-start.40 = (bf16[512,128]{1,0:T(8,128)(2,1)S(1)}, bf16[512,128]{1,0:T(8,128)(2,1)S(1)}, u32[]{:S(2)}, u32[]{:S(2)}) collective-permute-start(bf16[512,128]{1,0:T(8,128)(2,1)S(1)} %get-tuple-element.165), channel_id=1, source_target_pairs={{0,16},{8,24},{16,0},{24,8},{1,17},{9,25},{17,1},{25,9},{2,18},{10... | collective-permute-start | bytes 393224 | tf_op jit(solution)/shard_map/check_reduce_2/ppermute | solution.py:362
  (1 other events, 1.1 us)

commit v4 on v3

--- a/solution.py
+++ b/solution.py
@@ -152,7 +152,7 @@
     )(scalars, tokens, gu)
 
 
-def forward_kernel(steps, groups, t, scalars, tokens, own, far, a_gu, a_dn, ready, gu, dn, gu_out, dn_out, check_out, total, hidden):
+def forward_kernel(steps, groups, t, scalars, tokens, own, far, a_gu, a_dn, ready, gu, dn, gu_out, dn_out, check_out, total):
     step = pl.program_id(0)
     features = tokens.shape[1]
     scale = features ** (-0.5)
@@ -180,7 +180,11 @@
             part += lax.dot_general(
                 value, with_last(dn, dn_out, place, columns), (((1,), (1,)), ((), ())), preferred_element_type=F32
             )
-        hidden[...] = part
+        total[...] += part
+
+    @pl.when(step == 0)
+    def _():
+        total[...] = jnp.zeros_like(total)
 
     @pl.when(gate_ready)
     def _():
@@ -189,14 +193,6 @@
     @pl.when(jnp.logical_not(gate_ready))
     def _():
         run(False)
-
-    @pl.when(step == 0)
-    def _():
-        total[...] = hidden[...]
-
-    @pl.when(step > 0)
-    def _():
-        total[...] += hidden[...]
 
     @pl.when(step == 2 * steps - 1)
     def _():
@@ -230,7 +226,7 @@
             grid=(2 * steps,),
             in_specs=[pl.BlockSpec(tokens.shape, lambda i, s: (0, 0))] + pieces + group + [known, half, slab[1]],
             out_specs=group + [pl.BlockSpec(check_shape, lambda i, s: (0, 0, 0))],
-            scratch_shapes=[pltpu.VMEM((count, features), F32), pltpu.VMEM((count, features), F32)],
+            scratch_shapes=[pltpu.VMEM((count, features), F32)],
         ),
         out_shape=[
             jax.ShapeDtypeStruct(a_gu.shape, BF16),

time: 273 us -> 273 us (level)
  no operation moved by 1% of the time
where the time goes in v4:
time: 273 us; the launch traced here: 272 us
  Pallas kernels  121 us (44%)
  waiting for transfers between devices  89.2 us (33%)
  starting transfers between devices  44.4 us (16%)
  other arithmetic  8.92 us (3%)
  local copies, waits for them, and re-layouts  7.02 us (3%)
    pallas_call x4, Pallas kernels, project(): pl.pallas_call(project_kernel, grid_spec=pltpu.PrefetchScalarGridSpec(num...  80.6 us
    ppermute x9, waiting for transfers between devices, on_device(): lax.ppermute(cat([for_row(held[t], q ^ d) for t in deliver]), 'row', peer...  30.3 us
    ppermute x8, waiting for transfers between devices, along_ring(): return lax.ppermute(cat([held[t][i] for t, i, _ in step]), 'col', perm)  29.9 us
    ppermute x3, waiting for transfers between devices, on_device(): out['rows'] = lax.ppermute(rows, 'col', ring)  18 us
    pallas_call x1, Pallas kernels, forward(): pl.pallas_call(functools.partial(forward_kernel, steps, groups, t), grid_...  15.8 us
    pallas_call x3, Pallas kernels, merge_group(): pl.pallas_call(functools.partial(merge_kernel, steps), grid_spec=pltpu.Pr...  15.2 us
    ppermute x12, starting transfers between devices, on_device(): out['sums'].append(lax.ppermute(part, 'row', peers(d)))  14.2 us
    ppermute x9, starting transfers between devices, on_device(): lax.ppermute(cat([for_row(held[t], q ^ d) for t in deliver]), 'row', peer...  10.9 us
  transfers between devices with their start and end apart: 42, of which 15 were waited for; matrix products, arithmetic and copies ran while one was open for 3% of the time, Pallas kernels for 39%

profile of v4, /device:TPU:0, one launch (start us, length us, event | category | flops | bytes accessed | tf_op | source)
XLA Modules:
  0.0 271.7 jit_solution(17071453869670881625)
XLA Ops:
  0.6 1.3 constant_dynamic-update-slice_fusion.1
  2.5 2.6 collective-permute-start.1
  5.3 1.1 copy-done.1
  6.3 1.3 copy-done.2
  7.7 19.9 %project.4 = bf16[2,96,3584]{2,1,0:T(8,128)(2,1)S(1)} custom-call(s32[5]{0:T(128)S(1)} %stack.23.scalars, bf16[96,7168]{1,0:T(8,128)(2,1)S(1)} %constant_dynamic-update-slice_fusion.mine, bf16[96,7168]{1,0:T(8,128)(2,1)S(1)} %copy-done.2, bf16[7168,3584]{1,0:T(8,128)(2,1)} %panel.7), custom_call_target="tpu_custom_call" | custom-call | tf_op jit(solution)/shard_map/project/pallas_call | solution.py:53
  27.6 9.4 %collective-permute-done.1.mine = bf16[96,7168]{1,0:T(8,128)(2,1)} collective-permute-done((bf16[96,7168]{1,0:T(8,128)(2,1)S(1)}, bf16[96,7168]{1,0:T(8,128)(2,1)}, u32[]{:S(2)}, u32[]{:S(2)}) %collective-permute-start.1) | collective-permute-done | bytes 1376288 | tf_op jit(solution)/shard_map/rows_ring_0/ppermute | solution.py:288
  37.9 2.5 collective-permute-start.6
  41.4 20.7 %project.5 = bf16[2,96,3584]{2,1,0:T(8,128)(2,1)S(1)} custom-call(s32[5]{0:T(128)S(1)} %stack.23.scalars, bf16[96,7168]{1,0:T(8,128)(2,1)} %collective-permute-done.1.mine, bf16[96,7168]{1,0:T(8,128)(2,1)} %collective-permute-done.2.theirs, bf16[7168,3584]{1,0:T(8,128)(2,1)} %panel.7), custom_call_target="tpu_custom_call" | custom-call | tf_op jit(solution)/shard_map/project/pallas_call | solution.py:53
  62.2 8.5 %collective-permute-done.3.mine = bf16[96,7168]{1,0:T(8,128)(2,1)S(1)} collective-permute-done((bf16[96,7168]{1,0:T(8,128)(2,1)}, bf16[96,7168]{1,0:T(8,128)(2,1)S(1)}, u32[]{:S(2)}, u32[]{:S(2)}) %collective-permute-start.3) | collective-permute-done | bytes 1376288 | tf_op jit(solution)/shard_map/rows_ring_1/ppermute | solution.py:288
  70.8 0.9 collective-permute-start.10
  71.9 2.0 collective-permute-start.8
  74.0 2.6 collective-permute-start.13
  77.6 19.9 %project.6 = bf16[2,96,3584]{2,1,0:T(8,128)(2,1)S(1)} custom-call(s32[5]{0:T(128)S(1)} %stack.23.scalars, bf16[96,7168]{1,0:T(8,128)(2,1)S(1)} %collective-permute-done.3.mine, bf16[96,7168]{1,0:T(8,128)(2,1)S(1)} %collective-permute-done.9.theirs, bf16[7168,3584]{1,0:T(8,128)(2,1)} %panel.7), custom_call_target="tpu_custom_call" | custom-call | tf_op jit(solution)/shard_map/project/pallas_call | solution.py:53
  97.5 13.3 %collective-permute-done.8 = bf16[48,3584]{1,0:T(8,128)(2,1)S(1)} collective-permute-done((bf16[48,3584]{1,0:T(8,128)(2,1)S(1)}, bf16[48,3584]{1,0:T(8,128)(2,1)S(1)}, u32[]{:S(2)}, u32[]{:S(2)}) %collective-permute-start.8) | collective-permute-done | bytes 344096 | tf_op jit(solution)/shard_map/shares_onward_2/ppermute | solution.py:271
  110.8 1.6 collective-permute-start.7
  113.6 1.3 collective-permute-start.14
  114.9 1.1 dynamic-slice_bitcast_fusion.4
  116.0 2.5 collective-permute-start.18
  119.5 19.9 %project.7 = bf16[2,96,3584]{2,1,0:T(8,128)(2,1)S(1)} custom-call(s32[5]{0:T(128)S(1)} %stack.23.scalars, bf16[96,7168]{1,0:T(8,128)(2,1)S(1)} %collective-permute-done.10.mine, bf16[96,7168]{1,0:T(8,128)(2,1)S(1)} %collective-permute-done.15.theirs, bf16[7168,3584]{1,0:T(8,128)(2,1)} %panel.7), custom_call_target="tpu_custom_call" | custom-call | tf_op jit(solution)/shard_map/project/pallas_call | solution.py:53
  140.2 1.0 slice.48
  141.3 1.4 add_convert_fusion.1
  142.7 2.3 collective-permute-start.20
  145.1 2.6 collective-permute-start.23
  148.6 1.2 select_select_fusion.17
  149.9 14.7 %collective-permute-done.19 = bf16[48,3584]{1,0:T(8,128)(2,1)S(1)} collective-permute-done((bf16[48,3584]{1,0:T(8,128)(2,1)S(1)}, bf16[48,3584]{1,0:T(8,128)(2,1)S(1)}, u32[]{:S(2)}, u32[]{:S(2)}) %collective-permute-start.19) | collective-permute-done | bytes 344096 | tf_op jit(solution)/shard_map/shares_backward_4/ppermute | solution.py:271
  164.6 1.1 select_select_fusion.16
  165.8 1.6 collective-permute-start.25
  167.5 1.6 collective-permute-start.26
  170.6 1.3 collective-permute-start.24
  171.9 1.1 select_select_fusion.22
  173.1 11.1 %collective-permute-done.25 = bf16[96,3584]{1,0:T(8,128)(2,1)S(1)} collective-permute-done((bf16[96,3584]{1,0:T(8,128)(2,1)S(1)}, bf16[96,3584]{1,0:T(8,128)(2,1)S(1)}, u32[]{:S(2)}, u32[]{:S(2)}) %collective-permute-start.25) | collective-permute-done | bytes 688160 | tf_op jit(solution)/shard_map/deliver_5_1/ppermute | solution.py:318
  184.2 14.9 %collective-permute-done.26 = bf16[96,3584]{1,0:T(8,128)(2,1)S(1)} collective-permute-done((bf16[96,3584]{1,0:T(8,128)(2,1)S(1)}, bf16[96,3584]{1,0:T(8,128)(2,1)S(1)}, u32[]{:S(2)}, u32[]{:S(2)}) %collective-permute-start.26) | collective-permute-done | bytes 688160 | tf_op jit(solution)/shard_map/deliver_5_2/ppermute | solution.py:318
  199.1 1.9 collective-permute-done.24
  202.6 2.5 collective-permute-start.31
  207.6 5.0 %merge.3 = (bf16[512,7168]{1,0:T(8,128)(2,1)}, bf16[256,7168]{1,0:T(8,128)(2,1)}) custom-call(s32[5]{0:T(128)S(1)} %stack.23.scalars, bf16[384,3584]{1,0:T(8,128)(2,1)S(1)} %select_dynamic-update-slice_fusion.own, bf16[384,3584]{1,0:T(8,128)(2,1)S(1)} %collective-permute-done.33.far, bf16[512,7168]{1,0:T(8,128)(2,1)} %a_gu.7, bf16[256,7168]{1,0:T(8,128)(2,1)} %a_dn.7), custom_call_target="tpu_custom_call" | custom-call | tf_op jit(solution)/shard_map/merge/pallas_call | solution.py:115
  212.6 5.0 %merge.4 = (bf16[512,7168]{1,0:T(8,128)(2,1)}, bf16[256,7168]{1,0:T(8,128)(2,1)}) custom-call(s32[5]{0:T(128)S(1)} %stack.23.scalars, bf16[384,3584]{1,0:T(8,128)(2,1)S(1)} %select_dynamic-update-slice_fusion.own, bf16[384,3584]{1,0:T(8,128)(2,1)S(1)} %collective-permute-done.33.far, ...), custom_call_target="tpu_custom_call", output_to_operand_aliasing={{0}: (5, {}), {1}: (6, {})} | custom-call | tf_op jit(solution)/shard_map/merge/pallas_call | solution.py:115
  217.7 3.7 %collective-permute-done.30 = bf16[48,3584]{1,0:T(8,128)(2,1)S(1)} collective-permute-done((bf16[48,3584]{1,0:T(8,128)(2,1)S(1)}, bf16[48,3584]{1,0:T(8,128)(2,1)S(1)}, u32[]{:S(2)}, u32[]{:S(2)}) %collective-permute-start.30) | collective-permute-done | bytes 344096 | tf_op jit(solution)/shard_map/deliver_6_2/ppermute | solution.py:318
  222.0 1.7 collective-permute-start.36
  223.7 1.3 collective-permute-start.35
  225.7 5.1 %merge.5 = (bf16[512,7168]{1,0:T(8,128)(2,1)}, bf16[256,7168]{1,0:T(8,128)(2,1)}) custom-call(s32[5]{0:T(128)S(1)} %stack.23.scalars, bf16[192,3584]{1,0:T(8,128)(2,1)S(1)} %pad_maximum_fusion.own, bf16[192,3584]{1,0:T(8,128)(2,1)S(1)} %collective-permute-done.37.far, bf16[512,7168]{1,0:T(8,128)(2,1)} %a_gu.7, ...), custom_call_target="tpu_custom_call", output_to_operand_aliasing={{0}: (5, {}), {1}: (6, {})} | custom-call | tf_op jit(solution)/shard_map/merge/pallas_call | solution.py:115
  230.7 9.6 %ready.1 = bf16[1024,7168]{1,0:T(8,128)(2,1)} custom-call(s32[5]{0:T(128)S(1)} %stack.23.scalars, bf16[1024,256]{1,0:T(8,128)(2,1)S(1)} %copy-done, bf16[512,7168]{1,0:T(8,128)(2,1)} %get-tuple-element.118.rows.gu), custom_call_target="tpu_custom_call" | custom-call | tf_op jit(solution)/shard_map/ready/pallas_call | solution.py:138
  241.2 3.1 %collective-permute-done.38.far = bf16[192,3584]{1,0:T(8,128)(2,1)S(1)} collective-permute-done((bf16[192,3584]{1,0:T(8,128)(2,1)S(1)}, bf16[192,3584]{1,0:T(8,128)(2,1)S(1)}, u32[]{:S(2)}, u32[]{:S(2)}) %collective-permute-start.38) | collective-permute-done | bytes 1376288 | tf_op jit(solution)/shard_map/deliver_twin_8/ppermute | solution.py:328
  244.3 15.8 %forward.1 = (bf16[512,7168]{1,0:T(8,128)(2,1)}, bf16[256,7168]{1,0:T(8,128)(2,1)}, bf16[4,512,128]{2,1,0:T(8,128)(2,1)S(1)}) custom-call(s32[5]{0:T(128)S(1)} %stack.23.scalars, bf16[1024,256]{1,0:T(8,128)(2,1)S(1)} %copy-done, bf16[192,3584]{1,0:T(8,128)(2,1)S(1)} %pad_maximum_fusion.1.own, ...), custom_call_target="tpu_custom_call", output_to_operand_aliasing={{0}: (7, {}), {1}: (8, {})} | custom-call | tf_op jit(solution)/shard_map/forward/pallas_call | solution.py:222
  260.1 1.1 collective-permute-start.39
  261.3 1.8 collective-permute-start.41
  263.7 2.9 %collective-permute-done.39 = bf16[512,128]{1,0:T(8,128)(2,1)S(1)} collective-permute-done((bf16[512,128]{1,0:T(8,128)(2,1)S(1)}, bf16[512,128]{1,0:T(8,128)(2,1)S(1)}, u32[]{:S(2)}, u32[]{:S(2)}) %collective-permute-start.39) | collective-permute-done | bytes 131104 | tf_op jit(solution)/shard_map/check_reduce_1/ppermute | solution.py:358
  266.5 3.0 %collective-permute-done.41 = bf16[512,128]{1,0:T(8,128)(2,1)S(1)} collective-permute-done((bf16[512,128]{1,0:T(8,128)(2,1)S(1)}, bf16[512,128]{1,0:T(8,128)(2,1)S(1)}, u32[]{:S(2)}, u32[]{:S(2)}) %collective-permute-start.41) | collective-permute-done | bytes 131104 | tf_op jit(solution)/shard_map/check_reduce_3/ppermute | solution.py:358
  269.5 1.4 collective-permute-done.40
  (101 shorter events, 17.1 us)
Async XLA Ops:
  0.6 1.3 copy-start.6
  2.0 3.3 %collective-permute-start = (bf16[96,7168]{1,0:T(8,128)(2,1)S(1)}, bf16[96,7168]{1,0:T(8,128)(2,1)S(1)}, u32[]{:S(2)}, u32[]{:S(2)}) collective-permute-start(bf16[96,7168]{1,0:T(8,128)(2,1)S(1)} %constant_dynamic-update-slice_fusion.mine), channel_id=1, source_target_pairs={{0,1},{1,0},{2,3},{3,2},{4,5},{5,4},{6,7},{7,6},{8,9},{9,8},{10,11... | collective-permute-start | bytes 4128776 | tf_op jit(solution)/shard_map/rows_twin_0/ppermute | solution.py:290
  2.5 34.5 %collective-permute-start.1 = (bf16[96,7168]{1,0:T(8,128)(2,1)S(1)}, bf16[96,7168]{1,0:T(8,128)(2,1)}, u32[]{:S(2)}, u32[]{:S(2)}) collective-permute-start(bf16[96,7168]{1,0:T(8,128)(2,1)S(1)} %constant_dynamic-update-slice_fusion.mine), channel_id=1, source_target_pairs={{0,2},{1,3},{2,6},{3,7},{4,0},{5,1},{6,4},{7,5},{8,10},{9,11},{10,... | collective-permute-start | bytes 4128776 | tf_op jit(solution)/shard_map/rows_ring_0/ppermute | solution.py:288
  6.3 1.3 copy-start.2
  37.0 4.4 %collective-permute-start.2 = (bf16[96,7168]{1,0:T(8,128)(2,1)}, bf16[96,7168]{1,0:T(8,128)(2,1)}, u32[]{:S(2)}, u32[]{:S(2)}) collective-permute-start(bf16[96,7168]{1,0:T(8,128)(2,1)} %collective-permute-done.1.mine), channel_id=1, source_target_pairs={{0,1},{1,0},{2,3},{3,2},{4,5},{5,4},{6,7},{7,6},{8,9},{9,8},{10,11... | collective-permute-start | bytes 4128776 | tf_op jit(solution)/shard_map/rows_twin_1/ppermute | solution.py:290
  37.0 33.7 %collective-permute-start.3 = (bf16[96,7168]{1,0:T(8,128)(2,1)}, bf16[96,7168]{1,0:T(8,128)(2,1)S(1)}, u32[]{:S(2)}, u32[]{:S(2)}) collective-permute-start(bf16[96,7168]{1,0:T(8,128)(2,1)} %collective-permute-done.1.mine), channel_id=1, source_target_pairs={{0,2},{1,3},{2,6},{3,7},{4,0},{5,1},{6,4},{7,5},{8,10},{9,11},{10,... | collective-permute-start | bytes 4128776 | tf_op jit(solution)/shard_map/rows_ring_1/ppermute | solution.py:288
  37.9 24.3 %collective-permute-start.6 = (bf16[48,3584]{1,0:T(8,128)(2,1)S(1)}, bf16[48,3584]{1,0:T(8,128)(2,1)S(1)}, u32[]{:S(2)}, u32[]{:S(2)}) collective-permute-start(bf16[48,3584]{1,0:T(8,128)(2,1)S(1)} %get-tuple-element.156), channel_id=1, source_target_pairs={{0,24},{8,16},{16,8},{24,0},{1,25},{9,17},{17,9},{25,1},{2,26},{10... | collective-permute-start | bytes 1032200 | tf_op jit(solution)/shard_map/reduce_0_3/ppermute | solution.py:298
  40.4 21.8 %collective-permute-start.5 = (bf16[48,3584]{1,0:T(8,128)(2,1)S(1)}, bf16[48,3584]{1,0:T(8,128)(2,1)S(1)}, u32[]{:S(2)}, u32[]{:S(2)}) collective-permute-start(bf16[48,3584]{1,0:T(8,128)(2,1)S(1)} %get-tuple-element.157), channel_id=1, source_target_pairs={{0,16},{8,24},{16,0},{24,8},{1,17},{9,25},{17,1},{25,9},{2,18},{10... | collective-permute-start | bytes 1032200 | tf_op jit(solution)/shard_map/reduce_0_2/ppermute | solution.py:298
  40.9 21.3 %collective-permute-start.4 = (bf16[48,3584]{1,0:T(8,128)(2,1)S(1)}, bf16[48,3584]{1,0:T(8,128)(2,1)S(1)}, u32[]{:S(2)}, u32[]{:S(2)}) collective-permute-start(bf16[48,3584]{1,0:T(8,128)(2,1)S(1)} %get-tuple-element.158), channel_id=1, source_target_pairs={{0,8},{8,0},{16,24},{24,16},{1,9},{9,1},{17,25},{25,17},{2,10},{10... | collective-permute-start | bytes 1032200 | tf_op jit(solution)/shard_map/reduce_0_1/ppermute | solution.py:298
  70.8 41.7 %collective-permute-start.10 = (bf16[96,7168]{1,0:T(8,128)(2,1)S(1)}, bf16[96,7168]{1,0:T(8,128)(2,1)S(1)}, u32[]{:S(2)}, u32[]{:S(2)}) collective-permute-start(bf16[96,7168]{1,0:T(8,128)(2,1)S(1)} %collective-permute-done.3.mine), channel_id=1, source_target_pairs={{0,2},{1,3},{2,6},{3,7},{4,0},{5,1},{6,4},{7,5},{8,10},{9,11},{10,... | collective-permute-start | bytes 4128776 | tf_op jit(solution)/shard_map/rows_ring_2/ppermute | solution.py:288
  71.7 5.4 %collective-permute-start.9 = (bf16[96,7168]{1,0:T(8,128)(2,1)S(1)}, bf16[96,7168]{1,0:T(8,128)(2,1)S(1)}, u32[]{:S(2)}, u32[]{:S(2)}) collective-permute-start(bf16[96,7168]{1,0:T(8,128)(2,1)S(1)} %collective-permute-done.3.mine), channel_id=1, source_target_pairs={{0,1},{1,0},{2,3},{3,2},{4,5},{5,4},{6,7},{7,6},{8,9},{9,8},{10,11... | collective-permute-start | bytes 4128776 | tf_op jit(solution)/shard_map/rows_twin_2/ppermute | solution.py:290
  71.9 39.0 %collective-permute-start.8 = (bf16[48,3584]{1,0:T(8,128)(2,1)S(1)}, bf16[48,3584]{1,0:T(8,128)(2,1)S(1)}, u32[]{:S(2)}, u32[]{:S(2)}) collective-permute-start(bf16[48,3584]{1,0:T(8,128)(2,1)S(1)} %add_convert_fusion.3), channel_id=1, source_target_pairs={{2,0},{3,1},{6,2},{7,3},{0,4},{1,5},{4,6},{5,7},{10,8},{11,9},{14,... | collective-permute-start | bytes 1032200 | tf_op jit(solution)/shard_map/shares_onward_2/ppermute | solution.py:271
  74.0 38.4 %collective-permute-start.13 = (bf16[48,3584]{1,0:T(8,128)(2,1)S(1)}, bf16[48,3584]{1,0:T(8,128)(2,1)S(1)}, u32[]{:S(2)}, u32[]{:S(2)}) collective-permute-start(bf16[48,3584]{1,0:T(8,128)(2,1)S(1)} %get-tuple-element.152), channel_id=1, source_target_pairs={{0,24},{8,16},{16,8},{24,0},{1,25},{9,17},{17,9},{25,1},{2,26},{10... | collective-permute-start | bytes 1032200 | tf_op jit(solution)/shard_map/reduce_1_3/ppermute | solution.py:298
  76.6 35.8 %collective-permute-start.12 = (bf16[48,3584]{1,0:T(8,128)(2,1)S(1)}, bf16[48,3584]{1,0:T(8,128)(2,1)S(1)}, u32[]{:S(2)}, u32[]{:S(2)}) collective-permute-start(bf16[48,3584]{1,0:T(8,128)(2,1)S(1)} %get-tuple-element.153), channel_id=1, source_target_pairs={{0,16},{8,24},{16,0},{24,8},{1,17},{9,25},{17,1},{25,9},{2,18},{10... | collective-permute-start | bytes 1032200 | tf_op jit(solution)/shard_map/reduce_1_2/ppermute | solution.py:298
  77.1 35.3 %collective-permute-start.11 = (bf16[48,3584]{1,0:T(8,128)(2,1)S(1)}, bf16[48,3584]{1,0:T(8,128)(2,1)S(1)}, u32[]{:S(2)}, u32[]{:S(2)}) collective-permute-start(bf16[48,3584]{1,0:T(8,128)(2,1)S(1)} %get-tuple-element.154), channel_id=1, source_target_pairs={{0,8},{8,0},{16,24},{24,16},{1,9},{9,1},{17,25},{25,17},{2,10},{10... | collective-permute-start | bytes 1032200 | tf_op jit(solution)/shard_map/reduce_1_1/ppermute | solution.py:298
  110.8 2.8 %copy-start.3 = (bf16[48,3584]{1,0:T(8,128)(2,1)}, bf16[48,3584]{1,0:T(8,128)(2,1)S(1)}, u32[]{:S(2)}) copy-start(bf16[48,3584]{1,0:T(8,128)(2,1)S(1)} %collective-permute-done.8) | copy-start | bytes 1032196
  110.8 28.6 %collective-permute-start.7 = (bf16[48,3584]{1,0:T(8,128)(2,1)S(1)}, bf16[48,3584]{1,0:T(8,128)(2,1)}, u32[]{:S(2)}, u32[]{:S(2)}) collective-permute-start(bf16[48,3584]{1,0:T(8,128)(2,1)S(1)} %add_convert_fusion.3), channel_id=1, source_target_pairs={{0,2},{1,3},{2,6},{3,7},{4,0},{5,1},{6,4},{7,5},{8,10},{9,11},{10,... | collective-permute-start | bytes 1032200 | tf_op jit(solution)/shard_map/shares_backward_3/ppermute | solution.py:271
  112.4 6.6 %collective-permute-start.15 = (bf16[96,7168]{1,0:T(8,128)(2,1)S(1)}, bf16[96,7168]{1,0:T(8,128)(2,1)S(1)}, u32[]{:S(2)}, u32[]{:S(2)}) collective-permute-start(bf16[96,7168]{1,0:T(8,128)(2,1)S(1)} %collective-permute-done.10.mine), channel_id=1, source_target_pairs={{0,1},{1,0},{2,3},{3,2},{4,5},{5,4},{6,7},{7,6},{8,9},{9,8},{10,11... | collective-permute-start | bytes 4128776 | tf_op jit(solution)/shard_map/rows_twin_3/ppermute | solution.py:290
  113.6 26.6 %collective-permute-start.14 = (bf16[96,3584]{1,0:T(8,128)(2,1)}, bf16[96,3584]{1,0:T(8,128)(2,1)}, u32[]{:S(2)}, u32[]{:S(2)}) collective-permute-start(bf16[96,3584]{1,0:T(8,128)(2,1)} %pad_maximum_fusion.4), channel_id=1, source_target_pairs={{2,0},{3,1},{6,2},{7,3},{0,4},{1,5},{4,6},{5,7},{10,8},{11,9},{14,... | collective-permute-start | bytes 2064392 | tf_op jit(solution)/shard_map/shares_onward_3/ppermute | solution.py:271
  116.0 24.2 %collective-permute-start.18 = (bf16[48,3584]{1,0:T(8,128)(2,1)}, bf16[48,3584]{1,0:T(8,128)(2,1)}, u32[]{:S(2)}, u32[]{:S(2)}) collective-permute-start(bf16[48,3584]{1,0:T(8,128)(2,1)} %get-tuple-element.148), channel_id=1, source_target_pairs={{0,24},{8,16},{16,8},{24,0},{1,25},{9,17},{17,9},{25,1},{2,26},{10... | collective-permute-start | bytes 1032200 | tf_op jit(solution)/shard_map/reduce_2_3/ppermute | solution.py:298
  118.5 21.7 %collective-permute-start.17 = (bf16[48,3584]{1,0:T(8,128)(2,1)}, bf16[48,3584]{1,0:T(8,128)(2,1)}, u32[]{:S(2)}, u32[]{:S(2)}) collective-permute-start(bf16[48,3584]{1,0:T(8,128)(2,1)} %get-tuple-element.149), channel_id=1, source_target_pairs={{0,16},{8,24},{16,0},{24,8},{1,17},{9,25},{17,1},{25,9},{2,18},{10... | collective-permute-start | bytes 1032200 | tf_op jit(solution)/shard_map/reduce_2_2/ppermute | solution.py:298
  119.0 21.2 %collective-permute-start.16 = (bf16[48,3584]{1,0:T(8,128)(2,1)}, bf16[48,3584]{1,0:T(8,128)(2,1)}, u32[]{:S(2)}, u32[]{:S(2)}) collective-permute-start(bf16[48,3584]{1,0:T(8,128)(2,1)} %get-tuple-element.150), channel_id=1, source_target_pairs={{0,8},{8,0},{16,24},{24,16},{1,9},{9,1},{17,25},{25,17},{2,10},{10... | collective-permute-start | bytes 1032200 | tf_op jit(solution)/shard_map/reduce_2_1/ppermute | solution.py:298
  119.5 21.7 %copy-start.5 = (bf16[48,3584]{1,0:T(8,128)(2,1)S(1)}, bf16[48,3584]{1,0:T(8,128)(2,1)}, u32[]{:S(2)}) copy-start(bf16[48,3584]{1,0:T(8,128)(2,1)} %get-tuple-element.78) | copy-start | bytes 1032196
  139.5 25.1 %collective-permute-start.19 = (bf16[48,3584]{1,0:T(8,128)(2,1)S(1)}, bf16[48,3584]{1,0:T(8,128)(2,1)S(1)}, u32[]{:S(2)}, u32[]{:S(2)}) collective-permute-start(bf16[48,3584]{1,0:T(8,128)(2,1)S(1)} %add_convert_fusion.2), channel_id=1, source_target_pairs={{0,2},{1,3},{2,6},{3,7},{4,0},{5,1},{6,4},{7,5},{8,10},{9,11},{10,... | collective-permute-start | bytes 1032200 | tf_op jit(solution)/shard_map/shares_backward_4/ppermute | solution.py:271
  142.7 21.9 %collective-permute-start.20 = (bf16[96,3584]{1,0:T(8,128)(2,1)S(1)}, bf16[96,3584]{1,0:T(8,128)(2,1)S(1)}, u32[]{:S(2)}, u32[]{:S(2)}) collective-permute-start(bf16[96,3584]{1,0:T(8,128)(2,1)S(1)} %pad_maximum_fusion.5), channel_id=1, source_target_pairs={{2,0},{3,1},{6,2},{7,3},{0,4},{1,5},{4,6},{5,7},{10,8},{11,9},{14,... | collective-permute-start | bytes 2064392 | tf_op jit(solution)/shard_map/shares_onward_4/ppermute | solution.py:271
  145.0 3.7 %copy-start.4 = (bf16[48,3584]{1,0:T(8,128)(2,1)S(1)}, bf16[48,3584]{1,0:T(8,128)(2,1)}, u32[]{:S(2)}) copy-start(bf16[48,3584]{1,0:T(8,128)(2,1)} %copy-done.3) | copy-start | bytes 1032196
  145.1 19.5 %collective-permute-start.23 = (bf16[48,3584]{1,0:T(8,128)(2,1)S(1)}, bf16[48,3584]{1,0:T(8,128)(2,1)S(1)}, u32[]{:S(2)}, u32[]{:S(2)}) collective-permute-start(bf16[48,3584]{1,0:T(8,128)(2,1)S(1)} %get-tuple-element.144), channel_id=1, source_target_pairs={{0,24},{8,16},{16,8},{24,0},{1,25},{9,17},{17,9},{25,1},{2,26},{10... | collective-permute-start | bytes 1032200 | tf_op jit(solution)/shard_map/reduce_3_3/ppermute | solution.py:298
  147.6 16.9 %collective-permute-start.22 = (bf16[48,3584]{1,0:T(8,128)(2,1)S(1)}, bf16[48,3584]{1,0:T(8,128)(2,1)S(1)}, u32[]{:S(2)}, u32[]{:S(2)}) collective-permute-start(bf16[48,3584]{1,0:T(8,128)(2,1)S(1)} %get-tuple-element.145), channel_id=1, source_target_pairs={{0,16},{8,24},{16,0},{24,8},{1,17},{9,25},{17,1},{25,9},{2,18},{10... | collective-permute-start | bytes 1032200 | tf_op jit(solution)/shard_map/reduce_3_2/ppermute | solution.py:298
  148.1 16.4 %collective-permute-start.21 = (bf16[48,3584]{1,0:T(8,128)(2,1)S(1)}, bf16[48,3584]{1,0:T(8,128)(2,1)S(1)}, u32[]{:S(2)}, u32[]{:S(2)}) collective-permute-start(bf16[48,3584]{1,0:T(8,128)(2,1)S(1)} %get-tuple-element.146), channel_id=1, source_target_pairs={{0,8},{8,0},{16,24},{24,16},{1,9},{9,1},{17,25},{25,17},{2,10},{10... | collective-permute-start | bytes 1032200 | tf_op jit(solution)/shard_map/reduce_3_1/ppermute | solution.py:298
  165.8 18.4 %collective-permute-start.25 = (bf16[96,3584]{1,0:T(8,128)(2,1)S(1)}, bf16[96,3584]{1,0:T(8,128)(2,1)S(1)}, u32[]{:S(2)}, u32[]{:S(2)}) collective-permute-start(bf16[96,3584]{1,0:T(8,128)(2,1)S(1)} %pad_maximum_fusion.7), channel_id=1, source_target_pairs={{0,8},{8,0},{16,24},{24,16},{1,9},{9,1},{17,25},{25,17},{2,10},{10... | collective-permute-start | bytes 2064392 | tf_op jit(solution)/shard_map/deliver_5_1/ppermute | solution.py:318
  167.5 31.6 %collective-permute-start.26 = (bf16[96,3584]{1,0:T(8,128)(2,1)S(1)}, bf16[96,3584]{1,0:T(8,128)(2,1)S(1)}, u32[]{:S(2)}, u32[]{:S(2)}) collective-permute-start(bf16[96,3584]{1,0:T(8,128)(2,1)S(1)} %pad_maximum_fusion.8), channel_id=1, source_target_pairs={{0,16},{8,24},{16,0},{24,8},{1,17},{9,25},{17,1},{25,9},{2,18},{10... | collective-permute-start | bytes 2064392 | tf_op jit(solution)/shard_map/deliver_5_2/ppermute | solution.py:318
  169.1 30.0 %collective-permute-start.27 = (bf16[96,3584]{1,0:T(8,128)(2,1)S(1)}, bf16[96,3584]{1,0:T(8,128)(2,1)S(1)}, u32[]{:S(2)}, u32[]{:S(2)}) collective-permute-start(bf16[96,3584]{1,0:T(8,128)(2,1)S(1)} %pad_maximum_fusion.9), channel_id=1, source_target_pairs={{0,24},{8,16},{16,8},{24,0},{1,25},{9,17},{17,9},{25,1},{2,26},{10... | collective-permute-start | bytes 2064392 | tf_op jit(solution)/shard_map/deliver_5_3/ppermute | solution.py:318
  169.8 29.2 %collective-permute-start.28 = (bf16[96,3584]{1,0:T(8,128)(2,1)S(1)}, bf16[96,3584]{1,0:T(8,128)(2,1)S(1)}, u32[]{:S(2)}, u32[]{:S(2)}) collective-permute-start(bf16[96,3584]{1,0:T(8,128)(2,1)S(1)} %get-tuple-element.166), channel_id=1, source_target_pairs={{2,0},{3,1},{6,2},{7,3},{0,4},{1,5},{4,6},{5,7},{10,8},{11,9},{14,... | collective-permute-start | bytes 2064392 | tf_op jit(solution)/shard_map/shares_onward_5/ppermute | solution.py:271
  170.6 30.4 %collective-permute-start.24 = (bf16[96,3584]{1,0:T(8,128)(2,1)S(1)}, bf16[96,3584]{1,0:T(8,128)(2,1)S(1)}, u32[]{:S(2)}, u32[]{:S(2)}) collective-permute-start(bf16[96,3584]{1,0:T(8,128)(2,1)S(1)} %get-tuple-element.167), channel_id=1, source_target_pairs={{0,2},{1,3},{2,6},{3,7},{4,0},{5,1},{6,4},{7,5},{8,10},{9,11},{10,... | collective-permute-start | bytes 2064392 | tf_op jit(solution)/shard_map/shares_backward_5/ppermute | solution.py:271
  202.4 5.2 %collective-permute-start.33 = (bf16[384,3584]{1,0:T(8,128)(2,1)S(1)}, bf16[384,3584]{1,0:T(8,128)(2,1)S(1)}, u32[]{:S(2)}, u32[]{:S(2)}) collective-permute-start(bf16[384,3584]{1,0:T(8,128)(2,1)S(1)} %select_dynamic-update-slice_fusion.own), channel_id=1, source_target_pairs={{0,1},{1,0},{2,3},{3,2},{4,5},{5,4},{6,7},{7,6},{8,9},{9,8},{10,11... | collective-permute-start | bytes 8257544 | tf_op jit(solution)/shard_map/deliver_twin_6/ppermute | solution.py:328
  202.6 15.1 %collective-permute-start.31 = (bf16[48,3584]{1,0:T(8,128)(2,1)S(1)}, bf16[48,3584]{1,0:T(8,128)(2,1)S(1)}, u32[]{:S(2)}, u32[]{:S(2)}) collective-permute-start(bf16[48,3584]{1,0:T(8,128)(2,1)S(1)} %get-tuple-element.123), channel_id=1, source_target_pairs={{0,24},{8,16},{16,8},{24,0},{1,25},{9,17},{17,9},{25,1},{2,26},{10... | collective-permute-start | bytes 1032200 | tf_op jit(solution)/shard_map/deliver_6_3/ppermute | solution.py:318
  205.2 16.3 %collective-permute-start.30 = (bf16[48,3584]{1,0:T(8,128)(2,1)S(1)}, bf16[48,3584]{1,0:T(8,128)(2,1)S(1)}, u32[]{:S(2)}, u32[]{:S(2)}) collective-permute-start(bf16[48,3584]{1,0:T(8,128)(2,1)S(1)} %get-tuple-element.124), channel_id=1, source_target_pairs={{0,16},{8,24},{16,0},{24,8},{1,17},{9,25},{17,1},{25,9},{2,18},{10... | collective-permute-start | bytes 1032200 | tf_op jit(solution)/shard_map/deliver_6_2/ppermute | solution.py:318
  205.7 15.8 %collective-permute-start.29 = (bf16[48,3584]{1,0:T(8,128)(2,1)S(1)}, bf16[48,3584]{1,0:T(8,128)(2,1)S(1)}, u32[]{:S(2)}, u32[]{:S(2)}) collective-permute-start(bf16[48,3584]{1,0:T(8,128)(2,1)S(1)} %get-tuple-element.125), channel_id=1, source_target_pairs={{0,8},{8,0},{16,24},{24,16},{1,9},{9,1},{17,25},{25,17},{2,10},{10... | collective-permute-start | bytes 1032200 | tf_op jit(solution)/shard_map/deliver_6_1/ppermute | solution.py:318
  206.3 15.2 %collective-permute-start.32 = (bf16[48,3584]{1,0:T(8,128)(2,1)S(1)}, bf16[48,3584]{1,0:T(8,128)(2,1)S(1)}, u32[]{:S(2)}, u32[]{:S(2)}) collective-permute-start(bf16[48,3584]{1,0:T(8,128)(2,1)S(1)} %get-tuple-element.160), channel_id=1, source_target_pairs={{2,0},{3,1},{6,2},{7,3},{0,4},{1,5},{4,6},{5,7},{10,8},{11,9},{14,... | collective-permute-start | bytes 1032200 | tf_op jit(solution)/shard_map/shares_onward_6/ppermute | solution.py:271
  221.8 3.8 %collective-permute-start.37 = (bf16[192,3584]{1,0:T(8,128)(2,1)S(1)}, bf16[192,3584]{1,0:T(8,128)(2,1)S(1)}, u32[]{:S(2)}, u32[]{:S(2)}) collective-permute-start(bf16[192,3584]{1,0:T(8,128)(2,1)S(1)} %pad_maximum_fusion.own), channel_id=1, source_target_pairs={{0,1},{1,0},{2,3},{3,2},{4,5},{5,4},{6,7},{7,6},{8,9},{9,8},{10,11... | collective-permute-start | bytes 4128776 | tf_op jit(solution)/shard_map/deliver_twin_7/ppermute | solution.py:328
  222.0 18.3 %collective-permute-start.36 = (bf16[48,3584]{1,0:T(8,128)(2,1)S(1)}, bf16[48,3584]{1,0:T(8,128)(2,1)S(1)}, u32[]{:S(2)}, u32[]{:S(2)}) collective-permute-start(bf16[48,3584]{1,0:T(8,128)(2,1)S(1)} %get-tuple-element.126), channel_id=1, source_target_pairs={{0,24},{8,16},{16,8},{24,0},{1,25},{9,17},{17,9},{25,1},{2,26},{10... | collective-permute-start | bytes 1032200 | tf_op jit(solution)/shard_map/deliver_7_3/ppermute | solution.py:318
  223.7 17.1 %collective-permute-start.35 = (bf16[48,3584]{1,0:T(8,128)(2,1)S(1)}, bf16[48,3584]{1,0:T(8,128)(2,1)S(1)}, u32[]{:S(2)}, u32[]{:S(2)}) collective-permute-start(bf16[48,3584]{1,0:T(8,128)(2,1)S(1)} %get-tuple-element.127), channel_id=1, source_target_pairs={{0,16},{8,24},{16,0},{24,8},{1,17},{9,25},{17,1},{25,9},{2,18},{10... | collective-permute-start | bytes 1032200 | tf_op jit(solution)/shard_map/deliver_7_2/ppermute | solution.py:318
  225.0 15.8 %collective-permute-start.34 = (bf16[48,3584]{1,0:T(8,128)(2,1)S(1)}, bf16[48,3584]{1,0:T(8,128)(2,1)S(1)}, u32[]{:S(2)}, u32[]{:S(2)}) collective-permute-start(bf16[48,3584]{1,0:T(8,128)(2,1)S(1)} %get-tuple-element.128), channel_id=1, source_target_pairs={{0,8},{8,0},{16,24},{24,16},{1,9},{9,1},{17,25},{25,17},{2,10},{10... | collective-permute-start | bytes 1032200 | tf_op jit(solution)/shard_map/deliver_7_1/ppermute | solution.py:318
  225.6 5.1 %copy-start = (bf16[1024,256]{1,0:T(8,128)(2,1)S(1)}, bf16[1024,256]{1,0:T(8,128)(2,1)}, u32[]{:S(2)}) copy-start(bf16[1024,256]{1,0:T(8,128)(2,1)} %tokens.3) | copy-start | bytes 1572868
  241.1 3.2 %collective-permute-start.38 = (bf16[192,3584]{1,0:T(8,128)(2,1)S(1)}, bf16[192,3584]{1,0:T(8,128)(2,1)S(1)}, u32[]{:S(2)}, u32[]{:S(2)}) collective-permute-start(bf16[192,3584]{1,0:T(8,128)(2,1)S(1)} %pad_maximum_fusion.1.own), channel_id=1, source_target_pairs={{0,1},{1,0},{2,3},{3,2},{4,5},{5,4},{6,7},{7,6},{8,9},{9,8},{10,11... | collective-permute-start | bytes 4128776 | tf_op jit(solution)/shard_map/deliver_twin_8/ppermute | solution.py:328
  260.1 6.4 %collective-permute-start.39 = (bf16[512,128]{1,0:T(8,128)(2,1)S(1)}, bf16[512,128]{1,0:T(8,128)(2,1)S(1)}, u32[]{:S(2)}, u32[]{:S(2)}) collective-permute-start(bf16[512,128]{1,0:T(8,128)(2,1)S(1)} %get-tuple-element.163), channel_id=1, source_target_pairs={{0,8},{8,0},{16,24},{24,16},{1,9},{9,1},{17,25},{25,17},{2,10},{10... | collective-permute-start | bytes 393224 | tf_op jit(solution)/shard_map/check_reduce_1/ppermute | solution.py:358
  261.3 8.2 %collective-permute-start.41 = (bf16[512,128]{1,0:T(8,128)(2,1)S(1)}, bf16[512,128]{1,0:T(8,128)(2,1)S(1)}, u32[]{:S(2)}, u32[]{:S(2)}) collective-permute-start(bf16[512,128]{1,0:T(8,128)(2,1)S(1)} %get-tuple-element.164), channel_id=1, source_target_pairs={{0,24},{8,16},{16,8},{24,0},{1,25},{9,17},{17,9},{25,1},{2,26},{10... | collective-permute-start | bytes 393224 | tf_op jit(solution)/shard_map/check_reduce_3/ppermute | solution.py:358
  263.1 7.8 %collective-permute-start.40 = (bf16[512,128]{1,0:T(8,128)(2,1)S(1)}, bf16[512,128]{1,0:T(8,128)(2,1)S(1)}, u32[]{:S(2)}, u32[]{:S(2)}) collective-permute-start(bf16[512,128]{1,0:T(8,128)(2,1)S(1)} %get-tuple-element.165), channel_id=1, source_target_pairs={{0,16},{8,24},{16,0},{24,8},{1,17},{9,25},{17,1},{25,9},{2,18},{10... | collective-permute-start | bytes 393224 | tf_op jit(solution)/shard_map/check_reduce_2/ppermute | solution.py:358
  (1 other events, 1.1 us)
